TPU v7x, 256 devices: a whole 4x4x8 slice. The times are simulated.
256 devices in a mesh: head: 8 (over z_lo, y), ctx: 32 (over z_hi, x, core).
Axes of the slice: x: 4, y: 4, z: 8 (z_hi: 4, z_lo: 2; z = z_hi * 2 + z_lo), core: 2. Of those that a mesh axis runs over, the one named last changes fastest.
Arguments:
- queries: bfloat16 [512, 24576], P(None, 'head'), may hold values from -100 to 100
- attn_keys: bfloat16 [8192, 24576], P('ctx', 'head'), may hold values from -6 to 6
- index_queries: bfloat16 [512, 8192], P(None, 'head'), may hold values from -16 to 16
- index_keys: bfloat16 [8192, 128], P('ctx'), may hold values from -6 to 6
- head_weights: float32 [512, 64], P(None, 'head'), may hold values from 0.1 to 1
- query_pos: int32 [512], replicated, may hold values from 16 to 65535
- key_offset: int32 [8192], P('ctx'), may hold values from 0 to 7
Outputs:
- index_query_grad: float32 [512, 8192], P('ctx', 'head')
- index_key_grad: float32 [8192, 128], P('ctx')
All inputs are finite; a program needn't handle non-finite values.
Results may differ from a plain program's by a relative error of at most 0.0027.
Values sent between devices are 32-bit elements; how exact they have to be, the bound alone decides.
No kernel may reach another device: no remote copies, remote signals or barrier semaphores. Data moves between devices by JAX's collectives and lax.ppermute only.
A program may use at most 64 MiB of HBM per device.

v0:
```python
import math

import jax
import jax.numpy as jnp
from jax import lax
from jax.sharding import PartitionSpec as P

HEADS = 128
HEAD_DIM = 192
IDIM = 128
STRIDE = 8


NEG_FILL = -1e30


def row_stats(values, visible):
    masked = jnp.where(visible, values, NEG_FILL)
    local_top = jnp.max(masked, axis=-1)
    top_value = lax.pmax(local_top, "ctx")
    local_mass = jnp.sum(jnp.where(visible, jnp.exp(masked - top_value[..., None]), 0.0), axis=-1)
    total_mass = lax.psum(local_mass, "ctx")
    return jnp.where(visible, jnp.exp(masked - top_value[..., None]), 0.0) / total_mass[..., None]


def shards(queries, attn_keys, index_queries, index_keys, head_weights, query_pos, key_offset):
    query_rows = queries.shape[0]
    key_rows = attn_keys.shape[0]
    local_heads = attn_keys.shape[1] // HEAD_DIM
    index_heads = index_queries.shape[1] // IDIM
    key_start = lax.axis_index("ctx") * key_rows
    key_pos = STRIDE * (key_start + jnp.arange(key_rows, dtype=jnp.int32)) + key_offset
    visible = key_pos[None, :] <= query_pos[:, None]
    attn_scale = 1.0 / math.sqrt(HEAD_DIM)
    inv_scale = 1.0 / math.sqrt(IDIM)
    query_heads = queries.reshape(query_rows, local_heads, HEAD_DIM)
    key_heads = attn_keys.reshape(key_rows, local_heads, HEAD_DIM)
    scores = (
        jnp.einsum("thd,shd->hts", query_heads, key_heads, preferred_element_type=jnp.float32)
        * attn_scale
    )
    head_probs = row_stats(scores, visible[None])
    target_part = jnp.sum(head_probs, axis=0)
    index_heads_q = index_queries.reshape(query_rows, index_heads, IDIM)
    activation = (
        jnp.einsum("tjd,sd->tjs", index_heads_q, index_keys, preferred_element_type=jnp.float32)
        * inv_scale
    )
    logit_part = jnp.sum(head_weights[:, :, None] * jnp.maximum(activation, 0.0), axis=1)
    target = lax.psum(target_part, "head") / HEADS
    logits = lax.psum(logit_part, "head")
    prob_step = row_stats(logits, visible) - target
    grad_terms = jnp.where(
        activation > 0.0, prob_step[:, None, :] * head_weights[:, :, None] * inv_scale, 0.0
    ).astype(jnp.bfloat16)
    key_part = jnp.einsum(
        "tjs,tjd->sd", grad_terms, index_heads_q, preferred_element_type=jnp.float32
    )
    key_grad = lax.psum(key_part, "head")
    result = jnp.einsum("tjs,sd->tjd", grad_terms, index_keys, preferred_element_type=jnp.float32)
    query_grad = lax.psum_scatter(
        result.reshape(
            query_rows // lax.axis_size("ctx") * lax.axis_size("ctx"), index_heads * IDIM
        ),
        "ctx",
        scatter_dimension=0,
        tiled=True,
    )
    return (query_grad, key_grad)


def solution(mesh):
    in_specs = (
        P(None, "head"),
        P("ctx", "head"),
        P(None, "head"),
        P("ctx", None),
        P(None, "head"),
        P(),
        P("ctx"),
    )
    out_specs = (P("ctx", "head"), P("ctx", None))
    return jax.shard_map(shards, mesh=mesh, in_specs=in_specs, out_specs=out_specs, check_vma=False)
```

profile of v0, /device:TPU:8, one launch (start us, length us, event | category | flops | bytes accessed | tf_op | source)
XLA Modules:
  0.0 646.9 jit_solution(10858235190181605024)
XLA Ops:
  7.2 0.0 copy-start
  7.2 0.0 copy-start.7
  7.2 0.0 copy-start.5
  7.2 0.0 copy-start.2
  7.2 0.0 all-reduce.6.cloned.1.call-start
  7.3 1.1 copy-done
  8.4 4.2 multiply_reduce_fusion
  12.6 0.0 all-reduce.6.cloned.1.call-update
  12.6 0.0 all-reduce.8.cloned.1.call-start
  12.7 0.0 copy-done.7
  12.7 0.0 copy-done.5
  12.7 0.1 broadcast_compare_fusion
  12.9 0.2 copy.34
  13.1 0.0 copy-done.2
  13.1 1.6 copy.36
  14.7 0.0 copy-start.3
  14.7 4.8 copy.35
  19.5 0.0 copy-done.3
  19.5 6.8 %fusion = (f32[16,512]{1,0:T(8,128)S(1)}, f32[16,512,256]{1,2,0:T(8,128)}) fusion(pred[512,256]{0,1:T(8,128)(4,1)S(1)} %copy.34, bf16[512,16,192]{0,2,1:T(8,128)(2,1)} %bitcast.29, bf16[256,16,192]{0,2,1:T(8,128)(2,1)S(1)} %bitcast.31), kind=kOutput, calls=%fused_computation.3 | convolution fusion | flops 811589632 | bytes 13271040 | tf_op jit(solution)/shard_map/thd,shd->hts/dot_general | solution.py:39
  26.4 67.4 %all-reduce.6.cloned.1.call-done = f32[512,256]{1,0:T(8,128)} async-done(((f32[512,256]{1,0:T(8,128)}), f32[512,256]{1,0:T(8,128)}) %all-reduce.6.cloned.1.call-update) | async-done | bytes 524304 | tf_op jit(solution)/shard_map/psum | solution.py:51
  93.7 1.3 fusion.14
  95.0 138.2 %all-reduce.1 = (f32[16,512]{1,0:T(8,128)S(1)}, f32[512]{0:T(512)S(1)}) all-reduce(f32[16,512]{1,0:T(8,128)S(1)} %get-tuple-element.6, f32[512]{0:T(512)S(1)} %fusion.14), channel_id=1, replica_groups=mesh['head'=8,'ctx'=32] {'ctx'}, use_global_device_ids=true, to_apply=%region_7.8 | all-reduce | flops 8704 | bytes 69632 | tf_op jit(solution)/shard_map/pmax | solution.py:20
  233.2 0.0 copy-start.1
  233.2 4.5 fusion.1
  237.8 0.0 copy-done.1
  237.8 0.3 fusion.13
  238.1 138.2 %all-reduce = (f32[16,512]{1,0:T(8,128)S(1)}, f32[512]{0:T(512)S(1)}) all-reduce(f32[16,512]{1,0:T(8,128)S(1)} %fusion.1, f32[512]{0:T(512)S(1)} %fusion.13), channel_id=1, replica_groups=mesh['head'=8,'ctx'=32] {'ctx'}, use_global_device_ids=true, to_apply=%region_9.10 | all-reduce | flops 8704 | bytes 69632 | tf_op jit(solution)/shard_map/psum | solution.py:22
  376.3 4.7 divide_reduce_fusion
  380.9 0.0 copy-start.6
  381.0 1.0 copy.37
  382.0 0.0 all-reduce.8.cloned.1.call-update
  382.0 0.0 all-reduce.10.cloned.1.call-start
  382.0 2.9 fusion.8
  384.9 74.4 %all-reduce.8.cloned.1.call-done = f32[512,256]{1,0:T(8,128)} async-done(((f32[512,256]{1,0:T(8,128)}), f32[512,256]{1,0:T(8,128)}) %all-reduce.8.cloned.1.call-update) | async-done | bytes 524304 | tf_op jit(solution)/shard_map/psum | solution.py:50
  459.3 1.3 multiply_subtract_fusion
  460.7 0.0 copy-done.6
  460.7 0.0 copy-start.4
  460.7 2.3 fusion.4
  463.0 0.0 all-reduce.10.cloned.1.call-update
  463.0 0.0 reduce-scatter.2.cloned.1.call-start
  463.1 0.0 copy-done.4
  463.1 2.4 fusion.3
  465.5 2.9 copy.39
  468.4 0.0 reduce-scatter.2.cloned.1.call-update
  468.4 72.8 %all-reduce.10.cloned.1.call-done = f32[256,128]{1,0:T(8,128)} async-done(((f32[256,128]{1,0:T(8,128)}), f32[256,128]{1,0:T(8,128)}) %all-reduce.10.cloned.1.call-update) | async-done | bytes 131088 | tf_op jit(solution)/shard_map/psum | solution.py:59
  541.2 97.6 %reduce-scatter.2.cloned.1.call-done = f32[16,1024]{1,0:T(8,128)} async-done(((f32[512,1024]{1,0:T(8,128)}), f32[16,1024]{1,0:T(8,128)}) %reduce-scatter.2.cloned.1.call-update) | async-done | bytes 65552 | tf_op jit(solution)/shard_map/reduce_scatter | solution.py:61
  638.8 1.6 copy.59
  (1 shorter events, 0.0 us)
Async XLA Ops:
  7.2 1.2 copy-start
  7.2 5.5 copy-start.7
  7.2 5.5 copy-start.5
  7.2 5.9 copy-start.2
  7.2 86.5 %all-reduce.6.cloned.1.call-start = ((), (), s32[]{:S(2)}) async-start(), calls=%async_computation.1 | async-start | bytes 1048576 | tf_op jit(solution)/shard_map/psum | solution.py:51
  12.6 446.7 %all-reduce.8.cloned.1.call-start = ((), (), s32[]{:S(2)}) async-start(), calls=%async_computation.2 | async-start | bytes 1048576 | tf_op jit(solution)/shard_map/psum | solution.py:50
  14.7 4.8 copy-start.3
  233.2 4.5 copy-start.1
  380.9 79.7 %copy-start.6 = (f32[512,8]{0,1:T(8,128)S(1)}, f32[512,8]{0,1:T(8,128)}, u32[]{:S(2)}) copy-start(f32[512,8]{0,1:T(8,128)} %param.11) | copy-start | bytes 49156
  382.0 159.2 %all-reduce.10.cloned.1.call-start = ((), (), s32[]{:S(2)}) async-start(), calls=%async_computation.4 | async-start | bytes 262144 | tf_op jit(solution)/shard_map/psum | solution.py:59
  460.7 2.4 copy-start.4
  463.0 175.8 %reduce-scatter.2.cloned.1.call-start = ((), (), s32[]{:S(2)}) async-start(), calls=%async_computation.3 | async-start | bytes 2162688 | tf_op jit(solution)/shard_map/reduce_scatter | solution.py:61
Sparse Core Ops, SparseCore 0:
  12.8 80.9 all-reduce.5
  382.1 77.1 all-reduce.7
  463.2 77.9 all-reduce.9
  546.0 92.8 reduce-scatter.1
where the time goes:
time: 647 us
  waiting for transfers between devices  312 us (48%)
  blocking collectives  276 us (43%)
  matrix products  15.8 us (2%)
  other arithmetic  15.1 us (2%)
  between operations  13.9 us (2%)
  local copies, waits for them, and re-layouts  13.3 us (2%)
    pmax x1, blocking collectives, row_stats(): top_value = lax.pmax(local_top, 'ctx')  138 us
    psum x1, blocking collectives, row_stats(): total_mass = lax.psum(local_mass, 'ctx')  138 us
    reduce_scatter x1, waiting for transfers between devices, shards(): lax.psum_scatter(result.reshape(query_rows // lax.axis_size('ctx') * lax....  97.6 us
    psum x1, waiting for transfers between devices, shards(): target = lax.psum(target_part, 'head') / HEADS  74.4 us
    psum x1, waiting for transfers between devices, shards(): key_grad = lax.psum(key_part, 'head')  72.8 us
    psum x1, waiting for transfers between devices, shards(): logits = lax.psum(logit_part, 'head')  67.4 us
  transfers between devices with their start and end apart: 4, of which 4 were waited for; matrix products, arithmetic and copies ran while one was open for 3% of the time, Pallas kernels for 0%

commit v1 on v0

v1 whole, which is shorter than its diff:
```python
import math

import jax
import jax.numpy as jnp
from jax import lax
from jax.experimental import pallas as pl
from jax.experimental.pallas import tpu as pltpu
from jax.sharding import Mesh
from jax.sharding import PartitionSpec as P

HEADS = 128
HEAD_DIM = 192
IDIM = 128
STRIDE = 8
LANES = 128
LOG2E = math.log2(math.e)
NEG_FILL = -1e30
SCORE_SCALE = LOG2E / math.sqrt(HEAD_DIM)
INV_SCALE = 1.0 / math.sqrt(IDIM)

AXES = ("z_lo", "y", "z_hi", "x", "core")
HEAD = ("z_lo", "y")
CTX = ("z_hi", "x", "core")
CHIP = ("z_hi", "x")
F32, BF16 = jnp.float32, jnp.bfloat16
VMEM_SPEC = pl.BlockSpec(memory_space=pltpu.VMEM)
SMEM_SPEC = pl.BlockSpec(memory_space=pltpu.SMEM)
PARAMS = pltpu.CompilerParams(vmem_limit_bytes=40 * 2**20)


def shift(value, axis, size, step):
    return lax.ppermute(value, axis, [(i, (i + step) % size) for i in range(size)])


def merge(parts):
    top = jnp.max(parts, axis=0)
    return top + jnp.log2(jnp.sum(jnp.exp2(parts - top[None]), axis=0))


def dot_t(a, b):
    return lax.dot_general(a, b, (((1,), (1,)), ((), ())), preferred_element_type=F32)


def head_scores(q_ref, k_ref, which):
    lane = lax.broadcasted_iota(jnp.int32, (1, LANES), 1)
    low = (lane < HEAD_DIM - LANES).astype(F32)
    if which == 0:
        k = jnp.concatenate([k_ref[:, :LANES], k_ref[:, LANES : 2 * LANES] * low.astype(BF16)], axis=1)
        q = q_ref[:, : 2 * LANES]
    else:
        k = jnp.concatenate(
            [k_ref[:, LANES : 2 * LANES] * (1.0 - low).astype(BF16), k_ref[:, 2 * LANES :]], axis=1
        )
        q = q_ref[:, LANES:]
    return dot_t(k, q) * SCORE_SCALE


def fill_bias(bias, kp_ref, qp_ref):
    bias[...] = jnp.where(kp_ref[...] <= qp_ref[...], 0.0, NEG_FILL)


def lse_kernel(sc_ref, q_ref, k_ref, kp_ref, qp_ref, mine_ref, other_ref, bias):
    i = pl.program_id(0)

    @pl.when(i == 0)
    def _():
        fill_bias(bias, kp_ref, qp_ref)

    half_steps = mine_ref.shape[0] // 2
    for which in range(2):
        s = head_scores(q_ref, k_ref, which) + bias[...]
        top = jnp.max(s, axis=0, keepdims=True)
        value = top + jnp.log2(jnp.sum(jnp.exp2(s - top), axis=0, keepdims=True))
        row = pl.ds(2 * lax.rem(i, half_steps) + which, 1)

        @pl.when(i // half_steps == sc_ref[0])
        def _():
            mine_ref[row, :] = value

        @pl.when(i // half_steps != sc_ref[0])
        def _():
            other_ref[row, :] = value


def pair_specs(rows, keys):
    width = 2 * HEAD_DIM
    return [
        SMEM_SPEC,
        pl.BlockSpec((rows, width), lambda i: (0, i)),
        pl.BlockSpec((keys, width), lambda i: (0, i)),
        pl.BlockSpec((keys, 1), lambda i: (0, 0)),
        pl.BlockSpec((1, rows), lambda i: (0, 0)),
    ]


def scores_lse(sc, queries, attn_keys, kp, qp):
    rows, keys = queries.shape[0], attn_keys.shape[0]
    heads = queries.shape[1] // HEAD_DIM
    out = jax.ShapeDtypeStruct((heads // 2, rows), F32)
    spec = pl.BlockSpec((heads // 2, rows), lambda i: (0, 0))
    return pl.pallas_call(
        lse_kernel,
        grid=(heads // 2,),
        in_specs=pair_specs(rows, keys),
        out_specs=[spec, spec],
        out_shape=[out, out],
        scratch_shapes=[pltpu.VMEM((keys, rows), F32)],
        compiler_params=PARAMS,
        name="scores_lse",
    )(sc, queries, attn_keys, kp, qp)


def split_rows(tr, out_ref, value):
    turned = value.T
    n, blk, keys = out_ref.shape
    for half in range(keys // LANES):
        span = slice(half * LANES, (half + 1) * LANES)
        tr[half * n * blk : (half + 1) * n * blk, :] = turned[:, span]
        for h in range(n):
            out_ref[h, :, span] = tr[pl.ds(half * n * blk + h, blk, stride=n), :]


def probs_kernel(sc_ref, q_ref, k_ref, kp_ref, qp_ref, mine_ref, other_ref, out_ref, bias, acc, tr):
    i = pl.program_id(0)

    @pl.when(i == 0)
    def _():
        fill_bias(bias, kp_ref, qp_ref)
        acc[...] = jnp.zeros_like(acc)

    half_steps = mine_ref.shape[0] // 2
    own = i // half_steps == sc_ref[0]
    total = acc[...]
    for which in range(2):
        row = pl.ds(2 * lax.rem(i, half_steps) + which, 1)
        lse = jnp.where(own, mine_ref[row, :], other_ref[row, :])
        total += jnp.exp2(head_scores(q_ref, k_ref, which) + bias[...] - lse)
    acc[...] = total

    @pl.when(i == pl.num_programs(0) - 1)
    def _():
        split_rows(tr, out_ref, acc[...])


def probs_sum(sc, queries, attn_keys, kp, qp, mine, other, n_head):
    rows, keys = queries.shape[0], attn_keys.shape[0]
    heads = queries.shape[1] // HEAD_DIM
    spec = pl.BlockSpec(mine.shape, lambda i: (0, 0))
    shape = (n_head, rows // n_head, keys)
    return pl.pallas_call(
        probs_kernel,
        grid=(heads // 2,),
        in_specs=pair_specs(rows, keys) + [spec, spec],
        out_specs=pl.BlockSpec(shape, lambda i: (0, 0, 0)),
        out_shape=jax.ShapeDtypeStruct(shape, F32),
        scratch_shapes=[
            pltpu.VMEM((keys, rows), F32),
            pltpu.VMEM((keys, rows), F32),
            pltpu.VMEM((rows * keys // LANES, LANES), F32),
        ],
        compiler_params=PARAMS,
        name="probs_sum",
    )(sc, queries, attn_keys, kp, qp, mine, other)


def logits_kernel(iq_ref, ik_ref, w_ref, out_ref, tr):
    total = None
    for j in range(w_ref.shape[0]):
        act = dot_t(ik_ref[...], iq_ref[:, j * IDIM : (j + 1) * IDIM])
        term = jnp.maximum(act, 0.0) * w_ref[j : j + 1, :]
        total = term if total is None else total + term
    split_rows(tr, out_ref, total)


def part_logits(iq, ik, w, n_head):
    rows, keys = iq.shape[0], ik.shape[0]
    return pl.pallas_call(
        logits_kernel,
        in_specs=[VMEM_SPEC] * 3,
        out_specs=VMEM_SPEC,
        out_shape=jax.ShapeDtypeStruct((n_head, rows // n_head, keys), F32),
        scratch_shapes=[pltpu.VMEM((rows * keys // LANES, LANES), F32)],
        compiler_params=PARAMS,
        name="part_logits",
    )(iq, ik, w)


def merge_kernel(parts_ref, out_ref):
    out_ref[...] = merge(parts_ref[...])


def merge_parts(parts):
    return pl.pallas_call(
        merge_kernel,
        in_specs=[VMEM_SPEC],
        out_specs=VMEM_SPEC,
        out_shape=jax.ShapeDtypeStruct(parts.shape[1:], F32),
        name="merge_parts",
    )(parts)


def step_kernel(target_ref, logits_ref, lse_ref, wide_ref, chips_ref, tmp):
    target = jnp.sum(target_ref[...], axis=0) * (1.0 / HEADS)
    blk = target.shape[0]
    lse = merge(lse_ref[...]).T[:blk, :1]
    step = jnp.exp2(logits_ref[...] - lse) - target
    for h in range(wide_ref.shape[0]):
        wide_ref[h] = step
    n_chip, per = chips_ref.shape[0], chips_ref.shape[1] // 2
    for half in range(2):
        tmp[half * blk : (half + 1) * blk, :] = step[:, half * LANES : (half + 1) * LANES]
        for r in range(per):
            chips_ref[:, half * per + r, :] = tmp[pl.ds(half * blk + r, n_chip, stride=per), :]


def prob_step(target_parts, logits, lse_parts, n_chip):
    n_head, blk, keys = target_parts.shape
    return pl.pallas_call(
        step_kernel,
        in_specs=[VMEM_SPEC] * 3,
        out_specs=[VMEM_SPEC] * 2,
        out_shape=[
            jax.ShapeDtypeStruct((n_head, blk, keys), F32),
            jax.ShapeDtypeStruct((n_chip, 2 * blk // n_chip, LANES), F32),
        ],
        scratch_shapes=[pltpu.VMEM((blk * keys // LANES, LANES), F32)],
        name="prob_step",
    )(target_parts, logits, lse_parts)


def key_kernel(step_ref, iq_ref, ik_ref, w_ref, out_ref, tr):
    n, blk, keys = step_ref.shape
    turned = []
    for half in range(keys // LANES):
        base = half * n * blk
        for h in range(n):
            tr[pl.ds(base + h, blk, stride=n), :] = step_ref[h, :, half * LANES : (half + 1) * LANES]
        turned.append(tr[base : base + n * blk, :].T)
    step = jnp.concatenate(turned, axis=0)
    total = None
    for j in range(w_ref.shape[0]):
        iq = iq_ref[:, j * IDIM : (j + 1) * IDIM]
        act = dot_t(ik_ref[...], iq)
        terms = jnp.where(act > 0.0, step * (w_ref[j : j + 1, :] * INV_SCALE), 0.0).astype(BF16)
        part = jnp.dot(terms, iq, preferred_element_type=F32)
        total = part if total is None else total + part
    out_ref[...] = total


def key_part_grad(step, iq, ik, w):
    rows, keys = iq.shape[0], ik.shape[0]
    return pl.pallas_call(
        key_kernel,
        in_specs=[VMEM_SPEC] * 4,
        out_specs=VMEM_SPEC,
        out_shape=jax.ShapeDtypeStruct((keys, IDIM), F32),
        scratch_shapes=[pltpu.VMEM((rows * keys // LANES, LANES), F32)],
        compiler_params=PARAMS,
        name="key_part_grad",
    )(step, iq, ik, w)


def query_kernel(sc_ref, step_ref, both_ref, ik0_ref, ik1_ref, ik2_ref, ik3_ref, keep_ref, give_ref, tmp):
    n_head, pj = both_ref.shape[0], both_ref.shape[2]
    per = step_ref.shape[1] // 2
    jl = pj // per
    iq = both_ref[:, 0].reshape(n_head * pj, IDIM).astype(BF16)
    w = both_ref[:, 1].reshape(n_head * pj, LANES)
    total = None
    for dx, ik_ref in enumerate((ik0_ref, ik1_ref, ik2_ref, ik3_ref)):
        for dz in range(4):
            source = lax.rem(sc_ref[1] + 4 - dz, 4) * 4 + lax.rem(sc_ref[2] + 4 - dx, 4)
            ik = ik_ref[dz].astype(BF16)
            act = dot_t(iq, ik)
            tile = step_ref[source]
            halves = []
            for half in range(2):
                rows = [
                    jnp.broadcast_to(tile[half * per + r : half * per + r + 1, :], (jl, LANES))
                    for r in range(per)
                ]
                step = jnp.concatenate(rows * n_head, axis=0)
                halves.append(step * w)
            step = jnp.concatenate(halves, axis=1)
            terms = jnp.where(act > 0.0, step, 0.0).astype(BF16)
            part = jnp.dot(terms, ik, preferred_element_type=F32)
            total = part if total is None else total + part
    tmp[...] = total.reshape(tmp.shape)
    keep_ref[...] = tmp[:, sc_ref[0]]
    give_ref[...] = tmp[:, 1 - sc_ref[0]]


def query_part_grad(sc, step, both, blocks):
    n_head, _, pj, _ = both.shape
    out = jax.ShapeDtypeStruct((n_head, pj // 2, IDIM), F32)
    return pl.pallas_call(
        query_kernel,
        in_specs=[SMEM_SPEC] + [VMEM_SPEC] * 6,
        out_specs=[VMEM_SPEC] * 2,
        out_shape=[out, out],
        scratch_shapes=[pltpu.VMEM((n_head, 2, pj // 2, IDIM), F32)],
        compiler_params=PARAMS,
        name="query_part_grad",
    )(sc, step, both, *blocks)


def place_kernel(parts_ref, out_ref, tmp):
    n, rj, _ = parts_ref.shape
    jl = out_ref.shape[1] // IDIM
    tmp[...] = parts_ref[...].reshape(tmp.shape)
    for r in range(rj // jl):
        for j in range(jl):
            out_ref[r * n : (r + 1) * n, j * IDIM : (j + 1) * IDIM] = tmp[
                pl.ds(r * jl + j, n, stride=rj), :
            ]


def place_rows(parts, jl):
    n, rj, _ = parts.shape
    return pl.pallas_call(
        place_kernel,
        in_specs=[VMEM_SPEC],
        out_specs=VMEM_SPEC,
        out_shape=jax.ShapeDtypeStruct((n * rj // jl, jl * IDIM), F32),
        scratch_shapes=[pltpu.VMEM((n * rj, IDIM), F32)],
        name="place_rows",
    )(parts)


def shards(queries, attn_keys, index_queries, index_keys, head_weights, query_pos, key_offset):
    rows, keys = queries.shape[0], attn_keys.shape[0]
    jl = index_queries.shape[1] // IDIM
    n_head, n_chip = lax.axis_size(HEAD), lax.axis_size(CHIP)
    blk = rows // n_head
    per = blk // n_chip
    core, zi, xi = (lax.axis_index(a) for a in ("core", "z_hi", "x"))
    hd, chip = lax.axis_index(HEAD), lax.axis_index(CHIP)
    sc = jnp.stack([core, zi, xi]).astype(jnp.int32)

    key_pos = STRIDE * (lax.axis_index(CTX) * keys + jnp.arange(keys, dtype=jnp.int32)) + key_offset
    kp, qp = key_pos[:, None], query_pos[None, :]
    qp_a = lax.dynamic_index_in_dim(query_pos.reshape(blk, n_head), hd, 1, False)
    bias_a = jnp.where(key_pos[None, :] <= qp_a[:, None], 0.0, NEG_FILL)
    w_o = head_weights.T

    mine, other = scores_lse(sc, queries, attn_keys, kp, qp)
    mine = merge(jnp.stack([mine, shift(other, "core", 2, 1)]))
    mine = merge_parts(
        lax.all_to_all(jnp.broadcast_to(mine[None], (n_chip, *mine.shape)), CHIP, 0, 0)
    )
    other = shift(mine, "core", 2, 1)
    target = probs_sum(sc, queries, attn_keys, kp, qp, mine, other, n_head)
    target = lax.all_to_all(target, HEAD, 0, 0)

    logits = part_logits(index_queries, index_keys, w_o, n_head)
    logits = jnp.sum(lax.all_to_all(logits, HEAD, 0, 0), axis=0) * (LOG2E * INV_SCALE) + bias_a
    top = jnp.max(logits, axis=1)
    lse = top + jnp.log2(jnp.sum(jnp.exp2(logits - top[:, None]), axis=1))
    lse = jnp.broadcast_to(jnp.pad(lse, (0, LANES - blk))[None], (8, LANES))
    lse = merge(jnp.stack([lse, shift(lse, "core", 2, 1)]))
    lse = lax.all_to_all(jnp.broadcast_to(lse[None], (n_chip, 8, LANES)), CHIP, 0, 0)

    step_wide, step_chips = prob_step(target, logits, lse, n_chip)

    step_o = lax.all_to_all(step_wide, HEAD, 0, 0)
    key_part = key_part_grad(step_o, index_queries, index_keys, w_o)
    key_part = key_part + shift(key_part, "z_lo", 2, 1)
    key_grad = key_part
    for k in range(1, 4):
        key_grad = key_grad + shift(key_part, "y", 4, k)

    iq_b = lax.dynamic_index_in_dim(
        index_queries.reshape(n_chip, per, n_head, jl * IDIM), chip, 0, False
    ).transpose(1, 0, 2).astype(F32).reshape(n_head, per * jl, IDIM)
    w_b = lax.dynamic_index_in_dim(
        head_weights.reshape(n_chip, per, n_head, jl), chip, 0, False
    ).transpose(1, 0, 2) * INV_SCALE
    w_b = jnp.broadcast_to(w_b.reshape(n_head, per * jl, 1), iq_b.shape)
    both = lax.all_to_all(jnp.stack([iq_b, w_b], 1), HEAD, 0, 0)
    ik = index_keys.astype(F32)
    zs = jnp.stack([ik] + [shift(ik, "z_hi", 4, k) for k in range(1, 4)])
    blocks = [zs] + [shift(zs, "x", 4, k) for k in range(1, 4)]

    step_b = lax.all_to_all(step_chips, CHIP, 0, 0)
    keep, give = query_part_grad(sc, step_b, both, blocks)
    qg = keep + shift(give, "core", 2, 1)
    qg = lax.all_to_all(qg, HEAD, 0, 0)
    return (place_rows(qg, jl), key_grad)


def solution(mesh):
    mesh = Mesh(mesh.devices.reshape(2, 4, 4, 4, 2), AXES)
    in_specs = (
        P(None, HEAD),
        P(CTX, HEAD),
        P(None, HEAD),
        P(CTX, None),
        P(None, HEAD),
        P(),
        P(CTX),
    )
    out_specs = (P(CTX, HEAD), P(CTX, None))
    return jax.shard_map(shards, mesh=mesh, in_specs=in_specs, out_specs=out_specs, check_vma=False)
```

time: 647 us -> 163 us (0.25)
  blocking collectives: 276 us -> 9.05 us
  waiting for transfers between devices: 312 us -> 47.2 us
  starting transfers between devices: 0.16 us -> 62.9 us
  Pallas kernels: 0 us -> 23.4 us
  matrix products: 15.8 us -> 0 us
  between operations: 13.9 us -> 0.96 us
  other arithmetic: 15.1 us -> 4.63 us
    psum x3 -> x0, waiting for transfers between devices: 215 us -> none  [the longest x1 74.4 us: shards(): target = lax.psum(target_part, 'head') / HEADS]
    pmax x1 -> x0, blocking collectives: 138 us -> none  [row_stats(): top_value = lax.pmax(local_top, 'ctx')]
    psum x1 -> x0, blocking collectives: 138 us -> none  [row_stats(): total_mass = lax.psum(local_mass, 'ctx')]
    reduce_scatter x1 -> x0, waiting for transfers between devices: 97.6 us -> none  [shards(): lax.psum_scatter(result.reshape(query_rows // lax.axis_size('ctx') * lax....]
    all_to_all x0 -> x7, starting transfers between devices: none -> 41.5 us  [the longest x1 10.2 us: shards(): lax.all_to_all(jnp.broadcast_to(mine[None], (n_chip, *mine.shape)), CHIP,...]
    ppermute x0 -> x14, waiting for transfers between devices: none -> 24.5 us  [shift(): lax.ppermute(value, axis, [(i, (i + step) % size) for i in range(size)])]
    pallas_call x0 -> x8, Pallas kernels: none -> 23.4 us  [the longest x1 7.28 us: scores_lse(): pl.pallas_call(lse_kernel, grid=(heads // 2,), in_specs=pair_specs(rows,...]
    all_to_all x0 -> x7, waiting for transfers between devices: none -> 22.7 us  [the longest x1 13.3 us: shards(): lax.all_to_all(jnp.broadcast_to(mine[None], (n_chip, *mine.shape)), CHIP,...]
  transfers between devices with their start and end apart: 4 -> 21, of which waited for: 4 -> 9; matrix products, arithmetic and copies ran while one was open for 3% -> 3% of each run, Pallas kernels for 0% -> 13%
where the time goes in v1:
time: 163 us; the launch traced here: 160 us
  starting transfers between devices  62.9 us (39%)
  waiting for transfers between devices  47.2 us (29%)
  Pallas kernels  23.4 us (14%)
  local copies, waits for them, and re-layouts  12.2 us (7%)
  blocking collectives  9.05 us (6%)
  other arithmetic  4.63 us (3%)
    ppermute x14, waiting for transfers between devices, shift(): lax.ppermute(value, axis, [(i, (i + step) % size) for i in range(size)])  24.5 us
    ppermute x14, starting transfers between devices, shift(): lax.ppermute(value, axis, [(i, (i + step) % size) for i in range(size)])  21.4 us
    all_to_all x1, waiting for transfers between devices, shards(): lax.all_to_all(jnp.broadcast_to(mine[None], (n_chip, *mine.shape)), CHIP,...  13.3 us
    all_to_all x1, starting transfers between devices, shards(): lax.all_to_all(jnp.broadcast_to(mine[None], (n_chip, *mine.shape)), CHIP,...  10.2 us
    unnamed x35, local copies, waits for them, and re-layouts  9.81 us
    all_to_all x1, blocking collectives, shards(): qg = lax.all_to_all(qg, HEAD, 0, 0)  9.05 us
    pallas_call x1, Pallas kernels, scores_lse(): pl.pallas_call(lse_kernel, grid=(heads // 2,), in_specs=pair_specs(rows,...  7.28 us
    all_to_all x1, starting transfers between devices, shards(): lax.all_to_all(logits, HEAD, 0, 0)  6.4 us
  transfers between devices with their start and end apart: 21, of which 9 were waited for; matrix products, arithmetic and copies ran while one was open for 3% of the time, Pallas kernels for 13%

profile of v1, /device:TPU:8, one launch (start us, length us, event | category | flops | bytes accessed | tf_op | source)
XLA Modules:
  0.0 160.4 jit_solution(10660768131176901862)
XLA Ops:
  0.6 1.2 copy-done.4
  1.9 0.8 copy-done.7
  2.7 0.7 copy-done.9
  3.4 1.8 %part_logits.1 = f32[8,64,256]{2,1,0:T(8,128)} custom-call(bf16[512,1024]{1,0:T(8,128)(2,1)S(1)} %copy-done.4, bf16[256,128]{1,0:T(8,128)(2,1)S(1)} %copy-done.7, f32[8,512]{1,0:T(8,128)S(1)} %bitcast.30), custom_call_target="tpu_custom_call" | custom-call | tf_op jit(solution)/shard_map/part_logits/pallas_call | solution.py:177
  5.2 6.4 %all-to-all-start.2 = ((f32[8,64,256]{2,1,0:T(8,128)}), f32[8,64,256]{2,1,0:T(8,128)}, u32[]{:S(2)}, u32[]{:S(2)}) async-start(f32[8,64,256]{2,1,0:T(8,128)} %part_logits.1), calls=%async_computation.2 | async-start | bytes 1048576 | tf_op jit(solution)/shard_map/all_to_all | solution.py:356
  11.6 0.7 multiply_add_fusion.2
  12.3 0.1 copy.15.kp_ref
  12.5 1.9 %copy-done = bf16[512,3072]{1,0:T(8,128)(2,1)S(1)} copy-done((bf16[512,3072]{1,0:T(8,128)(2,1)S(1)}, bf16[512,3072]{1,0:T(8,128)(2,1)}, u32[]{:S(2)}) %copy-start) | copy-done | bytes 3145752
  14.4 1.4 copy-done.2
  15.8 0.7 copy-done.12
  16.5 7.3 %scores_lse.1 = (f32[8,512]{1,0:T(8,128)S(1)}, f32[8,512]{1,0:T(8,128)S(1)}) custom-call(s32[3]{0:T(128)S(1)} %pad_add_fusion.sc_ref, bf16[512,3072]{1,0:T(8,128)(2,1)S(1)} %copy-done, bf16[256,3072]{1,0:T(8,128)(2,1)S(1)} %copy-done.2, s32[256,1]{1,0:T(8,128)S(1)} %copy.15.kp_ref, s32[1,512]{1,0:T(1,128)S(1)} %bitcast.33), custom_call_target="tpu_custom_call" | custom-call | tf_op jit(solution)/shard_map/scores_lse/pallas_call | solution.py:101
  23.8 0.1 collective-permute-start
  23.9 0.1 reshape.44
  24.0 0.2 dynamic-slice_reduce_fusion
  24.2 0.9 collective-permute-done
  25.1 1.1 reduce_sum.37
  26.2 0.2 fusion.6
  26.4 0.2 exponential_reduce_fusion
  26.6 0.3 collective-permute-start.2
  26.9 0.7 broadcast_in_dim.18
  27.6 10.2 %all-to-all-start = ((f32[16,8,512]{2,1,0:T(8,128)}), f32[16,8,512]{2,1,0:T(8,128)}, u32[]{:S(2)}, u32[]{:S(2)}) async-start(f32[16,8,512]{2,1,0:T(8,128)} %broadcast_in_dim.18), calls=%async_computation | async-start | bytes 524288 | tf_op jit(solution)/shard_map/all_to_all | solution.py:349
  37.8 13.3 %all-to-all-done.parts_ref = f32[16,8,512]{2,1,0:T(8,128)} async-done(((f32[16,8,512]{2,1,0:T(8,128)}), f32[16,8,512]{2,1,0:T(8,128)}, u32[]{:S(2)}, u32[]{:S(2)}) %all-to-all-start) | async-done | bytes 262176 | tf_op jit(solution)/shard_map/all_to_all | solution.py:349
  51.1 0.6 broadcast_in_dim.21
  51.8 3.8 %all-to-all-start.3 = ((f32[16,8,128]{2,1,0:T(8,128)}), f32[16,8,128]{2,1,0:T(8,128)S(1)}, u32[]{:S(2)}, u32[]{:S(2)}) async-start(f32[16,8,128]{2,1,0:T(8,128)} %broadcast_in_dim.21), calls=%async_computation.3 | async-start | bytes 131072 | tf_op jit(solution)/shard_map/all_to_all | solution.py:361
  55.6 1.6 %merge_parts.1.mine_ref = f32[8,512]{1,0:T(8,128)} custom-call(f32[16,8,512]{2,1,0:T(8,128)} %all-to-all-done.parts_ref), custom_call_target="tpu_custom_call" | custom-call | tf_op jit(solution)/shard_map/merge_parts/pallas_call | solution.py:193
  57.2 1.4 collective-permute-done.1.other_ref
  58.6 1.4 copy-done.3
  60.0 0.7 copy-done.11
  60.7 4.5 %probs_sum.1 = f32[8,64,256]{2,1,0:T(8,128)S(1)} custom-call(s32[3]{0:T(128)S(1)} %pad_add_fusion.sc_ref, bf16[512,3072]{1,0:T(8,128)(2,1)S(1)} %copy-done.1, bf16[256,3072]{1,0:T(8,128)(2,1)S(1)} %copy-done.3, s32[256,1]{1,0:T(8,128)S(1)} %copy.15.kp_ref, s32[1,512]{1,0:T(1,128)S(1)} %bitcast.34, f32[8,512]{1,0:T(8,128)S(1)} %copy-done.11, ...), custom_call_target="tpu_custom_call" | custom-call | tf_op jit(solution)/shard_map/probs_sum/pallas_call | solution.py:150
  65.2 0.8 copy-done.6
  66.0 5.6 %all-to-all-start.1 = ((f32[8,64,256]{2,1,0:T(8,128)}), f32[8,64,256]{2,1,0:T(8,128)S(1)}, u32[]{:S(2)}, u32[]{:S(2)}) async-start(f32[8,64,256]{2,1,0:T(8,128)} %copy-done.6), calls=%async_computation.1 | async-start | bytes 1048576 | tf_op jit(solution)/shard_map/all_to_all | solution.py:353
  71.7 0.3 reshape.46
  72.0 0.9 dynamic-slice_convert_fusion
  72.9 0.1 copy.21
  73.0 0.1 copy.17
  73.1 0.1 stack_broadcast_in_dim.16
  73.2 0.1 stack_broadcast_in_dim.17
  73.3 0.7 pad_maximum_fusion.1
  74.0 6.0 %all-to-all-done.1.target_ref = f32[8,64,256]{2,1,0:T(8,128)S(1)} async-done(((f32[8,64,256]{2,1,0:T(8,128)}), f32[8,64,256]{2,1,0:T(8,128)S(1)}, u32[]{:S(2)}, u32[]{:S(2)}) %all-to-all-start.1) | async-done | bytes 524320 | tf_op jit(solution)/shard_map/all_to_all | solution.py:353
  80.0 4.8 %all-to-all-start.5 = ((f32[8,2,32,128]{3,2,1,0:T(8,128)}), f32[8,2,32,128]{3,2,1,0:T(8,128)S(1)}, u32[]{:S(2)}, u32[]{:S(2)}) async-start(f32[8,2,32,128]{3,2,1,0:T(8,128)} %pad_maximum_fusion.1), calls=%async_computation.5 | async-start | bytes 524288 | tf_op jit(solution)/shard_map/all_to_all | solution.py:379
  84.8 2.2 %prob_step.1 = (f32[8,64,256]{2,1,0:T(8,128)}, f32[16,8,128]{2,1,0:T(8,128)}) custom-call(f32[8,64,256]{2,1,0:T(8,128)} %copy-done.14, f32[64,256]{1,0:T(8,128)} %copy-done.15, f32[16,8,128]{2,1,0:T(8,128)} %copy-done.16), custom_call_target="tpu_custom_call" | custom-call | tf_op jit(solution)/shard_map/prob_step/pallas_call | solution.py:218
  87.0 3.4 %all-to-all-done.5.both_ref = f32[8,2,32,128]{3,2,1,0:T(8,128)S(1)} async-done(((f32[8,2,32,128]{3,2,1,0:T(8,128)}), f32[8,2,32,128]{3,2,1,0:T(8,128)S(1)}, u32[]{:S(2)}, u32[]{:S(2)}) %all-to-all-start.5) | async-done | bytes 262176 | tf_op jit(solution)/shard_map/all_to_all | solution.py:379
  90.4 5.2 %all-to-all-start.7 = ((f32[8,64,256]{2,1,0:T(8,128)}), f32[8,64,256]{2,1,0:T(8,128)S(1)}, u32[]{:S(2)}, u32[]{:S(2)}) async-start(f32[8,64,256]{2,1,0:T(8,128)} %get-tuple-element.13), calls=%async_computation.7 | async-start | bytes 1048576 | tf_op jit(solution)/shard_map/all_to_all | solution.py:365
  95.6 5.9 %collective-permute-start.4 = (f32[256,128]{1,0:T(8,128)S(1)}, f32[256,128]{1,0:T(8,128)S(1)}, u32[]{:S(2)}, u32[]{:S(2)}) collective-permute-start(f32[256,128]{1,0:T(8,128)S(1)} %get-tuple-element.17), channel_id=1, source_target_pairs={{0,16},{8,24},{16,0},{24,8},{1,17},{9,25},{17,1},{25,9},{2,18},{10... | collective-permute-start | bytes 393224 | tf_op jit(solution)/shard_map/ppermute | solution.py:32
  101.5 0.6 collective-permute-start.3
  102.1 3.6 %collective-permute-start.5 = (f32[256,128]{1,0:T(8,128)S(1)}, f32[256,128]{1,0:T(8,128)S(1)}, u32[]{:S(2)}, u32[]{:S(2)}) collective-permute-start(f32[256,128]{1,0:T(8,128)S(1)} %get-tuple-element.17), channel_id=1, source_target_pairs={{0,24},{8,0},{16,8},{24,16},{1,25},{9,1},{17,9},{25,17},{2,26},{10... | collective-permute-start | bytes 393224 | tf_op jit(solution)/shard_map/ppermute | solution.py:32
  105.7 9.5 %collective-permute-done.4 = f32[256,128]{1,0:T(8,128)S(1)} collective-permute-done((f32[256,128]{1,0:T(8,128)S(1)}, f32[256,128]{1,0:T(8,128)S(1)}, u32[]{:S(2)}, u32[]{:S(2)}) %collective-permute-start.4) | collective-permute-done | bytes 131104 | tf_op jit(solution)/shard_map/ppermute | solution.py:32
  115.1 0.7 collective-permute-done.3
  115.8 2.8 %collective-permute-start.8 = (f32[4,256,128]{2,1,0:T(8,128)S(1)}, f32[4,256,128]{2,1,0:T(8,128)S(1)}, u32[]{:S(2)}, u32[]{:S(2)}) collective-permute-start(f32[4,256,128]{2,1,0:T(8,128)S(1)} %pad_maximum_fusion.ik0_ref), channel_id=1, source_target_pairs={{0,6},{2,0},{4,2},{6,4},{1,7},{3,1},{5,3},{7,5},{8,14},{10,8},{12,... | collective-permute-start | bytes 1572872 | tf_op jit(solution)/shard_map/ppermute | solution.py:32
  118.6 0.9 collective-permute-start.7
  119.4 0.9 collective-permute-start.6
  120.3 5.6 %all-to-all-start.4 = ((f32[16,8,128]{2,1,0:T(8,128)}), f32[16,8,128]{2,1,0:T(8,128)S(1)}, u32[]{:S(2)}, u32[]{:S(2)}) async-start(f32[16,8,128]{2,1,0:T(8,128)} %get-tuple-element.10), calls=%async_computation.4 | async-start | bytes 131072 | tf_op jit(solution)/shard_map/all_to_all | solution.py:384
  125.9 1.9 %key_part_grad.1 = f32[256,128]{1,0:T(8,128)S(1)} custom-call(f32[8,64,256]{2,1,0:T(8,128)S(1)} %all-to-all-done.7.step_ref, bf16[512,1024]{1,0:T(8,128)(2,1)S(1)} %copy-done.5, bf16[256,128]{1,0:T(8,128)(2,1)S(1)} %copy-done.8, f32[8,512]{1,0:T(8,128)S(1)} %bitcast.31), custom_call_target="tpu_custom_call" | custom-call | tf_op jit(solution)/shard_map/key_part_grad/pallas_call | solution.py:252
  127.8 1.6 %collective-permute-start.10 = (f32[256,128]{1,0:T(8,128)S(1)}, f32[256,128]{1,0:T(8,128)S(1)}, u32[]{:S(2)}, u32[]{:S(2)}) collective-permute-start(f32[256,128]{1,0:T(8,128)S(1)} %key_part_grad.1), channel_id=1, source_target_pairs={{0,128},{128,0},{1,129},{129,1},{2,130},{130,2},{3,131},{131,3},{4... | collective-permute-start | bytes 393224 | tf_op jit(solution)/shard_map/ppermute | solution.py:32
  129.4 8.3 %collective-permute-done.8.ik3_ref = f32[4,256,128]{2,1,0:T(8,128)S(1)} collective-permute-done((f32[4,256,128]{2,1,0:T(8,128)S(1)}, f32[4,256,128]{2,1,0:T(8,128)S(1)}, u32[]{:S(2)}, u32[]{:S(2)}) %collective-permute-start.8) | collective-permute-done | bytes 524320 | tf_op jit(solution)/shard_map/ppermute | solution.py:32
  137.8 3.7 %collective-permute-done.6.ik1_ref = f32[4,256,128]{2,1,0:T(8,128)} collective-permute-done((f32[4,256,128]{2,1,0:T(8,128)S(1)}, f32[4,256,128]{2,1,0:T(8,128)}, u32[]{:S(2)}, u32[]{:S(2)}) %collective-permute-start.6) | collective-permute-done | bytes 524320 | tf_op jit(solution)/shard_map/ppermute | solution.py:32
  141.5 2.7 %query_part_grad.1 = (f32[8,16,128]{2,1,0:T(8,128)S(1)}, f32[8,16,128]{2,1,0:T(8,128)S(1)}) custom-call(s32[3]{0:T(128)S(1)} %pad_add_fusion.sc_ref, f32[16,8,128]{2,1,0:T(8,128)S(1)} %all-to-all-done.4.step_ref, f32[8,2,32,128]{3,2,1,0:T(8,128)S(1)} %all-to-all-done.5.both_ref, f32[4,256,128]{2,1,0:T(8,128)S(1)} %pad_maximum_fusion.ik0_ref, ...), custom_call_target="tpu_custom_call" | custom-call | tf_op jit(solution)/shard_map/query_part_grad/pallas_call | solution.py:296
  144.2 0.1 collective-permute-start.9
  144.4 0.8 collective-permute-start.13
  145.1 2.3 %collective-permute-start.12 = (f32[256,128]{1,0:T(8,128)S(1)}, f32[256,128]{1,0:T(8,128)S(1)}, u32[]{:S(2)}, u32[]{:S(2)}) collective-permute-start(f32[256,128]{1,0:T(8,128)S(1)} %add.78), channel_id=1, source_target_pairs={{0,64},{32,96},{64,0},{96,32},{1,65},{33,97},{65,1},{97,33},{2,66}... | collective-permute-start | bytes 393224 | tf_op jit(solution)/shard_map/ppermute | solution.py:32
  147.5 1.7 %collective-permute-start.11 = (f32[256,128]{1,0:T(8,128)S(1)}, f32[256,128]{1,0:T(8,128)S(1)}, u32[]{:S(2)}, u32[]{:S(2)}) collective-permute-start(f32[256,128]{1,0:T(8,128)S(1)} %add.78), channel_id=1, source_target_pairs={{0,32},{32,64},{64,96},{96,0},{1,33},{33,65},{65,97},{97,1},{2,34}... | collective-permute-start | bytes 393224 | tf_op jit(solution)/shard_map/ppermute | solution.py:32
  149.2 9.0 %all_to_all.40.parts_ref = f32[8,16,128]{2,1,0:T(8,128)} all-to-all(f32[8,16,128]{2,1,0:T(8,128)S(1)} %add.77), channel_id=1, replica_groups=mesh['z_lo'=2,'y'=4,'z_hi'=4,'x'=4,'core'=2] {'z_lo','y'}, dimensions={0} | all-to-all | bytes 131072 | tf_op jit(solution)/shard_map/all_to_all | solution.py:387
  158.2 1.5 place_rows.1
  159.7 0.7 add_add_fusion
  (55 shorter events, 0.4 us)
Async XLA Ops:
  0.6 1.2 copy-start.4
  1.9 0.8 copy-start.7
  2.7 0.7 copy-start.9
  5.2 18.7 %copy-start.13 = (s32[512]{0:T(512)S(1)}, s32[512]{0:T(512)}, u32[]{:S(2)}) copy-start(s32[512]{0:T(512)} %param.12) | copy-start | bytes 6148
  5.2 19.9 %all-to-all-start.2 = ((f32[8,64,256]{2,1,0:T(8,128)}), f32[8,64,256]{2,1,0:T(8,128)}, u32[]{:S(2)}, u32[]{:S(2)}) async-start(f32[8,64,256]{2,1,0:T(8,128)} %part_logits.1), calls=%async_computation.2 | async-start | bytes 1048576 | tf_op jit(solution)/shard_map/all_to_all | solution.py:356
  12.5 1.9 %copy-start = (bf16[512,3072]{1,0:T(8,128)(2,1)S(1)}, bf16[512,3072]{1,0:T(8,128)(2,1)}, u32[]{:S(2)}) copy-start(bf16[512,3072]{1,0:T(8,128)(2,1)} %q_ref.3) | copy-start | bytes 9437188
  14.4 1.4 copy-start.2
  15.8 0.7 copy-start.12
  16.5 42.1 %copy-start.1 = (bf16[512,3072]{1,0:T(8,128)(2,1)S(1)}, bf16[512,3072]{1,0:T(8,128)(2,1)}, u32[]{:S(2)}) copy-start(bf16[512,3072]{1,0:T(8,128)(2,1)} %q_ref.3) | copy-start | bytes 9437188
  23.8 1.3 collective-permute-start
  26.4 38.9 %copy-start.15 = (f32[64,256]{1,0:T(8,128)}, f32[64,256]{1,0:T(8,128)S(1)}, u32[]{:S(2)}) copy-start(f32[64,256]{1,0:T(8,128)S(1)} %get-tuple-element.15.logits_ref) | copy-start | bytes 196612
  26.6 11.2 %collective-permute-start.2 = (f32[8,128]{1,0:T(8,128)S(1)}, f32[8,128]{1,0:T(8,128)S(1)}, u32[]{:S(2)}, u32[]{:S(2)}) collective-permute-start(f32[8,128]{1,0:T(8,128)S(1)} %stack_broadcast_in_dim.14), channel_id=1, source_target_pairs={{0,1},{1,0},{2,3},{3,2},{4,5},{5,4},{6,7},{7,6},{8,9},{9,8},{10,11... | collective-permute-start | bytes 12296 | tf_op jit(solution)/shard_map/ppermute | solution.py:32
  27.6 23.5 %all-to-all-start = ((f32[16,8,512]{2,1,0:T(8,128)}), f32[16,8,512]{2,1,0:T(8,128)}, u32[]{:S(2)}, u32[]{:S(2)}) async-start(f32[16,8,512]{2,1,0:T(8,128)} %broadcast_in_dim.18), calls=%async_computation | async-start | bytes 524288 | tf_op jit(solution)/shard_map/all_to_all | solution.py:349
  51.8 14.3 %all-to-all-start.3 = ((f32[16,8,128]{2,1,0:T(8,128)}), f32[16,8,128]{2,1,0:T(8,128)S(1)}, u32[]{:S(2)}, u32[]{:S(2)}) async-start(f32[16,8,128]{2,1,0:T(8,128)} %broadcast_in_dim.21), calls=%async_computation.3 | async-start | bytes 131072 | tf_op jit(solution)/shard_map/all_to_all | solution.py:361
  55.5 16.1 %copy-start.10 = (f32[512,8]{0,1:T(8,128)S(1)}, f32[512,8]{0,1:T(8,128)}, u32[]{:S(2)}) copy-start(f32[512,8]{0,1:T(8,128)} %param.11) | copy-start | bytes 49156
  57.2 1.4 collective-permute-start.1
  58.6 1.4 copy-start.3
  60.0 0.7 copy-start.11
  65.2 0.8 copy-start.6
  66.0 29.6 %copy-start.8 = (bf16[256,128]{1,0:T(8,128)(2,1)S(1)}, bf16[256,128]{1,0:T(8,128)(2,1)}, u32[]{:S(2)}) copy-start(bf16[256,128]{1,0:T(8,128)(2,1)} %ik_ref.3) | copy-start | bytes 196612
  66.0 59.9 %copy-start.5 = (bf16[512,1024]{1,0:T(8,128)(2,1)S(1)}, bf16[512,1024]{1,0:T(8,128)(2,1)}, u32[]{:S(2)}) copy-start(bf16[512,1024]{1,0:T(8,128)(2,1)} %iq_ref.3) | copy-start | bytes 3145732
  66.0 18.8 %copy-start.16 = (f32[16,8,128]{2,1,0:T(8,128)}, f32[16,8,128]{2,1,0:T(8,128)S(1)}, u32[]{:S(2)}) copy-start(f32[16,8,128]{2,1,0:T(8,128)S(1)} %all-to-all-done.3.lse_ref) | copy-start | bytes 196612
  66.0 13.9 %all-to-all-start.1 = ((f32[8,64,256]{2,1,0:T(8,128)}), f32[8,64,256]{2,1,0:T(8,128)S(1)}, u32[]{:S(2)}, u32[]{:S(2)}) async-start(f32[8,64,256]{2,1,0:T(8,128)} %copy-done.6), calls=%async_computation.1 | async-start | bytes 1048576 | tf_op jit(solution)/shard_map/all_to_all | solution.py:353
  80.0 4.8 %copy-start.14 = (f32[8,64,256]{2,1,0:T(8,128)}, f32[8,64,256]{2,1,0:T(8,128)S(1)}, u32[]{:S(2)}) copy-start(f32[8,64,256]{2,1,0:T(8,128)S(1)} %all-to-all-done.1.target_ref) | copy-start | bytes 1572868
  80.0 10.4 %all-to-all-start.5 = ((f32[8,2,32,128]{3,2,1,0:T(8,128)}), f32[8,2,32,128]{3,2,1,0:T(8,128)S(1)}, u32[]{:S(2)}, u32[]{:S(2)}) async-start(f32[8,2,32,128]{3,2,1,0:T(8,128)} %pad_maximum_fusion.1), calls=%async_computation.5 | async-start | bytes 524288 | tf_op jit(solution)/shard_map/all_to_all | solution.py:379
  90.4 29.9 %all-to-all-start.7 = ((f32[8,64,256]{2,1,0:T(8,128)}), f32[8,64,256]{2,1,0:T(8,128)S(1)}, u32[]{:S(2)}, u32[]{:S(2)}) async-start(f32[8,64,256]{2,1,0:T(8,128)} %get-tuple-element.13), calls=%async_computation.7 | async-start | bytes 1048576 | tf_op jit(solution)/shard_map/all_to_all | solution.py:365
  95.6 19.5 %collective-permute-start.4 = (f32[256,128]{1,0:T(8,128)S(1)}, f32[256,128]{1,0:T(8,128)S(1)}, u32[]{:S(2)}, u32[]{:S(2)}) collective-permute-start(f32[256,128]{1,0:T(8,128)S(1)} %get-tuple-element.17), channel_id=1, source_target_pairs={{0,16},{8,24},{16,0},{24,8},{1,17},{9,25},{17,1},{25,9},{2,18},{10... | collective-permute-start | bytes 393224 | tf_op jit(solution)/shard_map/ppermute | solution.py:32
  101.5 14.3 %collective-permute-start.3 = (f32[256,128]{1,0:T(8,128)S(1)}, f32[256,128]{1,0:T(8,128)S(1)}, u32[]{:S(2)}, u32[]{:S(2)}) collective-permute-start(f32[256,128]{1,0:T(8,128)S(1)} %get-tuple-element.17), channel_id=1, source_target_pairs={{0,8},{8,16},{16,24},{24,0},{1,9},{9,17},{17,25},{25,1},{2,10},{10... | collective-permute-start | bytes 393224 | tf_op jit(solution)/shard_map/ppermute | solution.py:32
  102.1 13.7 %collective-permute-start.5 = (f32[256,128]{1,0:T(8,128)S(1)}, f32[256,128]{1,0:T(8,128)S(1)}, u32[]{:S(2)}, u32[]{:S(2)}) collective-permute-start(f32[256,128]{1,0:T(8,128)S(1)} %get-tuple-element.17), channel_id=1, source_target_pairs={{0,24},{8,0},{16,8},{24,16},{1,25},{9,1},{17,9},{25,17},{2,26},{10... | collective-permute-start | bytes 393224 | tf_op jit(solution)/shard_map/ppermute | solution.py:32
  115.8 21.9 %collective-permute-start.8 = (f32[4,256,128]{2,1,0:T(8,128)S(1)}, f32[4,256,128]{2,1,0:T(8,128)S(1)}, u32[]{:S(2)}, u32[]{:S(2)}) collective-permute-start(f32[4,256,128]{2,1,0:T(8,128)S(1)} %pad_maximum_fusion.ik0_ref), channel_id=1, source_target_pairs={{0,6},{2,0},{4,2},{6,4},{1,7},{3,1},{5,3},{7,5},{8,14},{10,8},{12,... | collective-permute-start | bytes 1572872 | tf_op jit(solution)/shard_map/ppermute | solution.py:32
  118.6 19.2 %collective-permute-start.7 = (f32[4,256,128]{2,1,0:T(8,128)S(1)}, f32[4,256,128]{2,1,0:T(8,128)}, u32[]{:S(2)}, u32[]{:S(2)}) collective-permute-start(f32[4,256,128]{2,1,0:T(8,128)S(1)} %pad_maximum_fusion.ik0_ref), channel_id=1, source_target_pairs={{0,4},{2,6},{4,0},{6,2},{1,5},{3,7},{5,1},{7,3},{8,12},{10,14},{12... | collective-permute-start | bytes 1572872 | tf_op jit(solution)/shard_map/ppermute | solution.py:32
  119.4 22.1 %collective-permute-start.6 = (f32[4,256,128]{2,1,0:T(8,128)S(1)}, f32[4,256,128]{2,1,0:T(8,128)}, u32[]{:S(2)}, u32[]{:S(2)}) collective-permute-start(f32[4,256,128]{2,1,0:T(8,128)S(1)} %pad_maximum_fusion.ik0_ref), channel_id=1, source_target_pairs={{0,2},{2,4},{4,6},{6,0},{1,3},{3,5},{5,7},{7,1},{8,10},{10,12},{12... | collective-permute-start | bytes 1572872 | tf_op jit(solution)/shard_map/ppermute | solution.py:32
  120.3 21.2 %all-to-all-start.4 = ((f32[16,8,128]{2,1,0:T(8,128)}), f32[16,8,128]{2,1,0:T(8,128)S(1)}, u32[]{:S(2)}, u32[]{:S(2)}) async-start(f32[16,8,128]{2,1,0:T(8,128)} %get-tuple-element.10), calls=%async_computation.4 | async-start | bytes 131072 | tf_op jit(solution)/shard_map/all_to_all | solution.py:384
  127.8 16.5 %collective-permute-start.10 = (f32[256,128]{1,0:T(8,128)S(1)}, f32[256,128]{1,0:T(8,128)S(1)}, u32[]{:S(2)}, u32[]{:S(2)}) collective-permute-start(f32[256,128]{1,0:T(8,128)S(1)} %key_part_grad.1), channel_id=1, source_target_pairs={{0,128},{128,0},{1,129},{129,1},{2,130},{130,2},{3,131},{131,3},{4... | collective-permute-start | bytes 393224 | tf_op jit(solution)/shard_map/ppermute | solution.py:32
  144.2 5.0 %collective-permute-start.9 = (f32[8,16,128]{2,1,0:T(8,128)S(1)}, f32[8,16,128]{2,1,0:T(8,128)S(1)}, u32[]{:S(2)}, u32[]{:S(2)}) collective-permute-start(f32[8,16,128]{2,1,0:T(8,128)S(1)} %get-tuple-element.12), channel_id=1, source_target_pairs={{0,1},{1,0},{2,3},{3,2},{4,5},{5,4},{6,7},{7,6},{8,9},{9,8},{10,11... | collective-permute-start | bytes 196616 | tf_op jit(solution)/shard_map/ppermute | solution.py:32
  144.4 15.4 %collective-permute-start.13 = (f32[256,128]{1,0:T(8,128)S(1)}, f32[256,128]{1,0:T(8,128)S(1)}, u32[]{:S(2)}, u32[]{:S(2)}) collective-permute-start(f32[256,128]{1,0:T(8,128)S(1)} %add.78), channel_id=1, source_target_pairs={{0,96},{32,0},{64,32},{96,64},{1,97},{33,1},{65,33},{97,65},{2,98}... | collective-permute-start | bytes 393224 | tf_op jit(solution)/shard_map/ppermute | solution.py:32
  145.1 14.6 %collective-permute-start.12 = (f32[256,128]{1,0:T(8,128)S(1)}, f32[256,128]{1,0:T(8,128)S(1)}, u32[]{:S(2)}, u32[]{:S(2)}) collective-permute-start(f32[256,128]{1,0:T(8,128)S(1)} %add.78), channel_id=1, source_target_pairs={{0,64},{32,96},{64,0},{96,32},{1,65},{33,97},{65,1},{97,33},{2,66}... | collective-permute-start | bytes 393224 | tf_op jit(solution)/shard_map/ppermute | solution.py:32
  147.5 12.3 %collective-permute-start.11 = (f32[256,128]{1,0:T(8,128)S(1)}, f32[256,128]{1,0:T(8,128)S(1)}, u32[]{:S(2)}, u32[]{:S(2)}) collective-permute-start(f32[256,128]{1,0:T(8,128)S(1)} %add.78), channel_id=1, source_target_pairs={{0,32},{32,64},{64,96},{96,0},{1,33},{33,65},{65,97},{97,1},{2,34}... | collective-permute-start | bytes 393224 | tf_op jit(solution)/shard_map/ppermute | solution.py:32

commit v2 on v0

v2 whole, which is shorter than its diff:
```python
import math

import jax
import jax.numpy as jnp
from jax import lax
from jax.experimental import pallas as pl
from jax.experimental.pallas import tpu as pltpu
from jax.sharding import Mesh
from jax.sharding import PartitionSpec as P

HEADS = 128
HEAD_DIM = 192
IDIM = 128
STRIDE = 8
LANES = 128
NEG_FILL = -1e30
SCORE_SCALE = 1.0 / math.sqrt(HEAD_DIM)
INV_SCALE = 1.0 / math.sqrt(IDIM)

AXES = ("z_lo", "y", "z_hi", "x", "core")
HEAD = ("z_lo", "y")
CTX = ("z_hi", "x", "core")
CHIP = ("z_hi", "x")
F32, BF16 = jnp.float32, jnp.bfloat16
VMEM_SPEC = pl.BlockSpec(memory_space=pltpu.VMEM)
SMEM_SPEC = pl.BlockSpec(memory_space=pltpu.SMEM)
ANY_SPEC = pl.BlockSpec(memory_space=pl.ANY)
PARAMS = pltpu.CompilerParams(vmem_limit_bytes=16 * 2**20)


def shift(value, axis, size, step):
    return lax.ppermute(value, axis, [(i, (i + step) % size) for i in range(size)])


def merge(parts):
    top = jnp.max(parts, axis=0)
    return top + jnp.log(jnp.sum(jnp.exp(parts - top[None]), axis=0))


def dot_t(a, b):
    return lax.dot_general(a, b, (((1,), (1,)), ((), ())), preferred_element_type=F32)


def head_scores(q_ref, k_ref, head):
    lane = lax.broadcasted_iota(jnp.int32, (1, LANES), 1)
    low = (lane < HEAD_DIM - LANES).astype(F32)
    at = head // 2 * 2 * HEAD_DIM + head % 2 * LANES
    q = q_ref[:, at : at + 2 * LANES]
    left, right = k_ref[:, at : at + LANES], k_ref[:, at + LANES : at + 2 * LANES]
    if head % 2 == 0:
        right = right * low.astype(BF16)
    else:
        left = left * (1.0 - low).astype(BF16)
    return dot_t(jnp.concatenate([left, right], axis=1), q) * SCORE_SCALE


def fill_bias(bias, kp_ref, qp_ref):
    bias[...] = jnp.where(kp_ref[...] <= qp_ref[...], 0.0, NEG_FILL)


def fetch(q_hbm, k_hbm, q_ref, k_ref, sems):
    width = 2 * HEAD_DIM
    copies = []
    for i in range(q_hbm.shape[1] // width):
        span = pl.ds(i * width, width)
        pair = [
            pltpu.make_async_copy(q_hbm.at[:, span], q_ref.at[:, span], sems.at[0, i]),
            pltpu.make_async_copy(k_hbm.at[:, span], k_ref.at[:, span], sems.at[1, i]),
        ]
        for copy in pair:
            copy.start()
        copies.append(pair)

    def wait(i):
        for copy in copies[i]:
            copy.wait()

    return wait


def lse_kernel(q_hbm, k_hbm, kp_ref, qp_ref, out_ref, q_ref, k_ref, sems, bias):
    wait = fetch(q_hbm, k_hbm, q_ref, k_ref, sems)
    fill_bias(bias, kp_ref, qp_ref)
    for head in range(out_ref.shape[0]):
        if head % 2 == 0:
            wait(head // 2)
        s = head_scores(q_ref, k_ref, head) + bias[...]
        top = jnp.max(s, axis=0, keepdims=True)
        out_ref[head : head + 1, :] = top + jnp.log(jnp.sum(jnp.exp(s - top), axis=0, keepdims=True))


def fetch_scratch(queries, attn_keys):
    pairs = queries.shape[1] // (2 * HEAD_DIM)
    return [
        pltpu.VMEM(queries.shape, BF16),
        pltpu.VMEM(attn_keys.shape, BF16),
        pltpu.SemaphoreType.DMA((2, pairs)),
        pltpu.VMEM((attn_keys.shape[0], queries.shape[0]), F32),
    ]


def scores_lse(queries, attn_keys, kp, qp):
    rows = queries.shape[0]
    heads = queries.shape[1] // HEAD_DIM
    return pl.pallas_call(
        lse_kernel,
        in_specs=[ANY_SPEC] * 2 + [VMEM_SPEC] * 2,
        out_specs=VMEM_SPEC,
        out_shape=jax.ShapeDtypeStruct((heads, rows), F32),
        scratch_shapes=fetch_scratch(queries, attn_keys),
        compiler_params=PARAMS,
        name="scores_lse",
    )(queries, attn_keys, kp, qp)


def index_logits(parts_ref, kp_ref, qp_ref):
    logits = jnp.sum(parts_ref[...], axis=0) * INV_SCALE
    return logits + jnp.where(kp_ref[...] <= qp_ref[...], 0.0, NEG_FILL)


def join_kernel(sc_ref, lse_ref, parts_ref, kp_ref, qp_ref, keep_ref, give_ref):
    half, rows = lse_ref.shape[0] // 2, lse_ref.shape[1]
    logits = index_logits(parts_ref, kp_ref, qp_ref)
    blk, _ = logits.shape
    top = jnp.max(logits, axis=1, keepdims=True)
    value = top + jnp.log(jnp.sum(jnp.exp(logits - top), axis=1, keepdims=True))
    value = jnp.broadcast_to(value, (blk, LANES))
    value = jnp.concatenate([value, jnp.zeros((LANES - blk, LANES), F32)], axis=0).T
    for out_ref, core in ((keep_ref, sc_ref[0]), (give_ref, 1 - sc_ref[0])):
        out_ref[:, :rows] = lse_ref[pl.ds(pl.multiple_of(core * half, half), half), :]
        out_ref[:, rows:] = value[:half]


def join_lse(sc, lse, parts, kp_row, qp_a):
    heads, rows = lse.shape
    out = jax.ShapeDtypeStruct((heads // 2, rows + LANES), F32)
    return pl.pallas_call(
        join_kernel,
        in_specs=[SMEM_SPEC] + [VMEM_SPEC] * 4,
        out_specs=[VMEM_SPEC] * 2,
        out_shape=[out, out],
        compiler_params=PARAMS,
        name="join_lse",
    )(sc, lse, parts, kp_row, qp_a)


def pair_kernel(mine_ref, got_ref, out_ref):
    both = merge(jnp.stack([mine_ref[...], got_ref[...]]))
    for c in range(out_ref.shape[0]):
        out_ref[c] = both


def pair_merge(mine, got, n_chip):
    return pl.pallas_call(
        pair_kernel,
        in_specs=[VMEM_SPEC] * 2,
        out_specs=VMEM_SPEC,
        out_shape=jax.ShapeDtypeStruct((n_chip, *mine.shape), F32),
        compiler_params=PARAMS,
        name="pair_merge",
    )(mine, got)


def merge_kernel(parts_ref, out_ref):
    out_ref[...] = merge(parts_ref[...])


def merge_parts(parts):
    return pl.pallas_call(
        merge_kernel,
        in_specs=[VMEM_SPEC],
        out_specs=VMEM_SPEC,
        out_shape=jax.ShapeDtypeStruct(parts.shape[1:], F32),
        compiler_params=PARAMS,
        name="merge_parts",
    )(parts)


def split_rows(tr, out_ref, value):
    turned = value.T
    n, blk, keys = out_ref.shape
    for half in range(keys // LANES):
        span = slice(half * LANES, (half + 1) * LANES)
        tr[half * n * blk : (half + 1) * n * blk, :] = turned[:, span]
        for h in range(n):
            out_ref[h, :, span] = tr[pl.ds(half * n * blk + h, blk, stride=n), :]


def probs_kernel(sc_ref, q_hbm, k_hbm, kp_ref, qp_ref, mine_ref, other_ref, out_ref, q_ref, k_ref, sems, bias, lse, tr):
    wait = fetch(q_hbm, k_hbm, q_ref, k_ref, sems)
    fill_bias(bias, kp_ref, qp_ref)
    half, rows = mine_ref.shape[0], lse.shape[1]
    for ref, core in ((mine_ref, sc_ref[0]), (other_ref, 1 - sc_ref[0])):
        lse[pl.ds(pl.multiple_of(core * half, half), half), :] = ref[:, :rows]
    total = None
    for head in range(0, lse.shape[0], 2):
        wait(head // 2)
        pair = [
            jnp.exp(head_scores(q_ref, k_ref, h) + bias[...] - lse[h : h + 1, :]) for h in (head, head + 1)
        ]
        total = pair[0] + pair[1] if total is None else total + (pair[0] + pair[1])
    split_rows(tr, out_ref, total)


def probs_sum(sc, queries, attn_keys, kp, qp, mine, other, n_head):
    rows, keys = queries.shape[0], attn_keys.shape[0]
    heads = queries.shape[1] // HEAD_DIM
    return pl.pallas_call(
        probs_kernel,
        in_specs=[SMEM_SPEC] + [ANY_SPEC] * 2 + [VMEM_SPEC] * 4,
        out_specs=VMEM_SPEC,
        out_shape=jax.ShapeDtypeStruct((n_head, rows // n_head, keys), F32),
        scratch_shapes=fetch_scratch(queries, attn_keys)
        + [pltpu.VMEM((heads, rows), F32), pltpu.VMEM((rows * keys // LANES, LANES), F32)],
        compiler_params=PARAMS,
        name="probs_sum",
    )(sc, queries, attn_keys, kp, qp, mine, other)


def logits_kernel(iq_ref, ik_ref, wt_ref, out_ref, wide_ref, tr):
    total = None
    for j in range(wt_ref.shape[0]):
        act = dot_t(ik_ref[...], iq_ref[:, j * IDIM : (j + 1) * IDIM])
        term = jnp.maximum(act, 0.0) * wt_ref[j : j + 1, :]
        total = term if total is None else total + term
    split_rows(tr, out_ref, total)
    wide_ref[...] = ik_ref[...].astype(F32)


def part_logits(iq, ik, wt, n_head):
    rows, keys = iq.shape[0], ik.shape[0]
    return pl.pallas_call(
        logits_kernel,
        in_specs=[VMEM_SPEC] * 3,
        out_specs=[VMEM_SPEC] * 2,
        out_shape=[
            jax.ShapeDtypeStruct((n_head, rows // n_head, keys), F32),
            jax.ShapeDtypeStruct(ik.shape, F32),
        ],
        scratch_shapes=[pltpu.VMEM((rows * keys // LANES, LANES), F32)],
        compiler_params=PARAMS,
        name="part_logits",
    )(iq, ik, wt)


def step_kernel(sc_ref, target_ref, index_ref, lse_ref, kp_ref, qp_ref, keep_ref, give_ref, tmp):
    target = jnp.sum(target_ref[...], axis=0) * (1.0 / HEADS)
    blk, keys = target.shape
    rows = lse_ref.shape[1] - LANES
    lse = lse_ref[:8, rows:].T[:blk, :1]
    step = jnp.exp(index_logits(index_ref, kp_ref, qp_ref) - lse) - target
    for half in range(keys // LANES):
        span = slice(half * LANES, (half + 1) * LANES)
        tmp[half * blk : (half + 1) * blk, :] = step[:, span]
        for out_ref, core in ((keep_ref, sc_ref[0]), (give_ref, 1 - sc_ref[0])):
            for x in range(4):
                for r in range(2):
                    out_ref[half, pl.ds(8 * x + r, 4, stride=2), :] = tmp[
                        pl.ds(half * blk + 4 * x + 2 * core + r, 4, stride=16), :
                    ]


def prob_step(sc, target_parts, index_parts, lse, kp_row, qp_a):
    _, blk, keys = target_parts.shape
    out = jax.ShapeDtypeStruct((keys // LANES, blk // 2, LANES), F32)
    return pl.pallas_call(
        step_kernel,
        in_specs=[SMEM_SPEC] + [VMEM_SPEC] * 5,
        out_specs=[VMEM_SPEC] * 2,
        out_shape=[out, out],
        scratch_shapes=[pltpu.VMEM((blk * keys // LANES, LANES), F32)],
        compiler_params=PARAMS,
        name="prob_step",
    )(sc, target_parts, index_parts, lse, kp_row, qp_a)


def wide_kernel(mine_ref, got_ref, out_ref):
    n = mine_ref.shape[0]
    for h in range(out_ref.shape[0]):
        out_ref[h, :n] = mine_ref[...]
        out_ref[h, n:] = got_ref[...]


def widen(mine, got, n_head):
    n, blk, _ = mine.shape
    return pl.pallas_call(
        wide_kernel,
        in_specs=[VMEM_SPEC] * 2,
        out_specs=VMEM_SPEC,
        out_shape=jax.ShapeDtypeStruct((n_head, 2 * n, blk, LANES), F32),
        compiler_params=PARAMS,
        name="widen",
    )(mine, got)


def row_blocks(sc_ref, x):
    return [pl.multiple_of(128 * z + 32 * x + 16 * sc_ref[0], 16) for z in range(4)]


def query_kernel(sc_ref, step_ref, iq_ref, ik_ref, ik2_ref, w_ref, o1_ref, o2_ref, o3_ref, o0_ref, tr):
    n_head, quarters = step_ref.shape[0], step_ref.shape[1]
    jl = iq_ref.shape[1] // IDIM
    ik = jnp.concatenate([ik_ref[...], ik2_ref[...]], axis=0).astype(BF16)
    for k, out_ref in ((1, o1_ref), (2, o2_ref), (3, o3_ref), (0, o0_ref)):
        x = lax.rem(sc_ref[1] + k, 4)
        size = out_ref.shape[0]
        each = size // n_head
        start = pl.multiple_of(x * each, each)
        for c in range(quarters):
            for h in range(n_head):
                tr[pl.ds(c * size + h, each, stride=n_head), :] = step_ref[h, c, pl.ds(start, each), :]
        step = jnp.concatenate([tr[c * size : (c + 1) * size, :] for c in range(quarters)], axis=1)
        blocks = row_blocks(sc_ref, x)
        iq = jnp.concatenate([iq_ref[pl.ds(b, 16), :] for b in blocks], axis=0)
        w = jnp.concatenate([w_ref[pl.ds(b, 16), :] for b in blocks], axis=0) * INV_SCALE
        for j in range(jl):
            act = dot_t(iq[:, j * IDIM : (j + 1) * IDIM], ik)
            terms = jnp.where(act > 0.0, step * w[:, j : j + 1], 0.0).astype(BF16)
            out_ref[:, j * IDIM : (j + 1) * IDIM] = jnp.dot(terms, ik, preferred_element_type=F32)


def query_pieces(sc, step, iq, ik, ik2, w):
    n_head, quarters, half, _ = step.shape
    size = half * n_head // 4
    out = jax.ShapeDtypeStruct((size, iq.shape[1]), F32)
    return pl.pallas_call(
        query_kernel,
        in_specs=[SMEM_SPEC] + [VMEM_SPEC] * 5,
        out_specs=[VMEM_SPEC] * 4,
        out_shape=[out] * 4,
        scratch_shapes=[pltpu.VMEM((quarters * size, LANES), F32)],
        compiler_params=PARAMS,
        name="query_pieces",
    )(sc, step, iq, ik, ik2, w)


def key_kernel(sc_ref, step_ref, iq_ref, ik_ref, ik2_ref, w_ref, keep_ref, give_ref, tr, iqs, ws):
    n, quarters, half, _ = step_ref.shape
    size = n * half
    turned = []
    for c in range(quarters):
        for h in range(n):
            tr[pl.ds(h, half, stride=n), :] = step_ref[h, c]
        turned.append(tr[...].T)
    step = jnp.concatenate(turned, axis=0)
    for x in range(4):
        for z, b in enumerate(row_blocks(sc_ref, x)):
            at = 64 * x + 16 * z
            iqs[at : at + 16, :] = iq_ref[pl.ds(b, 16), :]
            ws[at : at + 16, :] = w_ref[pl.ds(b, 16), :]
    wt = ws[...].T * INV_SCALE
    ik = jnp.concatenate([ik_ref[...], ik2_ref[...]], axis=0).astype(BF16)
    total = None
    for j in range(iq_ref.shape[1] // IDIM):
        iq = iqs[:, j * IDIM : (j + 1) * IDIM]
        act = dot_t(ik, iq)
        terms = jnp.where(act > 0.0, step * wt[j : j + 1, :], 0.0).astype(BF16)
        part = jnp.dot(terms, iq, preferred_element_type=F32)
        total = part if total is None else total + part
    keys = keep_ref.shape[0]
    keep_ref[...] = total[:keys]
    give_ref[...] = total[keys:]


def key_part_grad(sc, step, iq, ik, ik2, w):
    n, _, half, _ = step.shape
    size = n * half
    out = jax.ShapeDtypeStruct(ik.shape, F32)
    return pl.pallas_call(
        key_kernel,
        in_specs=[SMEM_SPEC] + [VMEM_SPEC] * 5,
        out_specs=[VMEM_SPEC] * 2,
        out_shape=[out, out],
        scratch_shapes=[
            pltpu.VMEM((size, LANES), F32),
            pltpu.VMEM((size, iq.shape[1]), BF16),
            pltpu.VMEM((size, LANES), F32),
        ],
        compiler_params=PARAMS,
        name="key_part_grad",
    )(sc, step, iq, ik, ik2, w)


def shards(queries, attn_keys, index_queries, index_keys, head_weights, query_pos, key_offset):
    rows, keys = queries.shape[0], attn_keys.shape[0]
    n_head, n_chip = lax.axis_size(HEAD), lax.axis_size(CHIP)
    blk = rows // n_head
    hd = lax.axis_index(HEAD)
    sc = jnp.stack([lax.axis_index(a) for a in ("core", "x", "z_hi")]).astype(jnp.int32)

    key_pos = STRIDE * (lax.axis_index(CTX) * keys + jnp.arange(keys, dtype=jnp.int32)) + key_offset
    kp, qp, kp_row = key_pos[:, None], query_pos[None, :], key_pos[None, :]
    qp_a = lax.dynamic_index_in_dim(query_pos.reshape(blk, n_head), hd, 1, True)
    w_pad = jnp.pad(head_weights, ((0, 0), (0, LANES - head_weights.shape[1])))

    index, ik = part_logits(index_queries, index_keys, head_weights.T, n_head)
    index = lax.all_to_all(index, HEAD, 0, 0)
    ik2 = shift(ik, "core", 2, 1)

    lse = scores_lse(queries, attn_keys, kp, qp)
    mine, give = join_lse(sc, lse, index, kp_row, qp_a)
    mine = pair_merge(mine, shift(give, "core", 2, 1), n_chip)
    mine = merge_parts(lax.all_to_all(mine, CHIP, 0, 0))
    other = shift(mine, "core", 2, 1)
    target = probs_sum(sc, queries, attn_keys, kp, qp, mine, other, n_head)
    target = lax.all_to_all(target, HEAD, 0, 0)

    step, give = prob_step(sc, target, index, mine, kp_row, qp_a)
    step = lax.all_to_all(widen(step, shift(give, "core", 2, 1), n_head), HEAD, 0, 0)

    p1, p2, p3, own = query_pieces(sc, step, index_queries, ik, ik2, w_pad)
    own = own + shift(p1, "x", 4, 1) + shift(p2, "x", 4, 2) + shift(p3, "x", 4, 3)
    own = own.reshape(4, own.shape[0] // 4, own.shape[1])
    zi = lax.axis_index("z_hi")
    pieces = [lax.dynamic_index_in_dim(own, (zi + k) % 4, 0, False) for k in range(4)]
    query_grad = pieces[0]
    for k in range(1, 4):
        query_grad = query_grad + shift(pieces[k], "z_hi", 4, k)

    key_part, give = key_part_grad(sc, step, index_queries, ik, ik2, w_pad)
    key_part = key_part + shift(give, "core", 2, 1)
    key_part = key_part + shift(key_part, "z_lo", 2, 1)
    key_grad = key_part
    for k in range(1, 4):
        key_grad = key_grad + shift(key_part, "y", 4, k)
    return (query_grad, key_grad)


def solution(mesh):
    mesh = Mesh(mesh.devices.reshape(2, 4, 4, 4, 2), AXES)
    in_specs = (
        P(None, HEAD),
        P(CTX, HEAD),
        P(None, HEAD),
        P(CTX, None),
        P(None, HEAD),
        P(),
        P(CTX),
    )
    out_specs = (P(CTX, HEAD), P(CTX, None))
    return jax.shard_map(shards, mesh=mesh, in_specs=in_specs, out_specs=out_specs, check_vma=False)
```

time: 647 us -> 128 us (0.20)
  waiting for transfers between devices: 312 us -> 22.7 us
  blocking collectives: 276 us -> 38.2 us
  starting transfers between devices: 0.16 us -> 28.6 us
  Pallas kernels: 0 us -> 23.9 us
  matrix products: 15.8 us -> 0 us
  between operations: 13.9 us -> 0.87 us
  other arithmetic: 15.1 us -> 3.29 us
    psum x3 -> x0, waiting for transfers between devices: 215 us -> none  [the longest x1 74.4 us: shards(): target = lax.psum(target_part, 'head') / HEADS]
    pmax x1 -> x0, blocking collectives: 138 us -> none  [row_stats(): top_value = lax.pmax(local_top, 'ctx')]
    psum x1 -> x0, blocking collectives: 138 us -> none  [row_stats(): total_mass = lax.psum(local_mass, 'ctx')]
    reduce_scatter x1 -> x0, waiting for transfers between devices: 97.6 us -> none  [shards(): lax.psum_scatter(result.reshape(query_rows // lax.axis_size('ctx') * lax....]
    all_to_all x0 -> x2, blocking collectives: none -> 38.2 us  [the longest x1 23.5 us: shards(): mine = merge_parts(lax.all_to_all(mine, CHIP, 0, 0))]
    pallas_call x0 -> x10, Pallas kernels: none -> 23.9 us  [the longest x1 5.88 us: query_pieces(): pl.pallas_call(query_kernel, in_specs=[SMEM_SPEC] + [VMEM_SPEC] * 5, out_...]
    ppermute x0 -> x15, starting transfers between devices: none -> 17.1 us  [shift(): lax.ppermute(value, axis, [(i, (i + step) % size) for i in range(size)])]
    dot_general x4 -> x0, matrix products: 15.8 us -> none  [the longest x1 6.82 us: shards(): jnp.einsum('thd,shd->hts', query_heads, key_heads, preferred_element_type...]
  transfers between devices with their start and end apart: 4 -> 17, of which waited for: 4 -> 11; matrix products, arithmetic and copies ran while one was open for 3% -> 3% of each run, Pallas kernels for 0% -> 6%
where the time goes in v2:
time: 128 us; the launch traced here: 127 us
  blocking collectives  38.2 us (30%)
  starting transfers between devices  28.6 us (22%)
  Pallas kernels  23.9 us (19%)
  waiting for transfers between devices  22.7 us (18%)
  local copies, waits for them, and re-layouts  9.32 us (7%)
  other arithmetic  3.29 us (3%)
    all_to_all x1, blocking collectives, shards(): mine = merge_parts(lax.all_to_all(mine, CHIP, 0, 0))  23.5 us
    ppermute x15, starting transfers between devices, shift(): lax.ppermute(value, axis, [(i, (i + step) % size) for i in range(size)])  17.1 us
    ppermute x15, waiting for transfers between devices, shift(): lax.ppermute(value, axis, [(i, (i + step) % size) for i in range(size)])  15.4 us
    all_to_all x1, blocking collectives, shards(): target = lax.all_to_all(target, HEAD, 0, 0)  14.7 us
    unnamed x23, local copies, waits for them, and re-layouts  8.3 us
    all_to_all x1, waiting for transfers between devices, shards(): lax.all_to_all(widen(step, shift(give, 'core', 2, 1), n_head), HEAD, 0, 0)  7.29 us
    all_to_all x1, starting transfers between devices, shards(): index = lax.all_to_all(index, HEAD, 0, 0)  6.27 us
    pallas_call x1, Pallas kernels, query_pieces(): pl.pallas_call(query_kernel, in_specs=[SMEM_SPEC] + [VMEM_SPEC] * 5, out_...  5.88 us
  transfers between devices with their start and end apart: 17, of which 11 were waited for; matrix products, arithmetic and copies ran while one was open for 3% of the time, Pallas kernels for 6%

profile of v2, /device:TPU:8, one launch (start us, length us, event | category | flops | bytes accessed | tf_op | source)
XLA Modules:
  0.0 126.9 jit_solution(15934627163922408846)
XLA Ops:
  0.6 0.0 copy-start.2
  0.6 1.2 copy-done.2
  1.9 0.7 copy-done.6
  2.6 0.8 copy-done.8
  3.4 1.7 %part_logits.1 = (f32[8,64,256]{2,1,0:T(8,128)}, f32[256,128]{1,0:T(8,128)S(1)}) custom-call(bf16[512,1024]{1,0:T(8,128)(2,1)S(1)} %copy-done.2, bf16[256,128]{1,0:T(8,128)(2,1)S(1)} %copy-done.8, f32[8,512]{1,0:T(8,128)S(1)} %bitcast.20), custom_call_target="tpu_custom_call" | custom-call | tf_op jit(solution)/shard_map/part_logits/pallas_call | solution.py:232
  5.2 6.3 %all-to-all-start = ((f32[8,64,256]{2,1,0:T(8,128)}), f32[8,64,256]{2,1,0:T(8,128)}, u32[]{:S(2)}, u32[]{:S(2)}) async-start(f32[8,64,256]{2,1,0:T(8,128)} %get-tuple-element.14), calls=%async_computation | async-start | bytes 1048576 | tf_op jit(solution)/shard_map/all_to_all | solution.py:397
  11.4 0.8 reshape.10
  12.2 0.7 multiply_add_fusion
  12.9 0.1 copy.11.kp_ref
  13.0 0.0 copy-start
  13.0 1.9 %copy-done = bf16[512,3072]{1,0:T(8,128)(2,1)S(1)} copy-done((bf16[512,3072]{1,0:T(8,128)(2,1)S(1)}, bf16[512,3072]{1,0:T(8,128)(2,1)}, u32[]{:S(2)}) %copy-start) | copy-done | bytes 3145752
  14.9 1.4 %copy-done.4 = bf16[256,3072]{1,0:T(8,128)(2,1)S(1)} copy-done((bf16[256,3072]{1,0:T(8,128)(2,1)S(1)}, bf16[256,3072]{1,0:T(8,128)(2,1)}, u32[]{:S(2)}) %copy-start.4) | copy-done | bytes 1572888
  16.3 0.7 copy-done.9
  17.0 5.4 %scores_lse.1.lse_ref = f32[16,512]{1,0:T(8,128)S(1)} custom-call(bf16[512,3072]{1,0:T(8,128)(2,1)S(1)} %copy-done, bf16[256,3072]{1,0:T(8,128)(2,1)S(1)} %copy-done.4, s32[256,1]{1,0:T(8,128)S(1)} %copy.11.kp_ref, s32[1,512]{1,0:T(1,128)S(1)} %bitcast.21), custom_call_target="tpu_custom_call" | custom-call | tf_op jit(solution)/shard_map/scores_lse/pallas_call | solution.py:105
  22.4 0.1 pad_add_fusion.sc_ref
  22.5 0.1 constant_dynamic-slice_fusion.qp_ref
  22.6 0.0 all-to-all-done.parts_ref.index_ref
  22.6 1.4 %join_lse.1 = (f32[8,640]{1,0:T(8,128)S(1)}, f32[8,640]{1,0:T(8,128)S(1)}) custom-call(s32[3]{0:T(128)S(1)} %pad_add_fusion.sc_ref, f32[16,512]{1,0:T(8,128)S(1)} %scores_lse.1.lse_ref, f32[8,64,256]{2,1,0:T(8,128)} %all-to-all-done.parts_ref.index_ref, s32[1,256]{1,0:T(1,128)S(1)} %bitcast.24, s32[64,1]{1,0:T(8,128)S(1)} %constant_dynamic-slice_fusion.qp_ref), custom_call_target="tpu_custom_call" | custom-call | tf_op jit(solution)/shard_map/join_lse/pallas_call | solution.py:137
  23.9 0.0 collective-permute-start
  24.0 1.2 collective-permute-done.got_ref
  25.2 23.5 %all_to_all.20.parts_ref = f32[16,8,640]{2,1,0:T(8,128)S(1)} all-to-all(f32[16,8,640]{2,1,0:T(8,128)S(1)} %pair_merge.1), channel_id=1, replica_groups=mesh['z_lo'=2,'y'=4,'z_hi'=4,'x'=4,'core'=2] {'z_hi','x'}, dimensions={0} | all-to-all | bytes 655360 | tf_op jit(solution)/shard_map/all_to_all | solution.py:403
  48.7 0.1 merge_parts.1.mine_ref.lse_ref
  48.8 0.1 collective-permute-start.1
  48.9 1.2 collective-permute-done.1.other_ref
  50.1 1.4 %copy-done.5 = bf16[256,3072]{1,0:T(8,128)(2,1)S(1)} copy-done((bf16[256,3072]{1,0:T(8,128)(2,1)S(1)}, bf16[256,3072]{1,0:T(8,128)(2,1)}, u32[]{:S(2)}) %copy-start.5) | copy-done | bytes 1572888
  51.5 5.3 %probs_sum.1 = f32[8,64,256]{2,1,0:T(8,128)S(1)} custom-call(s32[3]{0:T(128)S(1)} %pad_add_fusion.sc_ref, bf16[512,3072]{1,0:T(8,128)(2,1)S(1)} %copy-done.1, bf16[256,3072]{1,0:T(8,128)(2,1)S(1)} %copy-done.5, s32[256,1]{1,0:T(8,128)S(1)} %copy.11.kp_ref, s32[1,512]{1,0:T(1,128)S(1)} %bitcast.22, f32[8,640]{1,0:T(8,128)S(1)} %merge_parts.1.mine_ref.lse_ref, ...), custom_call_target="tpu_custom_call" | custom-call | tf_op jit(solution)/shard_map/probs_sum/pallas_call | solution.py:208
  56.8 0.0 copy-start.7
  56.8 0.0 copy-start.3
  56.8 14.7 %all_to_all.21.target_ref = f32[8,64,256]{2,1,0:T(8,128)S(1)} all-to-all(f32[8,64,256]{2,1,0:T(8,128)S(1)} %probs_sum.1), channel_id=1, replica_groups=mesh['z_lo'=2,'y'=4,'z_hi'=4,'x'=4,'core'=2] {'z_lo','y'}, dimensions={0} | all-to-all | bytes 1048576 | tf_op jit(solution)/shard_map/all_to_all | solution.py:406
  71.5 1.2 prob_step.1
  72.8 0.1 collective-permute-start.2
  72.9 1.2 collective-permute-done.2.got_ref
  74.1 0.8 widen.1
  74.9 5.2 %all-to-all-start.3 = ((f32[8,4,32,128]{3,2,1,0:T(8,128)}), f32[8,4,32,128]{3,2,1,0:T(8,128)S(1)}, u32[]{:S(2)}, u32[]{:S(2)}) async-start(f32[8,4,32,128]{3,2,1,0:T(8,128)} %widen.1), calls=%async_computation.3 | async-start | bytes 1048576 | tf_op jit(solution)/shard_map/all_to_all | solution.py:409
  80.1 0.0 collective-permute-start.3
  80.1 0.1 copy.12
  80.3 1.2 collective-permute-done.3.ik2_ref
  81.4 7.3 %all-to-all-done.3.step_ref = f32[8,4,32,128]{3,2,1,0:T(8,128)S(1)} async-done(((f32[8,4,32,128]{3,2,1,0:T(8,128)}), f32[8,4,32,128]{3,2,1,0:T(8,128)S(1)}, u32[]{:S(2)}, u32[]{:S(2)}) %all-to-all-start.3) | async-done | bytes 524320 | tf_op jit(solution)/shard_map/all_to_all | solution.py:409
  88.7 5.9 %query_pieces.1 = (f32[64,1024]{1,0:T(8,128)S(1)}, f32[64,1024]{1,0:T(8,128)S(1)}, f32[64,1024]{1,0:T(8,128)S(1)}, f32[64,1024]{1,0:T(8,128)S(1)}) custom-call(s32[3]{0:T(128)S(1)} %pad_add_fusion.sc_ref, f32[8,4,32,128]{3,2,1,0:T(8,128)S(1)} %all-to-all-done.3.step_ref, bf16[512,1024]{1,0:T(8,128)(2,1)S(1)} %copy-done.3, ...), custom_call_target="tpu_custom_call" | custom-call | tf_op jit(solution)/shard_map/query_pieces/pallas_call | solution.py:326
  94.6 0.6 collective-permute-start.4
  95.2 2.0 %collective-permute-start.5 = (f32[64,1024]{1,0:T(8,128)S(1)}, f32[64,1024]{1,0:T(8,128)}, u32[]{:S(2)}, u32[]{:S(2)}) collective-permute-start(f32[64,1024]{1,0:T(8,128)S(1)} %get-tuple-element.22), channel_id=1, source_target_pairs={{0,4},{2,6},{4,0},{6,2},{1,5},{3,7},{5,1},{7,3},{8,12},{10,14},{12... | collective-permute-start | bytes 786440 | tf_op jit(solution)/shard_map/ppermute | solution.py:32
  97.2 1.8 %collective-permute-start.6 = (f32[64,1024]{1,0:T(8,128)S(1)}, f32[64,1024]{1,0:T(8,128)}, u32[]{:S(2)}, u32[]{:S(2)}) collective-permute-start(f32[64,1024]{1,0:T(8,128)S(1)} %get-tuple-element.23), channel_id=1, source_target_pairs={{0,6},{2,0},{4,2},{6,4},{1,7},{3,1},{5,3},{7,5},{8,14},{10,8},{12,... | collective-permute-start | bytes 786440 | tf_op jit(solution)/shard_map/ppermute | solution.py:32
  99.0 2.1 %key_part_grad.1 = (f32[256,128]{1,0:T(8,128)S(1)}, f32[256,128]{1,0:T(8,128)S(1)}) custom-call(s32[3]{0:T(128)S(1)} %pad_add_fusion.sc_ref, f32[8,4,32,128]{3,2,1,0:T(8,128)S(1)} %all-to-all-done.3.step_ref, bf16[512,1024]{1,0:T(8,128)(2,1)S(1)} %copy-done.3, f32[256,128]{1,0:T(8,128)S(1)} %get-tuple-element.19.ik_ref, ...), custom_call_target="tpu_custom_call" | custom-call | tf_op jit(solution)/shard_map/key_part_grad/pallas_call | solution.py:369
  101.1 0.1 collective-permute-start.10
  101.2 1.3 %collective-permute-done.10 = f32[256,128]{1,0:T(8,128)S(1)} collective-permute-done((f32[256,128]{1,0:T(8,128)S(1)}, f32[256,128]{1,0:T(8,128)S(1)}, u32[]{:S(2)}, u32[]{:S(2)}) %collective-permute-start.10) | collective-permute-done | bytes 131104 | tf_op jit(solution)/shard_map/ppermute | solution.py:32
  102.5 1.5 %collective-permute-start.11 = (f32[256,128]{1,0:T(8,128)S(1)}, f32[256,128]{1,0:T(8,128)S(1)}, u32[]{:S(2)}, u32[]{:S(2)}) collective-permute-start(f32[256,128]{1,0:T(8,128)S(1)} %add.116), channel_id=1, source_target_pairs={{0,128},{128,0},{1,129},{129,1},{2,130},{130,2},{3,131},{131,3},{4... | collective-permute-start | bytes 393224 | tf_op jit(solution)/shard_map/ppermute | solution.py:32
  104.1 4.8 %collective-permute-done.4 = f32[64,1024]{1,0:T(8,128)} collective-permute-done((f32[64,1024]{1,0:T(8,128)S(1)}, f32[64,1024]{1,0:T(8,128)}, u32[]{:S(2)}, u32[]{:S(2)}) %collective-permute-start.4) | collective-permute-done | bytes 262176 | tf_op jit(solution)/shard_map/ppermute | solution.py:32
  108.9 0.0 collective-permute-done.5
  108.9 0.6 collective-permute-done.6
  109.5 1.2 add_add_fusion
  110.7 1.0 collective-permute-start.7
  111.7 3.5 %collective-permute-start.8 = (f32[16,1024]{1,0:T(8,128)S(1)}, f32[16,1024]{1,0:T(8,128)S(1)}, u32[]{:S(2)}, u32[]{:S(2)}) collective-permute-start(f32[16,1024]{1,0:T(8,128)S(1)} %get-tuple-element.28), channel_id=1, source_target_pairs={{0,16},{8,24},{16,0},{24,8},{1,17},{9,25},{17,1},{25,9},{2,18},{10... | collective-permute-start | bytes 196616 | tf_op jit(solution)/shard_map/ppermute | solution.py:32
  115.2 1.8 %collective-permute-start.9 = (f32[16,1024]{1,0:T(8,128)S(1)}, f32[16,1024]{1,0:T(8,128)S(1)}, u32[]{:S(2)}, u32[]{:S(2)}) collective-permute-start(f32[16,1024]{1,0:T(8,128)S(1)} %get-tuple-element.27), channel_id=1, source_target_pairs={{0,24},{8,0},{16,8},{24,16},{1,25},{9,1},{17,9},{25,17},{2,26},{10... | collective-permute-start | bytes 196616 | tf_op jit(solution)/shard_map/ppermute | solution.py:32
  117.0 0.0 collective-permute-done.11
  117.1 1.2 collective-permute-start.12
  118.3 1.9 %collective-permute-start.13 = (f32[256,128]{1,0:T(8,128)S(1)}, f32[256,128]{1,0:T(8,128)S(1)}, u32[]{:S(2)}, u32[]{:S(2)}) collective-permute-start(f32[256,128]{1,0:T(8,128)S(1)} %add.117), channel_id=1, source_target_pairs={{0,64},{32,96},{64,0},{96,32},{1,65},{33,97},{65,1},{97,33},{2,66}... | collective-permute-start | bytes 393224 | tf_op jit(solution)/shard_map/ppermute | solution.py:32
  120.2 0.0 collective-permute-done.7
  120.2 1.4 %collective-permute-start.14 = (f32[256,128]{1,0:T(8,128)S(1)}, f32[256,128]{1,0:T(8,128)S(1)}, u32[]{:S(2)}, u32[]{:S(2)}) collective-permute-start(f32[256,128]{1,0:T(8,128)S(1)} %add.117), channel_id=1, source_target_pairs={{0,96},{32,0},{64,32},{96,64},{1,97},{33,1},{65,33},{97,65},{2,98}... | collective-permute-start | bytes 393224 | tf_op jit(solution)/shard_map/ppermute | solution.py:32
  121.6 0.2 collective-permute-done.9
  121.8 0.6 fusion.1
  122.5 0.0 collective-permute-done.12
  122.5 2.4 %collective-permute-done.13 = f32[256,128]{1,0:T(8,128)S(1)} collective-permute-done((f32[256,128]{1,0:T(8,128)S(1)}, f32[256,128]{1,0:T(8,128)S(1)}, u32[]{:S(2)}, u32[]{:S(2)}) %collective-permute-start.13) | collective-permute-done | bytes 131104 | tf_op jit(solution)/shard_map/ppermute | solution.py:32
  124.9 1.3 %collective-permute-done.14 = f32[256,128]{1,0:T(8,128)S(1)} collective-permute-done((f32[256,128]{1,0:T(8,128)S(1)}, f32[256,128]{1,0:T(8,128)S(1)}, u32[]{:S(2)}, u32[]{:S(2)}) %collective-permute-start.14) | collective-permute-done | bytes 131104 | tf_op jit(solution)/shard_map/ppermute | solution.py:32
  126.2 0.7 add_add_fusion.1
  (17 shorter events, 0.1 us)
Async XLA Ops:
  0.6 1.2 copy-start.2
  1.9 0.7 copy-start.6
  2.6 0.8 copy-start.8
  5.2 17.4 %all-to-all-start = ((f32[8,64,256]{2,1,0:T(8,128)}), f32[8,64,256]{2,1,0:T(8,128)}, u32[]{:S(2)}, u32[]{:S(2)}) async-start(f32[8,64,256]{2,1,0:T(8,128)} %get-tuple-element.14), calls=%async_computation | async-start | bytes 1048576 | tf_op jit(solution)/shard_map/all_to_all | solution.py:397
  13.0 1.9 %copy-start = (bf16[512,3072]{1,0:T(8,128)(2,1)S(1)}, bf16[512,3072]{1,0:T(8,128)(2,1)}, u32[]{:S(2)}) copy-start(bf16[512,3072]{1,0:T(8,128)(2,1)} %q_hbm.3) | copy-start | bytes 9437188
  14.9 1.4 %copy-start.4 = (bf16[256,3072]{1,0:T(8,128)(2,1)S(1)}, bf16[256,3072]{1,0:T(8,128)(2,1)}, u32[]{:S(2)}) copy-start(bf16[256,3072]{1,0:T(8,128)(2,1)} %k_hbm.3) | copy-start | bytes 4718596
  16.3 0.7 copy-start.9
  17.0 33.0 %copy-start.1 = (bf16[512,3072]{1,0:T(8,128)(2,1)S(1)}, bf16[512,3072]{1,0:T(8,128)(2,1)}, u32[]{:S(2)}) copy-start(bf16[512,3072]{1,0:T(8,128)(2,1)} %q_hbm.3) | copy-start | bytes 9437188
  17.0 33.0 %copy-start.10 = (s32[512]{0:T(512)S(1)}, s32[512]{0:T(512)}, u32[]{:S(2)}) copy-start(s32[512]{0:T(512)} %param.12) | copy-start | bytes 6148
  23.9 1.2 collective-permute-start
  48.8 1.3 %collective-permute-start.1 = (f32[8,640]{1,0:T(8,128)S(1)}, f32[8,640]{1,0:T(8,128)S(1)}, u32[]{:S(2)}, u32[]{:S(2)}) collective-permute-start(f32[8,640]{1,0:T(8,128)S(1)} %merge_parts.1.mine_ref.lse_ref), channel_id=1, source_target_pairs={{0,1},{1,0},{2,3},{3,2},{4,5},{5,4},{6,7},{7,6},{8,9},{9,8},{10,11... | collective-permute-start | bytes 61448 | tf_op jit(solution)/shard_map/ppermute | solution.py:32
  50.1 1.4 %copy-start.5 = (bf16[256,3072]{1,0:T(8,128)(2,1)S(1)}, bf16[256,3072]{1,0:T(8,128)(2,1)}, u32[]{:S(2)}) copy-start(bf16[256,3072]{1,0:T(8,128)(2,1)} %k_hbm.3) | copy-start | bytes 4718596
  56.8 23.3 %copy-start.7 = (f32[512,8]{0,1:T(8,128)S(1)}, f32[512,8]{0,1:T(8,128)}, u32[]{:S(2)}) copy-start(f32[512,8]{0,1:T(8,128)} %param.11) | copy-start | bytes 49156
  56.8 31.9 %copy-start.3 = (bf16[512,1024]{1,0:T(8,128)(2,1)S(1)}, bf16[512,1024]{1,0:T(8,128)(2,1)}, u32[]{:S(2)}) copy-start(bf16[512,1024]{1,0:T(8,128)(2,1)} %iq_ref.5) | copy-start | bytes 3145732
  72.8 1.3 %collective-permute-start.2 = (f32[2,32,128]{2,1,0:T(8,128)S(1)}, f32[2,32,128]{2,1,0:T(8,128)S(1)}, u32[]{:S(2)}, u32[]{:S(2)}) collective-permute-start(f32[2,32,128]{2,1,0:T(8,128)S(1)} %get-tuple-element.18), channel_id=1, source_target_pairs={{0,1},{1,0},{2,3},{3,2},{4,5},{5,4},{6,7},{7,6},{8,9},{9,8},{10,11... | collective-permute-start | bytes 98312 | tf_op jit(solution)/shard_map/ppermute | solution.py:32
  74.9 13.8 %all-to-all-start.3 = ((f32[8,4,32,128]{3,2,1,0:T(8,128)}), f32[8,4,32,128]{3,2,1,0:T(8,128)S(1)}, u32[]{:S(2)}, u32[]{:S(2)}) async-start(f32[8,4,32,128]{3,2,1,0:T(8,128)} %widen.1), calls=%async_computation.3 | async-start | bytes 1048576 | tf_op jit(solution)/shard_map/all_to_all | solution.py:409
  80.1 1.3 %collective-permute-start.3 = (f32[256,128]{1,0:T(8,128)S(1)}, f32[256,128]{1,0:T(8,128)S(1)}, u32[]{:S(2)}, u32[]{:S(2)}) collective-permute-start(f32[256,128]{1,0:T(8,128)S(1)} %get-tuple-element.19.ik_ref), channel_id=1, source_target_pairs={{0,1},{1,0},{2,3},{3,2},{4,5},{5,4},{6,7},{7,6},{8,9},{9,8},{10,11... | collective-permute-start | bytes 393224 | tf_op jit(solution)/shard_map/ppermute | solution.py:32
  94.6 14.3 %collective-permute-start.4 = (f32[64,1024]{1,0:T(8,128)S(1)}, f32[64,1024]{1,0:T(8,128)}, u32[]{:S(2)}, u32[]{:S(2)}) collective-permute-start(f32[64,1024]{1,0:T(8,128)S(1)} %get-tuple-element.21), channel_id=1, source_target_pairs={{0,2},{2,4},{4,6},{6,0},{1,3},{3,5},{5,7},{7,1},{8,10},{10,12},{12... | collective-permute-start | bytes 786440 | tf_op jit(solution)/shard_map/ppermute | solution.py:32
  95.2 13.6 %collective-permute-start.5 = (f32[64,1024]{1,0:T(8,128)S(1)}, f32[64,1024]{1,0:T(8,128)}, u32[]{:S(2)}, u32[]{:S(2)}) collective-permute-start(f32[64,1024]{1,0:T(8,128)S(1)} %get-tuple-element.22), channel_id=1, source_target_pairs={{0,4},{2,6},{4,0},{6,2},{1,5},{3,7},{5,1},{7,3},{8,12},{10,14},{12... | collective-permute-start | bytes 786440 | tf_op jit(solution)/shard_map/ppermute | solution.py:32
  97.2 12.3 %collective-permute-start.6 = (f32[64,1024]{1,0:T(8,128)S(1)}, f32[64,1024]{1,0:T(8,128)}, u32[]{:S(2)}, u32[]{:S(2)}) collective-permute-start(f32[64,1024]{1,0:T(8,128)S(1)} %get-tuple-element.23), channel_id=1, source_target_pairs={{0,6},{2,0},{4,2},{6,4},{1,7},{3,1},{5,3},{7,5},{8,14},{10,8},{12,... | collective-permute-start | bytes 786440 | tf_op jit(solution)/shard_map/ppermute | solution.py:32
  101.1 1.4 %collective-permute-start.10 = (f32[256,128]{1,0:T(8,128)S(1)}, f32[256,128]{1,0:T(8,128)S(1)}, u32[]{:S(2)}, u32[]{:S(2)}) collective-permute-start(f32[256,128]{1,0:T(8,128)S(1)} %get-tuple-element.25), channel_id=1, source_target_pairs={{0,1},{1,0},{2,3},{3,2},{4,5},{5,4},{6,7},{7,6},{8,9},{9,8},{10,11... | collective-permute-start | bytes 393224 | tf_op jit(solution)/shard_map/ppermute | solution.py:32
  102.5 14.5 %collective-permute-start.11 = (f32[256,128]{1,0:T(8,128)S(1)}, f32[256,128]{1,0:T(8,128)S(1)}, u32[]{:S(2)}, u32[]{:S(2)}) collective-permute-start(f32[256,128]{1,0:T(8,128)S(1)} %add.116), channel_id=1, source_target_pairs={{0,128},{128,0},{1,129},{129,1},{2,130},{130,2},{3,131},{131,3},{4... | collective-permute-start | bytes 393224 | tf_op jit(solution)/shard_map/ppermute | solution.py:32
  110.7 9.5 %collective-permute-start.7 = (f32[16,1024]{1,0:T(8,128)S(1)}, f32[16,1024]{1,0:T(8,128)S(1)}, u32[]{:S(2)}, u32[]{:S(2)}) collective-permute-start(f32[16,1024]{1,0:T(8,128)S(1)} %get-tuple-element.26), channel_id=1, source_target_pairs={{0,8},{8,16},{16,24},{24,0},{1,9},{9,17},{17,25},{25,1},{2,10},{10... | collective-permute-start | bytes 196616 | tf_op jit(solution)/shard_map/ppermute | solution.py:32
  111.7 9.9 %collective-permute-start.8 = (f32[16,1024]{1,0:T(8,128)S(1)}, f32[16,1024]{1,0:T(8,128)S(1)}, u32[]{:S(2)}, u32[]{:S(2)}) collective-permute-start(f32[16,1024]{1,0:T(8,128)S(1)} %get-tuple-element.28), channel_id=1, source_target_pairs={{0,16},{8,24},{16,0},{24,8},{1,17},{9,25},{17,1},{25,9},{2,18},{10... | collective-permute-start | bytes 196616 | tf_op jit(solution)/shard_map/ppermute | solution.py:32
  115.2 6.6 %collective-permute-start.9 = (f32[16,1024]{1,0:T(8,128)S(1)}, f32[16,1024]{1,0:T(8,128)S(1)}, u32[]{:S(2)}, u32[]{:S(2)}) collective-permute-start(f32[16,1024]{1,0:T(8,128)S(1)} %get-tuple-element.27), channel_id=1, source_target_pairs={{0,24},{8,0},{16,8},{24,16},{1,25},{9,1},{17,9},{25,17},{2,26},{10... | collective-permute-start | bytes 196616 | tf_op jit(solution)/shard_map/ppermute | solution.py:32
  117.1 5.4 %collective-permute-start.12 = (f32[256,128]{1,0:T(8,128)S(1)}, f32[256,128]{1,0:T(8,128)S(1)}, u32[]{:S(2)}, u32[]{:S(2)}) collective-permute-start(f32[256,128]{1,0:T(8,128)S(1)} %add.117), channel_id=1, source_target_pairs={{0,32},{32,64},{64,96},{96,0},{1,33},{33,65},{65,97},{97,1},{2,34}... | collective-permute-start | bytes 393224 | tf_op jit(solution)/shard_map/ppermute | solution.py:32
  118.3 6.6 %collective-permute-start.13 = (f32[256,128]{1,0:T(8,128)S(1)}, f32[256,128]{1,0:T(8,128)S(1)}, u32[]{:S(2)}, u32[]{:S(2)}) collective-permute-start(f32[256,128]{1,0:T(8,128)S(1)} %add.117), channel_id=1, source_target_pairs={{0,64},{32,96},{64,0},{96,32},{1,65},{33,97},{65,1},{97,33},{2,66}... | collective-permute-start | bytes 393224 | tf_op jit(solution)/shard_map/ppermute | solution.py:32
  120.2 5.9 %collective-permute-start.14 = (f32[256,128]{1,0:T(8,128)S(1)}, f32[256,128]{1,0:T(8,128)S(1)}, u32[]{:S(2)}, u32[]{:S(2)}) collective-permute-start(f32[256,128]{1,0:T(8,128)S(1)} %add.117), channel_id=1, source_target_pairs={{0,96},{32,0},{64,32},{96,64},{1,97},{33,1},{65,33},{97,65},{2,98}... | collective-permute-start | bytes 393224 | tf_op jit(solution)/shard_map/ppermute | solution.py:32

commit v3 on v2

v3 whole, which is shorter than its diff:
```python
import math

import jax
import jax.numpy as jnp
from jax import lax
from jax.experimental import pallas as pl
from jax.experimental.pallas import tpu as pltpu
from jax.sharding import Mesh
from jax.sharding import PartitionSpec as P

HEADS = 128
HEAD_DIM = 192
IDIM = 128
STRIDE = 8
LANES = 128
NEG_FILL = -1e30
SCORE_SCALE = 1.0 / math.sqrt(HEAD_DIM)
INV_SCALE = 1.0 / math.sqrt(IDIM)

AXES = ("z_lo", "y", "z_hi", "x", "core")
HEAD = ("z_lo", "y")
CTX = ("z_hi", "x", "core")
CHIP = ("z_hi", "x")
F32, BF16 = jnp.float32, jnp.bfloat16
VMEM_SPEC = pl.BlockSpec(memory_space=pltpu.VMEM)
SMEM_SPEC = pl.BlockSpec(memory_space=pltpu.SMEM)
ANY_SPEC = pl.BlockSpec(memory_space=pl.ANY)
WIDE_PARAMS = pltpu.CompilerParams(vmem_limit_bytes=60 * 2**20)
PARAMS = pltpu.CompilerParams(vmem_limit_bytes=16 * 2**20)


def shift(value, axis, size, step):
    return lax.ppermute(value, axis, [(i, (i + step) % size) for i in range(size)])


def merge(parts):
    top = jnp.max(parts, axis=0)
    return top + jnp.log(jnp.sum(jnp.exp(parts - top[None]), axis=0))


def dot_t(a, b):
    return lax.dot_general(a, b, (((1,), (1,)), ((), ())), preferred_element_type=F32)


def head_scores(q_ref, k_ref, head):
    lane = lax.broadcasted_iota(jnp.int32, (1, LANES), 1)
    low = (lane < HEAD_DIM - LANES).astype(F32)
    at = head // 2 * 2 * HEAD_DIM + head % 2 * LANES
    q = q_ref[:, at : at + 2 * LANES]
    left, right = k_ref[:, at : at + LANES], k_ref[:, at + LANES : at + 2 * LANES]
    if head % 2 == 0:
        right = right * low.astype(BF16)
    else:
        left = left * (1.0 - low).astype(BF16)
    return dot_t(jnp.concatenate([left, right], axis=1), q) * SCORE_SCALE


def column(row, size):
    n = row.shape[1]
    wide = jnp.broadcast_to(row, (LANES, n))
    return jnp.concatenate([wide[:, i : i + LANES].T for i in range(0, n, LANES)], axis=0)


def key_positions(sc_ref, off_ref):
    keys = off_ref.shape[1]
    lane = lax.broadcasted_iota(jnp.int32, (1, keys), 1)
    return (STRIDE * (sc_ref[3] * keys + lane) + off_ref[...]).astype(F32)


def fill_bias(bias, sc_ref, off_ref, qp_ref):
    pos = column(key_positions(sc_ref, off_ref), LANES)
    for at in range(0, bias.shape[1], LANES):
        row = qp_ref[:, at : at + LANES].astype(F32)
        bias[:, at : at + LANES] = jnp.where(pos <= row, 0.0, NEG_FILL)


def split_rows(tr, out_ref, value):
    turned = value.T
    n, blk, keys = out_ref.shape
    for half in range(keys // LANES):
        span = slice(half * LANES, (half + 1) * LANES)
        tr[half * n * blk : (half + 1) * n * blk, :] = turned[:, span]
        for h in range(n):
            out_ref[h, :, span] = tr[pl.ds(half * n * blk + h, blk, stride=n), :]


def front_kernel(iq_hbm, ik_hbm, wt_hbm, out_ref, wide_ref, iq_ref, ik_ref, wt_ref, tr, sems):
    pairs = ((iq_hbm, iq_ref), (ik_hbm, ik_ref), (wt_hbm, wt_ref))
    copies = [pltpu.make_async_copy(a, b, sems.at[i]) for i, (a, b) in enumerate(pairs)]
    for copy in copies:
        copy.start()
    for copy in copies:
        copy.wait()
    total = None
    for j in range(wt_ref.shape[0]):
        act = dot_t(ik_ref[...], iq_ref[:, j * IDIM : (j + 1) * IDIM])
        term = jnp.maximum(act, 0.0) * wt_ref[j : j + 1, :]
        total = term if total is None else total + term
    split_rows(tr, out_ref, total)
    wide_ref[...] = ik_ref[...].astype(F32)


def front(iq, ik, wt, n_head):
    rows, keys = iq.shape[0], ik.shape[0]
    return pl.pallas_call(
        front_kernel,
        in_specs=[ANY_SPEC] * 3,
        out_specs=[VMEM_SPEC] * 2,
        out_shape=[
            jax.ShapeDtypeStruct((n_head, rows // n_head, keys), F32),
            jax.ShapeDtypeStruct(ik.shape, F32),
        ],
        scratch_shapes=[
            pltpu.VMEM(iq.shape, BF16),
            pltpu.VMEM(ik.shape, BF16),
            pltpu.VMEM(wt.shape, F32),
            pltpu.VMEM((rows * keys // LANES, LANES), F32),
            pltpu.SemaphoreType.DMA((3,)),
        ],
        compiler_params=WIDE_PARAMS,
        name="front",
    )(iq, ik, wt)


def lse_kernel(sc_ref, q_ref, k_ref, off_ref, qp_ref, out_ref, mask_ref, bias, tmp):
    fill_bias(bias, sc_ref, off_ref, qp_ref)
    rows, (blk, keys) = out_ref.shape[1], mask_ref.shape
    tmp[...] = column(qp_ref[...].astype(F32), LANES)
    pos_q = tmp[pl.ds(sc_ref[4], blk, stride=rows // blk), :]
    pos_k = key_positions(sc_ref, off_ref)
    for i in range(0, keys, LANES):
        mask_ref[:, i : i + LANES] = jnp.where(pos_k[:, i : i + LANES] <= pos_q, 0.0, NEG_FILL)
    for head in range(out_ref.shape[0]):
        s = head_scores(q_ref, k_ref, head) + bias[...]
        top = jnp.max(s, axis=0, keepdims=True)
        out_ref[head : head + 1, :] = top + jnp.log(jnp.sum(jnp.exp(s - top), axis=0, keepdims=True))


def scores_lse(sc, queries, attn_keys, off, qp, n_head):
    rows, keys = qp.shape[1], off.shape[1]
    heads = queries.shape[1] // HEAD_DIM
    return pl.pallas_call(
        lse_kernel,
        in_specs=[SMEM_SPEC] + [VMEM_SPEC] * 4,
        out_specs=[VMEM_SPEC] * 2,
        out_shape=[
            jax.ShapeDtypeStruct((heads, rows), F32),
            jax.ShapeDtypeStruct((rows // n_head, keys), F32),
        ],
        scratch_shapes=[pltpu.VMEM((keys, rows), F32), pltpu.VMEM((rows, LANES), F32)],
        compiler_params=PARAMS,
        name="scores_lse",
    )(sc, queries, attn_keys, off, qp)


def join_kernel(sc_ref, lse_ref, parts_ref, mask_ref, keep_ref, give_ref, logits_ref):
    half, rows = lse_ref.shape[0] // 2, lse_ref.shape[1]
    logits = jnp.sum(parts_ref[...], axis=0) * INV_SCALE + mask_ref[...]
    blk = logits.shape[0]
    logits_ref[...] = logits
    top = jnp.max(logits, axis=1, keepdims=True)
    value = top + jnp.log(jnp.sum(jnp.exp(logits - top), axis=1, keepdims=True))
    value = jnp.broadcast_to(value, (blk, LANES))
    value = jnp.concatenate([value, jnp.zeros((LANES - blk, LANES), F32)], axis=0).T
    for out_ref, core in ((keep_ref, sc_ref[0]), (give_ref, 1 - sc_ref[0])):
        out_ref[:, :rows] = lse_ref[pl.ds(pl.multiple_of(core * half, half), half), :]
        out_ref[:, rows:] = value[:half]


def join_lse(sc, lse, parts, mask):
    heads, rows = lse.shape
    out = jax.ShapeDtypeStruct((heads // 2, rows + LANES), F32)
    return pl.pallas_call(
        join_kernel,
        in_specs=[SMEM_SPEC] + [VMEM_SPEC] * 3,
        out_specs=[VMEM_SPEC] * 3,
        out_shape=[out, out, jax.ShapeDtypeStruct(mask.shape, F32)],
        compiler_params=PARAMS,
        name="join_lse",
    )(sc, lse, parts, mask)


def pair_kernel(mine_ref, got_ref, out_ref):
    both = merge(jnp.stack([mine_ref[...], got_ref[...]]))
    for c in range(out_ref.shape[0]):
        out_ref[c] = both


def pair_merge(mine, got, n_chip):
    return pl.pallas_call(
        pair_kernel,
        in_specs=[VMEM_SPEC] * 2,
        out_specs=VMEM_SPEC,
        out_shape=jax.ShapeDtypeStruct((n_chip, *mine.shape), F32),
        compiler_params=PARAMS,
        name="pair_merge",
    )(mine, got)


def merge_kernel(parts_ref, out_ref):
    out_ref[...] = merge(parts_ref[...])


def merge_parts(parts):
    return pl.pallas_call(
        merge_kernel,
        in_specs=[VMEM_SPEC],
        out_specs=VMEM_SPEC,
        out_shape=jax.ShapeDtypeStruct(parts.shape[1:], F32),
        compiler_params=PARAMS,
        name="merge_parts",
    )(parts)


def probs_kernel(
    sc_ref, q_ref, k_ref, off_ref, qp_ref, mine_ref, other_ref, b1, b2, b3, out_ref, stack_ref, bias, lse, tr
):
    fill_bias(bias, sc_ref, off_ref, qp_ref)
    half, rows = mine_ref.shape[0], lse.shape[1]
    for ref, core in ((mine_ref, sc_ref[0]), (other_ref, 1 - sc_ref[0])):
        lse[pl.ds(pl.multiple_of(core * half, half), half), :] = ref[:, :rows]
    for i, ref in enumerate((b1, b2, b3)):
        stack_ref[i] = ref[...]
    total = None
    for head in range(0, lse.shape[0], 2):
        pair = [
            jnp.exp(head_scores(q_ref, k_ref, h) + bias[...] - lse[h : h + 1, :]) for h in (head, head + 1)
        ]
        total = pair[0] + pair[1] if total is None else total + (pair[0] + pair[1])
    split_rows(tr, out_ref, total)


def probs_sum(sc, queries, attn_keys, off, qp, mine, other, blocks, n_head):
    rows, keys = qp.shape[1], off.shape[1]
    heads = queries.shape[1] // HEAD_DIM
    return pl.pallas_call(
        probs_kernel,
        in_specs=[SMEM_SPEC] + [VMEM_SPEC] * 9,
        out_specs=[VMEM_SPEC] * 2,
        out_shape=[
            jax.ShapeDtypeStruct((n_head, rows // n_head, keys), F32),
            jax.ShapeDtypeStruct((len(blocks), *blocks[0].shape), F32),
        ],
        scratch_shapes=[
            pltpu.VMEM((keys, rows), F32),
            pltpu.VMEM((heads, rows), F32),
            pltpu.VMEM((rows * keys // LANES, LANES), F32),
        ],
        compiler_params=PARAMS,
        name="probs_sum",
    )(sc, queries, attn_keys, off, qp, mine, other, *blocks)


def step_kernel(sc_ref, target_ref, logits_ref, lse_ref, keep_ref, give_ref, tmp):
    target = jnp.sum(target_ref[...], axis=0) * (1.0 / HEADS)
    blk, keys = target.shape
    rows = lse_ref.shape[1] - LANES
    lse = lse_ref[:8, rows:].T[:blk, :1]
    step = jnp.exp(logits_ref[...] - lse) - target
    for half in range(keys // LANES):
        span = slice(half * LANES, (half + 1) * LANES)
        tmp[half * blk : (half + 1) * blk, :] = step[:, span]
        for out_ref, core in ((keep_ref, sc_ref[0]), (give_ref, 1 - sc_ref[0])):
            for x in range(4):
                for r in range(2):
                    out_ref[half, pl.ds(8 * x + r, 4, stride=2), :] = tmp[
                        pl.ds(half * blk + 4 * x + 2 * core + r, 4, stride=16), :
                    ]


def prob_step(sc, target_parts, logits, lse):
    _, blk, keys = target_parts.shape
    out = jax.ShapeDtypeStruct((keys // LANES, blk // 2, LANES), F32)
    return pl.pallas_call(
        step_kernel,
        in_specs=[SMEM_SPEC] + [VMEM_SPEC] * 3,
        out_specs=[VMEM_SPEC] * 2,
        out_shape=[out, out],
        scratch_shapes=[pltpu.VMEM((blk * keys // LANES, LANES), F32)],
        compiler_params=PARAMS,
        name="prob_step",
    )(sc, target_parts, logits, lse)


def wide_kernel(sc_ref, mine_ref, got_ref, out_ref, x1_ref, x2_ref, x3_ref, x0_ref):
    n = mine_ref.shape[0]
    for h in range(out_ref.shape[0]):
        out_ref[h, :n] = mine_ref[...]
        out_ref[h, n:] = got_ref[...]
    each = x0_ref.shape[1]
    for k, x_ref in ((1, x1_ref), (2, x2_ref), (3, x3_ref), (0, x0_ref)):
        rows = pl.ds(pl.multiple_of(lax.rem(sc_ref[1] + k, 4) * each, each), each)
        x_ref[:n] = mine_ref[:, rows, :]
        x_ref[n:] = got_ref[:, rows, :]


def widen(sc, mine, got, n_head):
    n, half, _ = mine.shape
    piece = jax.ShapeDtypeStruct((2 * n, half // 4, LANES), F32)
    return pl.pallas_call(
        wide_kernel,
        in_specs=[SMEM_SPEC] + [VMEM_SPEC] * 2,
        out_specs=[VMEM_SPEC] * 5,
        out_shape=[jax.ShapeDtypeStruct((n_head, 2 * n, half, LANES), F32)] + [piece] * 4,
        compiler_params=PARAMS,
        name="widen",
    )(sc, mine, got)


def around_kernel(p0, p1, p2, p3, out_ref):
    for h in range(out_ref.shape[0]):
        for k, ref in enumerate((p0, p1, p2, p3)):
            out_ref[h, k] = ref[...]


def repeat_parts(parts, n_head):
    return pl.pallas_call(
        around_kernel,
        in_specs=[VMEM_SPEC] * 4,
        out_specs=VMEM_SPEC,
        out_shape=jax.ShapeDtypeStruct((n_head, len(parts), *parts[0].shape), F32),
        compiler_params=PARAMS,
        name="repeat_parts",
    )(*parts)


def weight_rows(wt_ref):
    wt = wt_ref[...] * INV_SCALE
    return jnp.concatenate([wt, jnp.zeros((LANES - wt.shape[0], wt.shape[1]), F32)], axis=0).T


def row_blocks(sc_ref, x):
    return [pl.multiple_of(128 * z + 32 * x + 16 * sc_ref[0], 16) for z in range(4)]


def query_kernel(sc_ref, step_ref, iq_ref, wt_ref, ik_ref, ik2_ref, own_ref, far_ref, o1_ref, o2_ref, o3_ref, o0_ref, tr, iqs, acc, w_ref):
    w_ref[...] = weight_rows(wt_ref)
    n_head, n_x, quarters, each, _ = step_ref.shape
    size = each * n_head
    jl = iq_ref.shape[1] // IDIM
    blocks = row_blocks(sc_ref, sc_ref[1])
    w = jnp.concatenate([w_ref[pl.ds(b, 16), :] for b in blocks], axis=0)
    for j in range(jl):
        for z, b in enumerate(blocks):
            iqs[j * size + 16 * z : j * size + 16 * z + 16, :] = iq_ref[pl.ds(b, 16), j * IDIM : (j + 1) * IDIM]
    total = None
    for k in range(n_x):
        for c in range(quarters):
            for h in range(n_head):
                at = (k * quarters + c) * size
                tr[pl.ds(at + h, each, stride=n_head), :] = step_ref[h, k, c]
        step = jnp.concatenate(
            [tr[(k * quarters + c) * size : (k * quarters + c + 1) * size, :] for c in range(quarters)], axis=1
        )
        near, far = (ik_ref[...], ik2_ref[...]) if k == 0 else (own_ref[k - 1], far_ref[k - 1])
        ik = jnp.concatenate([near, far], axis=0).astype(BF16)
        act = dot_t(iqs[...], ik)
        terms = jnp.concatenate(
            [
                jnp.where(act[j * size : (j + 1) * size] > 0.0, step * w[:, j : j + 1], 0.0).astype(BF16)
                for j in range(jl)
            ],
            axis=0,
        )
        part = jnp.dot(terms, ik, preferred_element_type=F32)
        total = part if total is None else total + part
    acc[...] = total
    piece = size // 4
    for k, out_ref in ((1, o1_ref), (2, o2_ref), (3, o3_ref), (0, o0_ref)):
        z = lax.rem(sc_ref[2] + k, 4)
        for j in range(jl):
            out_ref[:, j * IDIM : (j + 1) * IDIM] = acc[pl.ds(pl.multiple_of(j * size + z * piece, piece), piece), :]


def query_pieces(sc, step, iq, wt, ik, ik2, own, far):
    n_head, n_x, quarters, each, _ = step.shape
    size = each * n_head
    out = jax.ShapeDtypeStruct((size // 4, iq.shape[1]), F32)
    return pl.pallas_call(
        query_kernel,
        in_specs=[SMEM_SPEC] + [VMEM_SPEC] * 7,
        out_specs=[VMEM_SPEC] * 4,
        out_shape=[out] * 4,
        scratch_shapes=[
            pltpu.VMEM((n_x * quarters * size, LANES), F32),
            pltpu.VMEM((size * iq.shape[1] // IDIM, IDIM), BF16),
            pltpu.VMEM((size * iq.shape[1] // IDIM, IDIM), F32),
            pltpu.VMEM((iq.shape[0], LANES), F32),
        ],
        compiler_params=PARAMS,
        name="query_pieces",
    )(sc, step, iq, wt, ik, ik2, own, far)


def key_kernel(sc_ref, step_ref, iq_ref, ik_ref, ik2_ref, wt_ref, keep_ref, give_ref, tr, iqs, ws, w_ref):
    w_ref[...] = weight_rows(wt_ref)
    n, quarters, half, _ = step_ref.shape
    size = n * half
    turned = []
    for c in range(quarters):
        for h in range(n):
            tr[pl.ds(h, half, stride=n), :] = step_ref[h, c]
        turned.append(tr[...].T)
    step = jnp.concatenate(turned, axis=0)
    for x in range(4):
        for z, b in enumerate(row_blocks(sc_ref, x)):
            at = 64 * x + 16 * z
            iqs[at : at + 16, :] = iq_ref[pl.ds(b, 16), :]
            ws[at : at + 16, :] = w_ref[pl.ds(b, 16), :]
    wt = ws[...].T
    ik = jnp.concatenate([ik_ref[...], ik2_ref[...]], axis=0).astype(BF16)
    total = None
    for j in range(iq_ref.shape[1] // IDIM):
        iq = iqs[:, j * IDIM : (j + 1) * IDIM]
        act = dot_t(ik, iq)
        terms = jnp.where(act > 0.0, step * wt[j : j + 1, :], 0.0).astype(BF16)
        part = jnp.dot(terms, iq, preferred_element_type=F32)
        total = part if total is None else total + part
    keys = keep_ref.shape[0]
    keep_ref[...] = total[:keys]
    give_ref[...] = total[keys:]


def key_part_grad(sc, step, iq, ik, ik2, wt):
    n, _, half, _ = step.shape
    size = n * half
    out = jax.ShapeDtypeStruct(ik.shape, F32)
    return pl.pallas_call(
        key_kernel,
        in_specs=[SMEM_SPEC] + [VMEM_SPEC] * 5,
        out_specs=[VMEM_SPEC] * 2,
        out_shape=[out, out],
        scratch_shapes=[
            pltpu.VMEM((size, LANES), F32),
            pltpu.VMEM((size, iq.shape[1]), BF16),
            pltpu.VMEM((size, LANES), F32),
            pltpu.VMEM((iq.shape[0], LANES), F32),
        ],
        compiler_params=PARAMS,
        name="key_part_grad",
    )(sc, step, iq, ik, ik2, wt)


def shards(queries, attn_keys, index_queries, index_keys, head_weights, query_pos, key_offset):
    n_head, n_chip = lax.axis_size(HEAD), lax.axis_size(CHIP)
    sc = jnp.stack([lax.axis_index(a) for a in ("core", "x", "z_hi", CTX, HEAD)]).astype(jnp.int32)

    off, qp = key_offset[None, :], query_pos[None, :]
    w_t = head_weights.T

    index, ik = front(index_queries, index_keys, w_t, n_head)
    index = lax.all_to_all(index, HEAD, 0, 0)
    ik2 = shift(ik, "core", 2, 1)

    lse, mask = scores_lse(sc, queries, attn_keys, off, qp, n_head)
    mine, give, logits = join_lse(sc, lse, index, mask)
    mine = pair_merge(mine, shift(give, "core", 2, 1), n_chip)
    mine = merge_parts(lax.all_to_all(mine, CHIP, 0, 0))
    other = shift(mine, "core", 2, 1)
    around = [shift(ik, "x", 4, k) for k in range(1, 4)]
    target, around = probs_sum(sc, queries, attn_keys, off, qp, mine, other, around, n_head)
    target = lax.all_to_all(target, HEAD, 0, 0)

    step, give = prob_step(sc, target, logits, mine)
    step_key, *pieces = widen(sc, step, shift(give, "core", 2, 1), n_head)
    step_key = lax.all_to_all(step_key, HEAD, 0, 0)
    pieces = [pieces[3]] + [shift(pieces[k - 1], "x", 4, k) for k in range(1, 4)]
    step_query = lax.all_to_all(repeat_parts(pieces, n_head), HEAD, 0, 0)

    p1, p2, p3, query_grad = query_pieces(
        sc, step_query, index_queries, w_t, ik, ik2, around, shift(around, "core", 2, 1)
    )
    query_grad = query_grad + shift(p1, "z_hi", 4, 1) + shift(p2, "z_hi", 4, 2) + shift(p3, "z_hi", 4, 3)

    key_part, give = key_part_grad(sc, step_key, index_queries, ik, ik2, w_t)
    key_part = key_part + shift(give, "core", 2, 1)
    key_part = key_part + shift(key_part, "z_lo", 2, 1)
    key_grad = key_part
    for k in range(1, 4):
        key_grad = key_grad + shift(key_part, "y", 4, k)
    return (query_grad, key_grad)


def solution(mesh):
    mesh = Mesh(mesh.devices.reshape(2, 4, 4, 4, 2), AXES)
    in_specs = (
        P(None, HEAD),
        P(CTX, HEAD),
        P(None, HEAD),
        P(CTX, None),
        P(None, HEAD),
        P(),
        P(CTX),
    )
    out_specs = (P(CTX, HEAD), P(CTX, None))
    return jax.shard_map(shards, mesh=mesh, in_specs=in_specs, out_specs=out_specs, check_vma=False)
```

time: 128 us -> 118 us (0.922)
  blocking collectives: 38.2 us -> 14.6 us
  starting transfers between devices: 28.6 us -> 50.9 us
  Pallas kernels: 23.9 us -> 19.7 us
  other arithmetic: 3.29 us -> 1.37 us
  local copies, waits for them, and re-layouts: 9.32 us -> 7.52 us
    all_to_all x1 -> x0, blocking collectives: 23.5 us -> none  [shards(): mine = merge_parts(lax.all_to_all(mine, CHIP, 0, 0))]
    all_to_all x1 -> x3, starting transfers between devices: 5.21 us -> 20.2 us  [the longest x1 10.1 us: shards(): mine = merge_parts(lax.all_to_all(mine, CHIP, 0, 0))]
    ppermute x15 -> x19, starting transfers between devices: 17.1 us -> 24.5 us  [shift(): lax.ppermute(value, axis, [(i, (i + step) % size) for i in range(size)])]
    pallas_call x7 -> x8, Pallas kernels: 21.7 us -> 17.5 us  [the longest x1 3.99 us: probs_sum(): pl.pallas_call(probs_kernel, in_specs=[SMEM_SPEC] + [VMEM_SPEC] * 9, out_...]
    all_to_all x1 -> x3, waiting for transfers between devices: 7.29 us -> 10.2 us  [the longest x1 7.61 us: shards(): mine = merge_parts(lax.all_to_all(mine, CHIP, 0, 0))]
    ppermute x15 -> x19, waiting for transfers between devices: 15.4 us -> 12.6 us  [shift(): lax.ppermute(value, axis, [(i, (i + step) % size) for i in range(size)])]
    add x3 -> x1, other arithmetic: 2.49 us -> 0.65 us  [shards(): query_grad + shift(p1, 'z_hi', 4, 1) + shift(p2, 'z_hi', 4, 2)]
    unnamed x23 -> x28, local copies, waits for them, and re-layouts: 8.3 us -> 7.44 us
  transfers between devices with their start and end apart: 17 -> 23, of which waited for: 11 -> 14; matrix products, arithmetic and copies ran while one was open for 3% -> 1% of each run, Pallas kernels for 6% -> 8%
where the time goes in v3:
time: 118 us
  starting transfers between devices  50.9 us (43%)
  waiting for transfers between devices  22.7 us (19%)
  Pallas kernels  19.7 us (17%)
  blocking collectives  14.6 us (12%)
  local copies, waits for them, and re-layouts  7.52 us (6%)
  other arithmetic  1.37 us (1%)
    ppermute x19, starting transfers between devices, shift(): lax.ppermute(value, axis, [(i, (i + step) % size) for i in range(size)])  24.5 us
    all_to_all x1, blocking collectives, shards(): target = lax.all_to_all(target, HEAD, 0, 0)  14.6 us
    ppermute x19, waiting for transfers between devices, shift(): lax.ppermute(value, axis, [(i, (i + step) % size) for i in range(size)])  12.6 us
    all_to_all x1, starting transfers between devices, shards(): mine = merge_parts(lax.all_to_all(mine, CHIP, 0, 0))  10.1 us
    all_to_all x1, waiting for transfers between devices, shards(): mine = merge_parts(lax.all_to_all(mine, CHIP, 0, 0))  7.61 us
    unnamed x28, local copies, waits for them, and re-layouts  7.44 us
    all_to_all x1, starting transfers between devices, shards(): index = lax.all_to_all(index, HEAD, 0, 0)  6.28 us
    all_to_all x1, starting transfers between devices, shards(): step_key = lax.all_to_all(step_key, HEAD, 0, 0)  5.21 us
  transfers between devices with their start and end apart: 23, of which 14 were waited for; matrix products, arithmetic and copies ran while one was open for 1% of the time, Pallas kernels for 8%

profile of v3, /device:TPU:8, one launch (start us, length us, event | category | flops | bytes accessed | tf_op | source)
XLA Modules:
  0.0 117.7 jit_solution(17543316267907346910)
XLA Ops:
  0.6 3.0 %front.1 = (f32[8,64,256]{2,1,0:T(8,128)}, f32[256,128]{1,0:T(8,128)}) custom-call(bf16[512,1024]{1,0:T(8,128)(2,1)} %iq_ref.3, bf16[256,128]{1,0:T(8,128)(2,1)} %ik_hbm.1, f32[8,512]{1,0:T(8,128)} %bitcast.8), custom_call_target="tpu_custom_call" | custom-call | tf_op jit(solution)/shard_map/front/pallas_call | solution.py:105
  3.7 6.3 %all-to-all-start = ((f32[8,64,256]{2,1,0:T(8,128)}), f32[8,64,256]{2,1,0:T(8,128)}, u32[]{:S(2)}, u32[]{:S(2)}) async-start(f32[8,64,256]{2,1,0:T(8,128)} %get-tuple-element.25), calls=%async_computation | async-start | bytes 1048576 | tf_op jit(solution)/shard_map/all_to_all | solution.py:452
  10.0 0.1 stack.23.sc_ref
  10.0 1.9 %copy-done = bf16[512,3072]{1,0:T(8,128)(2,1)S(1)} copy-done((bf16[512,3072]{1,0:T(8,128)(2,1)S(1)}, bf16[512,3072]{1,0:T(8,128)(2,1)}, u32[]{:S(2)}) %copy-start) | copy-done | bytes 3145752
  11.9 1.4 %copy-done.3 = bf16[256,3072]{1,0:T(8,128)(2,1)S(1)} copy-done((bf16[256,3072]{1,0:T(8,128)(2,1)S(1)}, bf16[256,3072]{1,0:T(8,128)(2,1)}, u32[]{:S(2)}) %copy-start.3) | copy-done | bytes 1572888
  13.3 0.7 copy-done.10
  14.0 0.7 copy-done.12
  14.7 3.9 %scores_lse.1 = (f32[16,512]{1,0:T(8,128)S(1)}, f32[64,256]{1,0:T(8,128)S(1)}) custom-call(s32[5]{0:T(128)S(1)} %stack.23.sc_ref, bf16[512,3072]{1,0:T(8,128)(2,1)S(1)} %copy-done, bf16[256,3072]{1,0:T(8,128)(2,1)S(1)} %copy-done.3, s32[1,256]{1,0:T(1,128)S(1)} %bitcast.13, s32[1,512]{1,0:T(1,128)S(1)} %bitcast.11), custom_call_target="tpu_custom_call" | custom-call | tf_op jit(solution)/shard_map/scores_lse/pallas_call | solution.py:142
  18.6 0.0 all-to-all-done.parts_ref
  18.6 1.3 %join_lse.1 = (f32[8,640]{1,0:T(8,128)S(1)}, f32[8,640]{1,0:T(8,128)S(1)}, f32[64,256]{1,0:T(8,128)S(1)}) custom-call(s32[5]{0:T(128)S(1)} %stack.23.sc_ref, f32[16,512]{1,0:T(8,128)S(1)} %get-tuple-element.24.lse_ref, f32[8,64,256]{2,1,0:T(8,128)} %all-to-all-done.parts_ref, f32[64,256]{1,0:T(8,128)S(1)} %get-tuple-element.26.mask_ref), custom_call_target="tpu_custom_call" | custom-call | tf_op jit(solution)/shard_map/join_lse/pallas_call | solution.py:173
  19.9 0.6 copy-done.8
  20.5 1.2 %collective-permute-done.got_ref = f32[8,640]{1,0:T(8,128)S(1)} collective-permute-done((f32[8,640]{1,0:T(8,128)S(1)}, f32[8,640]{1,0:T(8,128)S(1)}, u32[]{:S(2)}, u32[]{:S(2)}) %collective-permute-start) | collective-permute-done | bytes 20512 | tf_op jit(solution)/shard_map/ppermute | solution.py:33
  21.8 0.7 copy-done.5
  22.5 10.1 %all-to-all-start.1 = ((f32[16,8,640]{2,1,0:T(8,128)}), f32[16,8,640]{2,1,0:T(8,128)S(1)}, u32[]{:S(2)}, u32[]{:S(2)}) async-start(f32[16,8,640]{2,1,0:T(8,128)} %copy-done.5), calls=%async_computation.1 | async-start | bytes 655360 | tf_op jit(solution)/shard_map/all_to_all | solution.py:458
  32.6 1.9 %collective-permute-start.2 = (f32[256,128]{1,0:T(8,128)}, f32[256,128]{1,0:T(8,128)}, u32[]{:S(2)}, u32[]{:S(2)}) collective-permute-start(f32[256,128]{1,0:T(8,128)} %get-tuple-element.29.ik_ref), channel_id=1, source_target_pairs={{0,2},{2,4},{4,6},{6,0},{1,3},{3,5},{5,7},{7,1},{8,10},{10,12},{12... | collective-permute-start | bytes 393224 | tf_op jit(solution)/shard_map/ppermute | solution.py:33
  34.6 2.7 %collective-permute-start.3 = (f32[256,128]{1,0:T(8,128)}, f32[256,128]{1,0:T(8,128)}, u32[]{:S(2)}, u32[]{:S(2)}) collective-permute-start(f32[256,128]{1,0:T(8,128)} %get-tuple-element.29.ik_ref), channel_id=1, source_target_pairs={{0,4},{2,6},{4,0},{6,2},{1,5},{3,7},{5,1},{7,3},{8,12},{10,14},{12... | collective-permute-start | bytes 393224 | tf_op jit(solution)/shard_map/ppermute | solution.py:33
  37.2 1.5 %collective-permute-start.4 = (f32[256,128]{1,0:T(8,128)}, f32[256,128]{1,0:T(8,128)}, u32[]{:S(2)}, u32[]{:S(2)}) collective-permute-start(f32[256,128]{1,0:T(8,128)} %get-tuple-element.29.ik_ref), channel_id=1, source_target_pairs={{0,6},{2,0},{4,2},{6,4},{1,7},{3,1},{5,3},{7,5},{8,14},{10,8},{12,... | collective-permute-start | bytes 393224 | tf_op jit(solution)/shard_map/ppermute | solution.py:33
  38.7 7.6 %all-to-all-done.1.parts_ref = f32[16,8,640]{2,1,0:T(8,128)S(1)} async-done(((f32[16,8,640]{2,1,0:T(8,128)}), f32[16,8,640]{2,1,0:T(8,128)S(1)}, u32[]{:S(2)}, u32[]{:S(2)}) %all-to-all-start.1) | async-done | bytes 327712 | tf_op jit(solution)/shard_map/all_to_all | solution.py:458
  46.3 0.1 merge_parts.1.mine_ref.lse_ref
  46.4 0.1 collective-permute-start.1
  46.5 0.0 collective-permute-done.2.b1
  46.5 0.0 collective-permute-done.3.b2
  46.5 1.1 collective-permute-done.1.other_ref
  47.7 0.0 copy-start.4
  47.7 1.4 %copy-done.4 = bf16[256,3072]{1,0:T(8,128)(2,1)S(1)} copy-done((bf16[256,3072]{1,0:T(8,128)(2,1)S(1)}, bf16[256,3072]{1,0:T(8,128)(2,1)}, u32[]{:S(2)}) %copy-start.4) | copy-done | bytes 1572888
  49.1 4.0 %probs_sum.1 = (f32[8,64,256]{2,1,0:T(8,128)S(1)}, f32[3,256,128]{2,1,0:T(8,128)S(1)}) custom-call(s32[5]{0:T(128)S(1)} %stack.23.sc_ref, bf16[512,3072]{1,0:T(8,128)(2,1)S(1)} %copy-done.1, bf16[256,3072]{1,0:T(8,128)(2,1)S(1)} %copy-done.4, s32[1,256]{1,0:T(1,128)S(1)} %bitcast.14, s32[1,512]{1,0:T(1,128)S(1)} %bitcast.12, ...), custom_call_target="tpu_custom_call" | custom-call | tf_op jit(solution)/shard_map/probs_sum/pallas_call | solution.py:236
  53.1 0.0 copy-start.6
  53.1 0.0 copy-start.2
  53.1 0.0 copy-start.7
  53.1 14.6 %all_to_all.25.target_ref = f32[8,64,256]{2,1,0:T(8,128)S(1)} all-to-all(f32[8,64,256]{2,1,0:T(8,128)S(1)} %get-tuple-element.30), channel_id=1, replica_groups=mesh['z_lo'=2,'y'=4,'z_hi'=4,'x'=4,'core'=2] {'z_lo','y'}, dimensions={0} | all-to-all | bytes 1048576 | tf_op jit(solution)/shard_map/all_to_all | solution.py:462
  67.7 0.7 prob_step.1
  68.4 0.1 collective-permute-start.5
  68.5 1.2 %collective-permute-done.5.got_ref = f32[2,32,128]{2,1,0:T(8,128)S(1)} collective-permute-done((f32[2,32,128]{2,1,0:T(8,128)S(1)}, f32[2,32,128]{2,1,0:T(8,128)S(1)}, u32[]{:S(2)}, u32[]{:S(2)}) %collective-permute-start.5) | collective-permute-done | bytes 32800 | tf_op jit(solution)/shard_map/ppermute | solution.py:33
  69.7 1.4 %widen.1 = (f32[8,4,32,128]{3,2,1,0:T(8,128)}, f32[4,8,128]{2,1,0:T(8,128)S(1)}, f32[4,8,128]{2,1,0:T(8,128)S(1)}, f32[4,8,128]{2,1,0:T(8,128)S(1)}, f32[4,8,128]{2,1,0:T(8,128)S(1)}) custom-call(s32[5]{0:T(128)S(1)} %stack.23.sc_ref, f32[2,32,128]{2,1,0:T(8,128)S(1)} %get-tuple-element.32.mine_ref, f32[2,32,128]{2,1,0:T(8,128)S(1)} %collective-permute-done.5.got_ref), custom_call_target="tpu_custom_call" | custom-call | tf_op jit(solution)/shard_map/widen/pallas_call | solution.py:300
  71.1 5.2 %all-to-all-start.4 = ((f32[8,4,32,128]{3,2,1,0:T(8,128)}), f32[8,4,32,128]{3,2,1,0:T(8,128)S(1)}, u32[]{:S(2)}, u32[]{:S(2)}) async-start(f32[8,4,32,128]{3,2,1,0:T(8,128)} %get-tuple-element.43), calls=%async_computation.4 | async-start | bytes 1048576 | tf_op jit(solution)/shard_map/all_to_all | solution.py:466
  76.3 0.6 collective-permute-start.6
  76.9 2.0 %collective-permute-start.7 = (f32[4,8,128]{2,1,0:T(8,128)S(1)}, f32[4,8,128]{2,1,0:T(8,128)S(1)}, u32[]{:S(2)}, u32[]{:S(2)}) collective-permute-start(f32[4,8,128]{2,1,0:T(8,128)S(1)} %get-tuple-element.36), channel_id=1, source_target_pairs={{0,4},{2,6},{4,0},{6,2},{1,5},{3,7},{5,1},{7,3},{8,12},{10,14},{12... | collective-permute-start | bytes 49160 | tf_op jit(solution)/shard_map/ppermute | solution.py:33
  78.9 1.8 %collective-permute-start.8 = (f32[4,8,128]{2,1,0:T(8,128)S(1)}, f32[4,8,128]{2,1,0:T(8,128)S(1)}, u32[]{:S(2)}, u32[]{:S(2)}) collective-permute-start(f32[4,8,128]{2,1,0:T(8,128)S(1)} %get-tuple-element.37), channel_id=1, source_target_pairs={{0,6},{2,0},{4,2},{6,4},{1,7},{3,1},{5,3},{7,5},{8,14},{10,8},{12,... | collective-permute-start | bytes 49160 | tf_op jit(solution)/shard_map/ppermute | solution.py:33
  80.7 0.6 collective-permute-done.6.p1
  81.3 0.9 collective-permute-done.7.p2
  82.1 0.5 collective-permute-done.8.p3
  82.6 0.9 repeat_parts.1
  83.5 1.5 %all-to-all-done.4.step_ref = f32[8,4,32,128]{3,2,1,0:T(8,128)S(1)} async-done(((f32[8,4,32,128]{3,2,1,0:T(8,128)}), f32[8,4,32,128]{3,2,1,0:T(8,128)S(1)}, u32[]{:S(2)}, u32[]{:S(2)}) %all-to-all-start.4) | async-done | bytes 524320 | tf_op jit(solution)/shard_map/all_to_all | solution.py:466
  85.0 4.8 %all-to-all-start.3 = ((f32[8,4,4,8,128]{4,3,2,1,0:T(8,128)}), f32[8,4,4,8,128]{4,3,2,1,0:T(8,128)S(1)}, u32[]{:S(2)}, u32[]{:S(2)}) async-start(f32[8,4,4,8,128]{4,3,2,1,0:T(8,128)} %repeat_parts.1), calls=%async_computation.3 | async-start | bytes 1048576 | tf_op jit(solution)/shard_map/all_to_all | solution.py:468
  89.8 0.5 collective-permute-start.9
  90.3 1.4 %collective-permute-done.9.ik2_ref = f32[256,128]{1,0:T(8,128)S(1)} collective-permute-done((f32[256,128]{1,0:T(8,128)S(1)}, f32[256,128]{1,0:T(8,128)S(1)}, u32[]{:S(2)}, u32[]{:S(2)}) %collective-permute-start.9) | collective-permute-done | bytes 131104 | tf_op jit(solution)/shard_map/ppermute | solution.py:33
  91.7 2.1 %key_part_grad.1 = (f32[256,128]{1,0:T(8,128)S(1)}, f32[256,128]{1,0:T(8,128)S(1)}) custom-call(s32[5]{0:T(128)S(1)} %stack.23.sc_ref, f32[8,4,32,128]{3,2,1,0:T(8,128)S(1)} %all-to-all-done.4.step_ref, bf16[512,1024]{1,0:T(8,128)(2,1)S(1)} %copy-done.2, f32[256,128]{1,0:T(8,128)S(1)} %copy-done.6, f32[256,128]{1,0:T(8,128)S(1)} %collective-permute-done.9.ik2_ref, ...), custom_call_target="tpu_custom_call" | custom-call | tf_op jit(solution)/shard_map/key_part_grad/pallas_call | solution.py:428
  93.8 0.2 collective-permute-start.14
  94.1 1.2 %collective-permute-done.14 = f32[256,128]{1,0:T(8,128)S(1)} collective-permute-done((f32[256,128]{1,0:T(8,128)S(1)}, f32[256,128]{1,0:T(8,128)S(1)}, u32[]{:S(2)}, u32[]{:S(2)}) %collective-permute-start.14) | collective-permute-done | bytes 131104 | tf_op jit(solution)/shard_map/ppermute | solution.py:33
  95.3 1.6 %collective-permute-start.15 = (f32[256,128]{1,0:T(8,128)S(1)}, f32[256,128]{1,0:T(8,128)S(1)}, u32[]{:S(2)}, u32[]{:S(2)}) collective-permute-start(f32[256,128]{1,0:T(8,128)S(1)} %add.39), channel_id=1, source_target_pairs={{0,128},{128,0},{1,129},{129,1},{2,130},{130,2},{3,131},{131,3},{4... | collective-permute-start | bytes 393224 | tf_op jit(solution)/shard_map/ppermute | solution.py:33
  96.9 0.0 collective-permute-done.10.far_ref
  96.9 1.1 all-to-all-done.3.step_ref
  98.0 2.3 %query_pieces.1 = (f32[16,1024]{1,0:T(8,128)S(1)}, f32[16,1024]{1,0:T(8,128)S(1)}, f32[16,1024]{1,0:T(8,128)S(1)}, f32[16,1024]{1,0:T(8,128)S(1)}) custom-call(s32[5]{0:T(128)S(1)} %stack.23.sc_ref, f32[8,4,4,8,128]{4,3,2,1,0:T(8,128)S(1)} %all-to-all-done.3.step_ref, bf16[512,1024]{1,0:T(8,128)(2,1)S(1)} %copy-done.2, f32[8,512]{1,0:T(8,128)S(1)} %bitcast.10, ...), custom_call_target="tpu_custom_call" | custom-call | tf_op jit(solution)/shard_map/query_pieces/pallas_call | solution.py:379
  100.3 1.2 %collective-permute-start.11 = (f32[16,1024]{1,0:T(8,128)S(1)}, f32[16,1024]{1,0:T(8,128)S(1)}, u32[]{:S(2)}, u32[]{:S(2)}) collective-permute-start(f32[16,1024]{1,0:T(8,128)S(1)} %get-tuple-element.40), channel_id=1, source_target_pairs={{0,8},{8,16},{16,24},{24,0},{1,9},{9,17},{17,25},{25,1},{2,10},{10... | collective-permute-start | bytes 196616 | tf_op jit(solution)/shard_map/ppermute | solution.py:33
  101.5 3.4 %collective-permute-start.12 = (f32[16,1024]{1,0:T(8,128)S(1)}, f32[16,1024]{1,0:T(8,128)S(1)}, u32[]{:S(2)}, u32[]{:S(2)}) collective-permute-start(f32[16,1024]{1,0:T(8,128)S(1)} %get-tuple-element.41), channel_id=1, source_target_pairs={{0,16},{8,24},{16,0},{24,8},{1,17},{9,25},{17,1},{25,9},{2,18},{10... | collective-permute-start | bytes 196616 | tf_op jit(solution)/shard_map/ppermute | solution.py:33
  104.9 2.3 %collective-permute-start.13 = (f32[16,1024]{1,0:T(8,128)S(1)}, f32[16,1024]{1,0:T(8,128)S(1)}, u32[]{:S(2)}, u32[]{:S(2)}) collective-permute-start(f32[16,1024]{1,0:T(8,128)S(1)} %get-tuple-element.42), channel_id=1, source_target_pairs={{0,24},{8,0},{16,8},{24,16},{1,25},{9,1},{17,9},{25,17},{2,26},{10... | collective-permute-start | bytes 196616 | tf_op jit(solution)/shard_map/ppermute | solution.py:33
  107.2 1.4 %collective-permute-start.16 = (f32[256,128]{1,0:T(8,128)S(1)}, f32[256,128]{1,0:T(8,128)S(1)}, u32[]{:S(2)}, u32[]{:S(2)}) collective-permute-start(f32[256,128]{1,0:T(8,128)S(1)} %add.40), channel_id=1, source_target_pairs={{0,32},{32,64},{64,96},{96,0},{1,33},{33,65},{65,97},{97,1},{2,34}... | collective-permute-start | bytes 393224 | tf_op jit(solution)/shard_map/ppermute | solution.py:33
  108.6 2.4 %collective-permute-start.17 = (f32[256,128]{1,0:T(8,128)S(1)}, f32[256,128]{1,0:T(8,128)S(1)}, u32[]{:S(2)}, u32[]{:S(2)}) collective-permute-start(f32[256,128]{1,0:T(8,128)S(1)} %add.40), channel_id=1, source_target_pairs={{0,64},{32,96},{64,0},{96,32},{1,65},{33,97},{65,1},{97,33},{2,66}... | collective-permute-start | bytes 393224 | tf_op jit(solution)/shard_map/ppermute | solution.py:33
  111.0 0.9 collective-permute-start.18
  111.9 1.2 %collective-permute-done.13 = f32[16,1024]{1,0:T(8,128)S(1)} collective-permute-done((f32[16,1024]{1,0:T(8,128)S(1)}, f32[16,1024]{1,0:T(8,128)S(1)}, u32[]{:S(2)}, u32[]{:S(2)}) %collective-permute-start.13) | collective-permute-done | bytes 65568 | tf_op jit(solution)/shard_map/ppermute | solution.py:33
  113.1 0.6 add_add_fusion.1
  113.7 2.1 %collective-permute-done.17 = f32[256,128]{1,0:T(8,128)S(1)} collective-permute-done((f32[256,128]{1,0:T(8,128)S(1)}, f32[256,128]{1,0:T(8,128)S(1)}, u32[]{:S(2)}, u32[]{:S(2)}) %collective-permute-start.17) | collective-permute-done | bytes 131104 | tf_op jit(solution)/shard_map/ppermute | solution.py:33
  115.8 1.1 collective-permute-done.18
  117.0 0.7 add_add_fusion
  (27 shorter events, 0.1 us)
Async XLA Ops:
  3.7 14.9 %all-to-all-start = ((f32[8,64,256]{2,1,0:T(8,128)}), f32[8,64,256]{2,1,0:T(8,128)}, u32[]{:S(2)}, u32[]{:S(2)}) async-start(f32[8,64,256]{2,1,0:T(8,128)} %get-tuple-element.25), calls=%async_computation | async-start | bytes 1048576 | tf_op jit(solution)/shard_map/all_to_all | solution.py:452
  10.0 1.9 %copy-start = (bf16[512,3072]{1,0:T(8,128)(2,1)S(1)}, bf16[512,3072]{1,0:T(8,128)(2,1)}, u32[]{:S(2)}) copy-start(bf16[512,3072]{1,0:T(8,128)(2,1)} %q_ref.3) | copy-start | bytes 9437188
  11.9 1.4 %copy-start.3 = (bf16[256,3072]{1,0:T(8,128)(2,1)S(1)}, bf16[256,3072]{1,0:T(8,128)(2,1)}, u32[]{:S(2)}) copy-start(bf16[256,3072]{1,0:T(8,128)(2,1)} %k_ref.3) | copy-start | bytes 4718596
  13.3 0.7 copy-start.10
  14.0 0.7 copy-start.12
  14.7 33.0 %copy-start.1 = (bf16[512,3072]{1,0:T(8,128)(2,1)S(1)}, bf16[512,3072]{1,0:T(8,128)(2,1)}, u32[]{:S(2)}) copy-start(bf16[512,3072]{1,0:T(8,128)(2,1)} %q_ref.3) | copy-start | bytes 9437188
  14.7 33.0 %copy-start.11 = (s32[512]{0:T(512)S(1)}, s32[512]{0:T(512)}, u32[]{:S(2)}) copy-start(s32[512]{0:T(512)} %param.12) | copy-start | bytes 6148
  14.7 33.0 %copy-start.13 = (s32[256]{0:T(256)S(1)}, s32[256]{0:T(256)}, u32[]{:S(2)}) copy-start(s32[256]{0:T(256)} %param.13) | copy-start | bytes 3076
  19.9 0.6 copy-start.8
  20.5 1.2 %collective-permute-start = (f32[8,640]{1,0:T(8,128)S(1)}, f32[8,640]{1,0:T(8,128)S(1)}, u32[]{:S(2)}, u32[]{:S(2)}) collective-permute-start(f32[8,640]{1,0:T(8,128)S(1)} %get-tuple-element.28), channel_id=1, source_target_pairs={{0,1},{1,0},{2,3},{3,2},{4,5},{5,4},{6,7},{7,6},{8,9},{9,8},{10,11... | collective-permute-start | bytes 61448 | tf_op jit(solution)/shard_map/ppermute | solution.py:33
  21.8 0.7 copy-start.5
  22.5 23.8 %all-to-all-start.1 = ((f32[16,8,640]{2,1,0:T(8,128)}), f32[16,8,640]{2,1,0:T(8,128)S(1)}, u32[]{:S(2)}, u32[]{:S(2)}) async-start(f32[16,8,640]{2,1,0:T(8,128)} %copy-done.5), calls=%async_computation.1 | async-start | bytes 655360 | tf_op jit(solution)/shard_map/all_to_all | solution.py:458
  32.6 13.9 %collective-permute-start.2 = (f32[256,128]{1,0:T(8,128)}, f32[256,128]{1,0:T(8,128)}, u32[]{:S(2)}, u32[]{:S(2)}) collective-permute-start(f32[256,128]{1,0:T(8,128)} %get-tuple-element.29.ik_ref), channel_id=1, source_target_pairs={{0,2},{2,4},{4,6},{6,0},{1,3},{3,5},{5,7},{7,1},{8,10},{10,12},{12... | collective-permute-start | bytes 393224 | tf_op jit(solution)/shard_map/ppermute | solution.py:33
  34.6 11.9 %collective-permute-start.3 = (f32[256,128]{1,0:T(8,128)}, f32[256,128]{1,0:T(8,128)}, u32[]{:S(2)}, u32[]{:S(2)}) collective-permute-start(f32[256,128]{1,0:T(8,128)} %get-tuple-element.29.ik_ref), channel_id=1, source_target_pairs={{0,4},{2,6},{4,0},{6,2},{1,5},{3,7},{5,1},{7,3},{8,12},{10,14},{12... | collective-permute-start | bytes 393224 | tf_op jit(solution)/shard_map/ppermute | solution.py:33
  37.2 9.3 %collective-permute-start.4 = (f32[256,128]{1,0:T(8,128)}, f32[256,128]{1,0:T(8,128)}, u32[]{:S(2)}, u32[]{:S(2)}) collective-permute-start(f32[256,128]{1,0:T(8,128)} %get-tuple-element.29.ik_ref), channel_id=1, source_target_pairs={{0,6},{2,0},{4,2},{6,4},{1,7},{3,1},{5,3},{7,5},{8,14},{10,8},{12,... | collective-permute-start | bytes 393224 | tf_op jit(solution)/shard_map/ppermute | solution.py:33
  46.3 21.4 %copy-start.9 = (f32[64,256]{1,0:T(8,128)S(1)}, f32[64,256]{1,0:T(8,128)}, u32[]{:S(2)}) copy-start(f32[64,256]{1,0:T(8,128)} %copy-done.8) | copy-start | bytes 196612
  46.4 1.3 %collective-permute-start.1 = (f32[8,640]{1,0:T(8,128)S(1)}, f32[8,640]{1,0:T(8,128)S(1)}, u32[]{:S(2)}, u32[]{:S(2)}) collective-permute-start(f32[8,640]{1,0:T(8,128)S(1)} %merge_parts.1.mine_ref.lse_ref), channel_id=1, source_target_pairs={{0,1},{1,0},{2,3},{3,2},{4,5},{5,4},{6,7},{7,6},{8,9},{9,8},{10,11... | collective-permute-start | bytes 61448 | tf_op jit(solution)/shard_map/ppermute | solution.py:33
  47.7 1.4 %copy-start.4 = (bf16[256,3072]{1,0:T(8,128)(2,1)S(1)}, bf16[256,3072]{1,0:T(8,128)(2,1)}, u32[]{:S(2)}) copy-start(bf16[256,3072]{1,0:T(8,128)(2,1)} %k_ref.3) | copy-start | bytes 4718596
  53.1 36.7 %copy-start.6 = (f32[256,128]{1,0:T(8,128)S(1)}, f32[256,128]{1,0:T(8,128)}, u32[]{:S(2)}) copy-start(f32[256,128]{1,0:T(8,128)} %get-tuple-element.29.ik_ref) | copy-start | bytes 393220
  53.1 38.6 %copy-start.2 = (bf16[512,1024]{1,0:T(8,128)(2,1)S(1)}, bf16[512,1024]{1,0:T(8,128)(2,1)}, u32[]{:S(2)}) copy-start(bf16[512,1024]{1,0:T(8,128)(2,1)} %iq_ref.3) | copy-start | bytes 3145732
  53.1 38.6 %copy-start.7 = (f32[512,8]{0,1:T(8,128)S(1)}, f32[512,8]{0,1:T(8,128)}, u32[]{:S(2)}) copy-start(f32[512,8]{0,1:T(8,128)} %param.11) | copy-start | bytes 49156
  68.4 1.3 %collective-permute-start.5 = (f32[2,32,128]{2,1,0:T(8,128)S(1)}, f32[2,32,128]{2,1,0:T(8,128)S(1)}, u32[]{:S(2)}, u32[]{:S(2)}) collective-permute-start(f32[2,32,128]{2,1,0:T(8,128)S(1)} %get-tuple-element.33), channel_id=1, source_target_pairs={{0,1},{1,0},{2,3},{3,2},{4,5},{5,4},{6,7},{7,6},{8,9},{9,8},{10,11... | collective-permute-start | bytes 98312 | tf_op jit(solution)/shard_map/ppermute | solution.py:33
  71.1 13.8 %all-to-all-start.4 = ((f32[8,4,32,128]{3,2,1,0:T(8,128)}), f32[8,4,32,128]{3,2,1,0:T(8,128)S(1)}, u32[]{:S(2)}, u32[]{:S(2)}) async-start(f32[8,4,32,128]{3,2,1,0:T(8,128)} %get-tuple-element.43), calls=%async_computation.4 | async-start | bytes 1048576 | tf_op jit(solution)/shard_map/all_to_all | solution.py:466
  76.3 5.0 %collective-permute-start.6 = (f32[4,8,128]{2,1,0:T(8,128)S(1)}, f32[4,8,128]{2,1,0:T(8,128)S(1)}, u32[]{:S(2)}, u32[]{:S(2)}) collective-permute-start(f32[4,8,128]{2,1,0:T(8,128)S(1)} %get-tuple-element.35), channel_id=1, source_target_pairs={{0,2},{2,4},{4,6},{6,0},{1,3},{3,5},{5,7},{7,1},{8,10},{10,12},{12... | collective-permute-start | bytes 49160 | tf_op jit(solution)/shard_map/ppermute | solution.py:33
  76.9 5.2 %collective-permute-start.7 = (f32[4,8,128]{2,1,0:T(8,128)S(1)}, f32[4,8,128]{2,1,0:T(8,128)S(1)}, u32[]{:S(2)}, u32[]{:S(2)}) collective-permute-start(f32[4,8,128]{2,1,0:T(8,128)S(1)} %get-tuple-element.36), channel_id=1, source_target_pairs={{0,4},{2,6},{4,0},{6,2},{1,5},{3,7},{5,1},{7,3},{8,12},{10,14},{12... | collective-permute-start | bytes 49160 | tf_op jit(solution)/shard_map/ppermute | solution.py:33
  78.9 3.7 %collective-permute-start.8 = (f32[4,8,128]{2,1,0:T(8,128)S(1)}, f32[4,8,128]{2,1,0:T(8,128)S(1)}, u32[]{:S(2)}, u32[]{:S(2)}) collective-permute-start(f32[4,8,128]{2,1,0:T(8,128)S(1)} %get-tuple-element.37), channel_id=1, source_target_pairs={{0,6},{2,0},{4,2},{6,4},{1,7},{3,1},{5,3},{7,5},{8,14},{10,8},{12,... | collective-permute-start | bytes 49160 | tf_op jit(solution)/shard_map/ppermute | solution.py:33
  85.0 13.0 %all-to-all-start.3 = ((f32[8,4,4,8,128]{4,3,2,1,0:T(8,128)}), f32[8,4,4,8,128]{4,3,2,1,0:T(8,128)S(1)}, u32[]{:S(2)}, u32[]{:S(2)}) async-start(f32[8,4,4,8,128]{4,3,2,1,0:T(8,128)} %repeat_parts.1), calls=%async_computation.3 | async-start | bytes 1048576 | tf_op jit(solution)/shard_map/all_to_all | solution.py:468
  89.8 7.1 %collective-permute-start.10 = (f32[3,256,128]{2,1,0:T(8,128)S(1)}, f32[3,256,128]{2,1,0:T(8,128)S(1)}, u32[]{:S(2)}, u32[]{:S(2)}) collective-permute-start(f32[3,256,128]{2,1,0:T(8,128)S(1)} %get-tuple-element.38.own_ref), channel_id=1, source_target_pairs={{0,1},{1,0},{2,3},{3,2},{4,5},{5,4},{6,7},{7,6},{8,9},{9,8},{10,11... | collective-permute-start | bytes 1179656 | tf_op jit(solution)/shard_map/ppermute | solution.py:33
  89.8 1.9 %collective-permute-start.9 = (f32[256,128]{1,0:T(8,128)S(1)}, f32[256,128]{1,0:T(8,128)S(1)}, u32[]{:S(2)}, u32[]{:S(2)}) collective-permute-start(f32[256,128]{1,0:T(8,128)S(1)} %copy-done.6), channel_id=1, source_target_pairs={{0,1},{1,0},{2,3},{3,2},{4,5},{5,4},{6,7},{7,6},{8,9},{9,8},{10,11... | collective-permute-start | bytes 393224 | tf_op jit(solution)/shard_map/ppermute | solution.py:33
  93.8 1.4 %collective-permute-start.14 = (f32[256,128]{1,0:T(8,128)S(1)}, f32[256,128]{1,0:T(8,128)S(1)}, u32[]{:S(2)}, u32[]{:S(2)}) collective-permute-start(f32[256,128]{1,0:T(8,128)S(1)} %get-tuple-element.45), channel_id=1, source_target_pairs={{0,1},{1,0},{2,3},{3,2},{4,5},{5,4},{6,7},{7,6},{8,9},{9,8},{10,11... | collective-permute-start | bytes 393224 | tf_op jit(solution)/shard_map/ppermute | solution.py:33
  95.3 11.9 %collective-permute-start.15 = (f32[256,128]{1,0:T(8,128)S(1)}, f32[256,128]{1,0:T(8,128)S(1)}, u32[]{:S(2)}, u32[]{:S(2)}) collective-permute-start(f32[256,128]{1,0:T(8,128)S(1)} %add.39), channel_id=1, source_target_pairs={{0,128},{128,0},{1,129},{129,1},{2,130},{130,2},{3,131},{131,3},{4... | collective-permute-start | bytes 393224 | tf_op jit(solution)/shard_map/ppermute | solution.py:33
  100.3 10.8 %collective-permute-start.11 = (f32[16,1024]{1,0:T(8,128)S(1)}, f32[16,1024]{1,0:T(8,128)S(1)}, u32[]{:S(2)}, u32[]{:S(2)}) collective-permute-start(f32[16,1024]{1,0:T(8,128)S(1)} %get-tuple-element.40), channel_id=1, source_target_pairs={{0,8},{8,16},{16,24},{24,0},{1,9},{9,17},{17,25},{25,1},{2,10},{10... | collective-permute-start | bytes 196616 | tf_op jit(solution)/shard_map/ppermute | solution.py:33
  101.5 10.4 %collective-permute-start.12 = (f32[16,1024]{1,0:T(8,128)S(1)}, f32[16,1024]{1,0:T(8,128)S(1)}, u32[]{:S(2)}, u32[]{:S(2)}) collective-permute-start(f32[16,1024]{1,0:T(8,128)S(1)} %get-tuple-element.41), channel_id=1, source_target_pairs={{0,16},{8,24},{16,0},{24,8},{1,17},{9,25},{17,1},{25,9},{2,18},{10... | collective-permute-start | bytes 196616 | tf_op jit(solution)/shard_map/ppermute | solution.py:33
  104.9 8.2 %collective-permute-start.13 = (f32[16,1024]{1,0:T(8,128)S(1)}, f32[16,1024]{1,0:T(8,128)S(1)}, u32[]{:S(2)}, u32[]{:S(2)}) collective-permute-start(f32[16,1024]{1,0:T(8,128)S(1)} %get-tuple-element.42), channel_id=1, source_target_pairs={{0,24},{8,0},{16,8},{24,16},{1,25},{9,1},{17,9},{25,17},{2,26},{10... | collective-permute-start | bytes 196616 | tf_op jit(solution)/shard_map/ppermute | solution.py:33
  107.2 6.5 %collective-permute-start.16 = (f32[256,128]{1,0:T(8,128)S(1)}, f32[256,128]{1,0:T(8,128)S(1)}, u32[]{:S(2)}, u32[]{:S(2)}) collective-permute-start(f32[256,128]{1,0:T(8,128)S(1)} %add.40), channel_id=1, source_target_pairs={{0,32},{32,64},{64,96},{96,0},{1,33},{33,65},{65,97},{97,1},{2,34}... | collective-permute-start | bytes 393224 | tf_op jit(solution)/shard_map/ppermute | solution.py:33
  108.6 7.2 %collective-permute-start.17 = (f32[256,128]{1,0:T(8,128)S(1)}, f32[256,128]{1,0:T(8,128)S(1)}, u32[]{:S(2)}, u32[]{:S(2)}) collective-permute-start(f32[256,128]{1,0:T(8,128)S(1)} %add.40), channel_id=1, source_target_pairs={{0,64},{32,96},{64,0},{96,32},{1,65},{33,97},{65,1},{97,33},{2,66}... | collective-permute-start | bytes 393224 | tf_op jit(solution)/shard_map/ppermute | solution.py:33
  111.0 6.0 %collective-permute-start.18 = (f32[256,128]{1,0:T(8,128)S(1)}, f32[256,128]{1,0:T(8,128)S(1)}, u32[]{:S(2)}, u32[]{:S(2)}) collective-permute-start(f32[256,128]{1,0:T(8,128)S(1)} %add.40), channel_id=1, source_target_pairs={{0,96},{32,0},{64,32},{96,64},{1,97},{33,1},{65,33},{97,65},{2,98}... | collective-permute-start | bytes 393224 | tf_op jit(solution)/shard_map/ppermute | solution.py:33

commit v4 on v3

--- a/solution.py
+++ b/solution.py
@@ -213,14 +213,12 @@
 
 
 def probs_kernel(
-    sc_ref, q_ref, k_ref, off_ref, qp_ref, mine_ref, other_ref, b1, b2, b3, out_ref, stack_ref, bias, lse, tr
+    sc_ref, q_ref, k_ref, off_ref, qp_ref, mine_ref, other_ref, b1, b2, b3, out_ref, bias, lse, tr
 ):
     fill_bias(bias, sc_ref, off_ref, qp_ref)
     half, rows = mine_ref.shape[0], lse.shape[1]
     for ref, core in ((mine_ref, sc_ref[0]), (other_ref, 1 - sc_ref[0])):
         lse[pl.ds(pl.multiple_of(core * half, half), half), :] = ref[:, :rows]
-    for i, ref in enumerate((b1, b2, b3)):
-        stack_ref[i] = ref[...]
     total = None
     for head in range(0, lse.shape[0], 2):
         pair = [
@@ -235,12 +233,9 @@
     heads = queries.shape[1] // HEAD_DIM
     return pl.pallas_call(
         probs_kernel,
-        in_specs=[SMEM_SPEC] + [VMEM_SPEC] * 9,
-        out_specs=[VMEM_SPEC] * 2,
-        out_shape=[
-            jax.ShapeDtypeStruct((n_head, rows // n_head, keys), F32),
-            jax.ShapeDtypeStruct((len(blocks), *blocks[0].shape), F32),
-        ],
+        in_specs=[SMEM_SPEC] + [VMEM_SPEC] * 6 + [ANY_SPEC] * 3,
+        out_specs=VMEM_SPEC,
+        out_shape=jax.ShapeDtypeStruct((n_head, rows // n_head, keys), F32),
         scratch_shapes=[
             pltpu.VMEM((keys, rows), F32),
             pltpu.VMEM((heads, rows), F32),
@@ -251,77 +246,54 @@
     )(sc, queries, attn_keys, off, qp, mine, other, *blocks)
 
 
-def step_kernel(sc_ref, target_ref, logits_ref, lse_ref, keep_ref, give_ref, tmp):
+def step_kernel(sc_ref, target_ref, logits_ref, lse_ref, wide_ref, x1_ref, x2_ref, x3_ref, x0_ref, tmp, turn):
     target = jnp.sum(target_ref[...], axis=0) * (1.0 / HEADS)
     blk, keys = target.shape
     rows = lse_ref.shape[1] - LANES
     lse = lse_ref[:8, rows:].T[:blk, :1]
     step = jnp.exp(logits_ref[...] - lse) - target
     for half in range(keys // LANES):
-        span = slice(half * LANES, (half + 1) * LANES)
-        tmp[half * blk : (half + 1) * blk, :] = step[:, span]
-        for out_ref, core in ((keep_ref, sc_ref[0]), (give_ref, 1 - sc_ref[0])):
+        part = step[:, half * LANES : (half + 1) * LANES]
+        for h in range(wide_ref.shape[0]):
+            wide_ref[h, half] = part
+        tmp[half] = part
+        for z in range(4):
             for x in range(4):
-                for r in range(2):
-                    out_ref[half, pl.ds(8 * x + r, 4, stride=2), :] = tmp[
-                        pl.ds(half * blk + 4 * x + 2 * core + r, 4, stride=16), :
-                    ]
+                turn[half, 16 * x + 4 * z : 16 * x + 4 * z + 4, :] = tmp[half, 16 * z + 4 * x : 16 * z + 4 * x + 4, :]
+    for k, x_ref in ((1, x1_ref), (2, x2_ref), (3, x3_ref), (0, x0_ref)):
+        x_ref[...] = turn[:, pl.ds(pl.multiple_of(lax.rem(sc_ref[1] + k, 4) * 16, 16), 16), :]
 
 
 def prob_step(sc, target_parts, logits, lse):
-    _, blk, keys = target_parts.shape
-    out = jax.ShapeDtypeStruct((keys // LANES, blk // 2, LANES), F32)
+    n_head, blk, keys = target_parts.shape
+    halves = keys // LANES
+    piece = jax.ShapeDtypeStruct((halves, blk // 4, LANES), F32)
     return pl.pallas_call(
         step_kernel,
         in_specs=[SMEM_SPEC] + [VMEM_SPEC] * 3,
-        out_specs=[VMEM_SPEC] * 2,
-        out_shape=[out, out],
-        scratch_shapes=[pltpu.VMEM((blk * keys // LANES, LANES), F32)],
+        out_specs=[VMEM_SPEC] * 5,
+        out_shape=[jax.ShapeDtypeStruct((n_head, halves, blk, LANES), F32)] + [piece] * 4,
+        scratch_shapes=[pltpu.VMEM((halves, blk, LANES), F32)] * 2,
         compiler_params=PARAMS,
         name="prob_step",
     )(sc, target_parts, logits, lse)
 
 
-def wide_kernel(sc_ref, mine_ref, got_ref, out_ref, x1_ref, x2_ref, x3_ref, x0_ref):
-    n = mine_ref.shape[0]
-    for h in range(out_ref.shape[0]):
-        out_ref[h, :n] = mine_ref[...]
-        out_ref[h, n:] = got_ref[...]
-    each = x0_ref.shape[1]
-    for k, x_ref in ((1, x1_ref), (2, x2_ref), (3, x3_ref), (0, x0_ref)):
-        rows = pl.ds(pl.multiple_of(lax.rem(sc_ref[1] + k, 4) * each, each), each)
-        x_ref[:n] = mine_ref[:, rows, :]
-        x_ref[n:] = got_ref[:, rows, :]
-
-
-def widen(sc, mine, got, n_head):
-    n, half, _ = mine.shape
-    piece = jax.ShapeDtypeStruct((2 * n, half // 4, LANES), F32)
-    return pl.pallas_call(
-        wide_kernel,
-        in_specs=[SMEM_SPEC] + [VMEM_SPEC] * 2,
-        out_specs=[VMEM_SPEC] * 5,
-        out_shape=[jax.ShapeDtypeStruct((n_head, 2 * n, half, LANES), F32)] + [piece] * 4,
-        compiler_params=PARAMS,
-        name="widen",
-    )(sc, mine, got)
-
-
-def around_kernel(p0, p1, p2, p3, out_ref):
+def around_kernel(p0, p1, p2, p3, first, out_ref):
     for h in range(out_ref.shape[0]):
         for k, ref in enumerate((p0, p1, p2, p3)):
             out_ref[h, k] = ref[...]
 
 
-def repeat_parts(parts, n_head):
+def repeat_parts(parts, first, n_head):
     return pl.pallas_call(
         around_kernel,
-        in_specs=[VMEM_SPEC] * 4,
+        in_specs=[VMEM_SPEC] * 4 + [ANY_SPEC],
         out_specs=VMEM_SPEC,
         out_shape=jax.ShapeDtypeStruct((n_head, len(parts), *parts[0].shape), F32),
         compiler_params=PARAMS,
         name="repeat_parts",
-    )(*parts)
+    )(*parts, first)
 
 
 def weight_rows(wt_ref):
@@ -329,31 +301,27 @@
     return jnp.concatenate([wt, jnp.zeros((LANES - wt.shape[0], wt.shape[1]), F32)], axis=0).T
 
 
-def row_blocks(sc_ref, x):
-    return [pl.multiple_of(128 * z + 32 * x + 16 * sc_ref[0], 16) for z in range(4)]
-
-
-def query_kernel(sc_ref, step_ref, iq_ref, wt_ref, ik_ref, ik2_ref, own_ref, far_ref, o1_ref, o2_ref, o3_ref, o0_ref, tr, iqs, acc, w_ref):
+def query_kernel(sc_ref, step_ref, iq_ref, wt_ref, i0_ref, i1_ref, i2_ref, i3_ref, first, keep_ref, give_ref, tr, iqs, acc, w_ref):
     w_ref[...] = weight_rows(wt_ref)
     n_head, n_x, quarters, each, _ = step_ref.shape
     size = each * n_head
+    block = size // 4
     jl = iq_ref.shape[1] // IDIM
-    blocks = row_blocks(sc_ref, sc_ref[1])
-    w = jnp.concatenate([w_ref[pl.ds(b, 16), :] for b in blocks], axis=0)
+    starts = [pl.multiple_of(4 * block * z + block * sc_ref[1], block) for z in range(4)]
+    w = jnp.concatenate([w_ref[pl.ds(b, block), :] for b in starts], axis=0)
     for j in range(jl):
-        for z, b in enumerate(blocks):
-            iqs[j * size + 16 * z : j * size + 16 * z + 16, :] = iq_ref[pl.ds(b, 16), j * IDIM : (j + 1) * IDIM]
+        for z, b in enumerate(starts):
+            at = j * size + block * z
+            iqs[at : at + block, :] = iq_ref[pl.ds(b, block), j * IDIM : (j + 1) * IDIM]
     total = None
-    for k in range(n_x):
+    for k, ik_ref in enumerate((i0_ref, i1_ref, i2_ref, i3_ref)):
         for c in range(quarters):
             for h in range(n_head):
-                at = (k * quarters + c) * size
-                tr[pl.ds(at + h, each, stride=n_head), :] = step_ref[h, k, c]
+                tr[pl.ds((k * quarters + c) * size + h, each, stride=n_head), :] = step_ref[h, k, c]
         step = jnp.concatenate(
             [tr[(k * quarters + c) * size : (k * quarters + c + 1) * size, :] for c in range(quarters)], axis=1
         )
-        near, far = (ik_ref[...], ik2_ref[...]) if k == 0 else (own_ref[k - 1], far_ref[k - 1])
-        ik = jnp.concatenate([near, far], axis=0).astype(BF16)
+        ik = ik_ref[...].astype(BF16)
         act = dot_t(iqs[...], ik)
         terms = jnp.concatenate(
             [
@@ -365,80 +333,85 @@
         part = jnp.dot(terms, ik, preferred_element_type=F32)
         total = part if total is None else total + part
     acc[...] = total
-    piece = size // 4
-    for k, out_ref in ((1, o1_ref), (2, o2_ref), (3, o3_ref), (0, o0_ref)):
-        z = lax.rem(sc_ref[2] + k, 4)
-        for j in range(jl):
-            out_ref[:, j * IDIM : (j + 1) * IDIM] = acc[pl.ds(pl.multiple_of(j * size + z * piece, piece), piece), :]
-
-
-def query_pieces(sc, step, iq, wt, ik, ik2, own, far):
+    piece = block // 2
+    for out_ref, core in ((give_ref, 1 - sc_ref[0]), (keep_ref, sc_ref[0])):
+        for i, k in enumerate((1, 2, 3, 0)):
+            z = lax.rem(sc_ref[2] + k, 4)
+            for j in range(jl):
+                at = pl.multiple_of(j * size + z * block + core * piece, piece)
+                out_ref[i * piece : (i + 1) * piece, j * IDIM : (j + 1) * IDIM] = acc[pl.ds(at, piece), :]
+
+
+def query_pieces(sc, step, iq, wt, blocks, first):
     n_head, n_x, quarters, each, _ = step.shape
     size = each * n_head
-    out = jax.ShapeDtypeStruct((size // 4, iq.shape[1]), F32)
+    jl = iq.shape[1] // IDIM
+    out = jax.ShapeDtypeStruct((size // 2, iq.shape[1]), F32)
     return pl.pallas_call(
         query_kernel,
-        in_specs=[SMEM_SPEC] + [VMEM_SPEC] * 7,
+        in_specs=[SMEM_SPEC] + [VMEM_SPEC] * 7 + [ANY_SPEC],
+        out_specs=[VMEM_SPEC] * 2,
+        out_shape=[out] * 2,
+        scratch_shapes=[
+            pltpu.VMEM((n_x * quarters * size, LANES), F32),
+            pltpu.VMEM((size * jl, IDIM), BF16),
+            pltpu.VMEM((size * jl, IDIM), F32),
+            pltpu.VMEM((iq.shape[0], LANES), F32),
+        ],
+        compiler_params=PARAMS,
+        name="query_pieces",
+    )(sc, step, iq, wt, *blocks, first)
+
+
+def fold_kernel(keep_ref, got_ref, o1_ref, o2_ref, o3_ref, o0_ref):
+    piece = o0_ref.shape[0]
+    for i, out_ref in enumerate((o1_ref, o2_ref, o3_ref, o0_ref)):
+        out_ref[...] = keep_ref[i * piece : (i + 1) * piece] + got_ref[i * piece : (i + 1) * piece]
+
+
+def fold(keep, got):
+    out = jax.ShapeDtypeStruct((keep.shape[0] // 4, keep.shape[1]), F32)
+    return pl.pallas_call(
+        fold_kernel,
+        in_specs=[VMEM_SPEC] * 2,
         out_specs=[VMEM_SPEC] * 4,
         out_shape=[out] * 4,
-        scratch_shapes=[
-            pltpu.VMEM((n_x * quarters * size, LANES), F32),
-            pltpu.VMEM((size * iq.shape[1] // IDIM, IDIM), BF16),
-            pltpu.VMEM((size * iq.shape[1] // IDIM, IDIM), F32),
-            pltpu.VMEM((iq.shape[0], LANES), F32),
-        ],
-        compiler_params=PARAMS,
-        name="query_pieces",
-    )(sc, step, iq, wt, ik, ik2, own, far)
-
-
-def key_kernel(sc_ref, step_ref, iq_ref, ik_ref, ik2_ref, wt_ref, keep_ref, give_ref, tr, iqs, ws, w_ref):
-    w_ref[...] = weight_rows(wt_ref)
-    n, quarters, half, _ = step_ref.shape
-    size = n * half
+        compiler_params=PARAMS,
+        name="fold",
+    )(keep, got)
+
+
+def key_kernel(step_ref, iq_ref, ik_ref, wt_ref, out_ref, tr):
+    n, halves, blk, _ = step_ref.shape
     turned = []
-    for c in range(quarters):
+    for c in range(halves):
+        base = c * n * blk
         for h in range(n):
-            tr[pl.ds(h, half, stride=n), :] = step_ref[h, c]
-        turned.append(tr[...].T)
+            tr[pl.ds(base + h, blk, stride=n), :] = step_ref[h, c]
+        turned.append(tr[base : base + n * blk, :].T)
     step = jnp.concatenate(turned, axis=0)
-    for x in range(4):
-        for z, b in enumerate(row_blocks(sc_ref, x)):
-            at = 64 * x + 16 * z
-            iqs[at : at + 16, :] = iq_ref[pl.ds(b, 16), :]
-            ws[at : at + 16, :] = w_ref[pl.ds(b, 16), :]
-    wt = ws[...].T
-    ik = jnp.concatenate([ik_ref[...], ik2_ref[...]], axis=0).astype(BF16)
+    ik = ik_ref[...].astype(BF16)
     total = None
-    for j in range(iq_ref.shape[1] // IDIM):
-        iq = iqs[:, j * IDIM : (j + 1) * IDIM]
+    for j in range(wt_ref.shape[0]):
+        iq = iq_ref[:, j * IDIM : (j + 1) * IDIM]
         act = dot_t(ik, iq)
-        terms = jnp.where(act > 0.0, step * wt[j : j + 1, :], 0.0).astype(BF16)
+        terms = jnp.where(act > 0.0, step * (wt_ref[j : j + 1, :] * INV_SCALE), 0.0).astype(BF16)
         part = jnp.dot(terms, iq, preferred_element_type=F32)
         total = part if total is None else total + part
-    keys = keep_ref.shape[0]
-    keep_ref[...] = total[:keys]
-    give_ref[...] = total[keys:]
-
-
-def key_part_grad(sc, step, iq, ik, ik2, wt):
-    n, _, half, _ = step.shape
-    size = n * half
-    out = jax.ShapeDtypeStruct(ik.shape, F32)
+    out_ref[...] = total
+
+
+def key_part_grad(step, iq, ik, wt):
+    n, halves, blk, _ = step.shape
     return pl.pallas_call(
         key_kernel,
-        in_specs=[SMEM_SPEC] + [VMEM_SPEC] * 5,
-        out_specs=[VMEM_SPEC] * 2,
-        out_shape=[out, out],
-        scratch_shapes=[
-            pltpu.VMEM((size, LANES), F32),
-            pltpu.VMEM((size, iq.shape[1]), BF16),
-            pltpu.VMEM((size, LANES), F32),
-            pltpu.VMEM((iq.shape[0], LANES), F32),
-        ],
+        in_specs=[VMEM_SPEC] * 4,
+        out_specs=VMEM_SPEC,
+        out_shape=jax.ShapeDtypeStruct(ik.shape, F32),
+        scratch_shapes=[pltpu.VMEM((n * halves * blk, LANES), F32)],
         compiler_params=PARAMS,
         name="key_part_grad",
-    )(sc, step, iq, ik, ik2, wt)
+    )(step, iq, ik, wt)
 
 
 def shards(queries, attn_keys, index_queries, index_keys, head_weights, query_pos, key_offset):
@@ -450,7 +423,6 @@
 
     index, ik = front(index_queries, index_keys, w_t, n_head)
     index = lax.all_to_all(index, HEAD, 0, 0)
-    ik2 = shift(ik, "core", 2, 1)
 
     lse, mask = scores_lse(sc, queries, attn_keys, off, qp, n_head)
     mine, give, logits = join_lse(sc, lse, index, mask)
@@ -458,26 +430,23 @@
     mine = merge_parts(lax.all_to_all(mine, CHIP, 0, 0))
     other = shift(mine, "core", 2, 1)
     around = [shift(ik, "x", 4, k) for k in range(1, 4)]
-    target, around = probs_sum(sc, queries, attn_keys, off, qp, mine, other, around, n_head)
+    target = probs_sum(sc, queries, attn_keys, off, qp, mine, other, around, n_head)
     target = lax.all_to_all(target, HEAD, 0, 0)
 
-    step, give = prob_step(sc, target, logits, mine)
-    step_key, *pieces = widen(sc, step, shift(give, "core", 2, 1), n_head)
+    step_key, *pieces = prob_step(sc, target, logits, mine)
     step_key = lax.all_to_all(step_key, HEAD, 0, 0)
     pieces = [pieces[3]] + [shift(pieces[k - 1], "x", 4, k) for k in range(1, 4)]
-    step_query = lax.all_to_all(repeat_parts(pieces, n_head), HEAD, 0, 0)
-
-    p1, p2, p3, query_grad = query_pieces(
-        sc, step_query, index_queries, w_t, ik, ik2, around, shift(around, "core", 2, 1)
-    )
-    query_grad = query_grad + shift(p1, "z_hi", 4, 1) + shift(p2, "z_hi", 4, 2) + shift(p3, "z_hi", 4, 3)
-
-    key_part, give = key_part_grad(sc, step_key, index_queries, ik, ik2, w_t)
-    key_part = key_part + shift(give, "core", 2, 1)
+    step_query = lax.all_to_all(repeat_parts(pieces, step_key, n_head), HEAD, 0, 0)
+
+    key_part = key_part_grad(step_key, index_queries, ik, w_t)
     key_part = key_part + shift(key_part, "z_lo", 2, 1)
     key_grad = key_part
     for k in range(1, 4):
         key_grad = key_grad + shift(key_part, "y", 4, k)
+
+    keep, give = query_pieces(sc, step_query, index_queries, w_t, [ik] + around, key_part)
+    p1, p2, p3, query_grad = fold(keep, shift(give, "core", 2, 1))
+    query_grad = query_grad + shift(p1, "z_hi", 4, 1) + shift(p2, "z_hi", 4, 2) + shift(p3, "z_hi", 4, 3)
     return (query_grad, key_grad)
 
 

time: 118 us -> 117 us (level)
  starting transfers between devices: 50.9 us -> 49.1 us
  waiting for transfers between devices: 22.7 us -> 24 us
    ppermute x19 -> x16, starting transfers between devices: 24.5 us -> 22.5 us  [shift(): lax.ppermute(value, axis, [(i, (i + step) % size) for i in range(size)])]
    ppermute x19 -> x16, waiting for transfers between devices: 12.6 us -> 14.6 us  [shift(): lax.ppermute(value, axis, [(i, (i + step) % size) for i in range(size)])]
    pallas_call x5, Pallas kernels: 10.6 us -> 8.96 us  [the longest x1 3.49 us: probs_sum(): pl.pallas_call(probs_kernel, in_specs=[SMEM_SPEC] + [VMEM_SPEC] * 6 + [AN...]
    unnamed x28 -> x24, local copies, waits for them, and re-layouts: 7.44 us -> 6.81 us
  transfers between devices with their start and end apart: 23 -> 20, of which waited for: 14 -> 11; matrix products, arithmetic and copies ran while one was open for 1% -> 1% of each run, Pallas kernels for 8% -> 5%
where the time goes in v4:
time: 117 us; the launch traced here: 116 us
  starting transfers between devices  49.1 us (42%)
  waiting for transfers between devices  24 us (21%)
  Pallas kernels  18.7 us (16%)
  blocking collectives  14.6 us (12%)
  local copies, waits for them, and re-layouts  6.89 us (6%)
  other arithmetic  1.35 us (1%)
    ppermute x16, starting transfers between devices, shift(): lax.ppermute(value, axis, [(i, (i + step) % size) for i in range(size)])  22.5 us
    all_to_all x1, blocking collectives, shards(): target = lax.all_to_all(target, HEAD, 0, 0)  14.6 us
    ppermute x16, waiting for transfers between devices, shift(): lax.ppermute(value, axis, [(i, (i + step) % size) for i in range(size)])  14.6 us
    all_to_all x1, starting transfers between devices, shards(): mine = merge_parts(lax.all_to_all(mine, CHIP, 0, 0))  10.1 us
    all_to_all x1, waiting for transfers between devices, shards(): mine = merge_parts(lax.all_to_all(mine, CHIP, 0, 0))  8.74 us
    unnamed x24, local copies, waits for them, and re-layouts  6.81 us
    all_to_all x1, starting transfers between devices, shards(): index = lax.all_to_all(index, HEAD, 0, 0)  6.28 us
    all_to_all x1, starting transfers between devices, shards(): step_key = lax.all_to_all(step_key, HEAD, 0, 0)  5.21 us
  transfers between devices with their start and end apart: 20, of which 11 were waited for; matrix products, arithmetic and copies ran while one was open for 1% of the time, Pallas kernels for 5%

profile of v4, /device:TPU:8, one launch (start us, length us, event | category | flops | bytes accessed | tf_op | source)
XLA Modules:
  0.0 115.5 jit_solution(3253468118637853173)
XLA Ops:
  0.6 3.0 %front.1 = (f32[8,64,256]{2,1,0:T(8,128)}, f32[256,128]{1,0:T(8,128)}) custom-call(bf16[512,1024]{1,0:T(8,128)(2,1)} %iq_ref.3, bf16[256,128]{1,0:T(8,128)(2,1)} %ik_hbm.1, f32[8,512]{1,0:T(8,128)} %bitcast.8), custom_call_target="tpu_custom_call" | custom-call | tf_op jit(solution)/shard_map/front/pallas_call | solution.py:105
  3.7 6.3 %all-to-all-start = ((f32[8,64,256]{2,1,0:T(8,128)}), f32[8,64,256]{2,1,0:T(8,128)}, u32[]{:S(2)}, u32[]{:S(2)}) async-start(f32[8,64,256]{2,1,0:T(8,128)} %get-tuple-element.21), calls=%async_computation | async-start | bytes 1048576 | tf_op jit(solution)/shard_map/all_to_all | solution.py:425
  10.0 0.1 stack.23.sc_ref
  10.0 1.9 %copy-done = bf16[512,3072]{1,0:T(8,128)(2,1)S(1)} copy-done((bf16[512,3072]{1,0:T(8,128)(2,1)S(1)}, bf16[512,3072]{1,0:T(8,128)(2,1)}, u32[]{:S(2)}) %copy-start) | copy-done | bytes 3145752
  11.9 1.4 %copy-done.3 = bf16[256,3072]{1,0:T(8,128)(2,1)S(1)} copy-done((bf16[256,3072]{1,0:T(8,128)(2,1)S(1)}, bf16[256,3072]{1,0:T(8,128)(2,1)}, u32[]{:S(2)}) %copy-start.3) | copy-done | bytes 1572888
  13.3 0.7 copy-done.8
  14.0 0.7 copy-done.10
  14.7 3.7 %scores_lse.1 = (f32[16,512]{1,0:T(8,128)S(1)}, f32[64,256]{1,0:T(8,128)S(1)}) custom-call(s32[5]{0:T(128)S(1)} %stack.23.sc_ref, bf16[512,3072]{1,0:T(8,128)(2,1)S(1)} %copy-done, bf16[256,3072]{1,0:T(8,128)(2,1)S(1)} %copy-done.3, s32[1,256]{1,0:T(1,128)S(1)} %bitcast.13, s32[1,512]{1,0:T(1,128)S(1)} %bitcast.11), custom_call_target="tpu_custom_call" | custom-call | tf_op jit(solution)/shard_map/scores_lse/pallas_call | solution.py:142
  18.4 0.0 all-to-all-done.parts_ref
  18.4 1.3 %join_lse.1 = (f32[8,640]{1,0:T(8,128)S(1)}, f32[8,640]{1,0:T(8,128)S(1)}, f32[64,256]{1,0:T(8,128)S(1)}) custom-call(s32[5]{0:T(128)S(1)} %stack.23.sc_ref, f32[16,512]{1,0:T(8,128)S(1)} %get-tuple-element.20.lse_ref, f32[8,64,256]{2,1,0:T(8,128)} %all-to-all-done.parts_ref, f32[64,256]{1,0:T(8,128)S(1)} %get-tuple-element.22.mask_ref), custom_call_target="tpu_custom_call" | custom-call | tf_op jit(solution)/shard_map/join_lse/pallas_call | solution.py:173
  19.7 0.0 collective-permute-start
  19.8 1.2 %collective-permute-done.got_ref = f32[8,640]{1,0:T(8,128)S(1)} collective-permute-done((f32[8,640]{1,0:T(8,128)S(1)}, f32[8,640]{1,0:T(8,128)S(1)}, u32[]{:S(2)}, u32[]{:S(2)}) %collective-permute-start) | collective-permute-done | bytes 20512 | tf_op jit(solution)/shard_map/ppermute | solution.py:33
  21.0 0.7 copy-done.5
  21.7 10.1 %all-to-all-start.1 = ((f32[16,8,640]{2,1,0:T(8,128)}), f32[16,8,640]{2,1,0:T(8,128)S(1)}, u32[]{:S(2)}, u32[]{:S(2)}) async-start(f32[16,8,640]{2,1,0:T(8,128)} %copy-done.5), calls=%async_computation.1 | async-start | bytes 655360 | tf_op jit(solution)/shard_map/all_to_all | solution.py:430
  31.9 3.1 %collective-permute-start.4 = (f32[256,128]{1,0:T(8,128)}, f32[256,128]{1,0:T(8,128)}, u32[]{:S(2)}, u32[]{:S(2)}) collective-permute-start(f32[256,128]{1,0:T(8,128)} %get-tuple-element.25.ik_ref.i0_ref), channel_id=1, source_target_pairs={{0,6},{2,0},{4,2},{6,4},{1,7},{3,1},{5,3},{7,5},{8,14},{10,8},{12,... | collective-permute-start | bytes 393224 | tf_op jit(solution)/shard_map/ppermute | solution.py:33
  35.0 0.9 collective-permute-start.3
  35.9 0.9 collective-permute-start.2
  36.7 8.7 %all-to-all-done.1.parts_ref = f32[16,8,640]{2,1,0:T(8,128)S(1)} async-done(((f32[16,8,640]{2,1,0:T(8,128)}), f32[16,8,640]{2,1,0:T(8,128)S(1)}, u32[]{:S(2)}, u32[]{:S(2)}) %all-to-all-start.1) | async-done | bytes 327712 | tf_op jit(solution)/shard_map/all_to_all | solution.py:430
  45.5 0.1 merge_parts.1.mine_ref.lse_ref
  45.5 0.1 collective-permute-start.1
  45.6 0.0 collective-permute-done.4.b3.i3_ref
  45.7 0.0 collective-permute-done.3.b2.i2_ref
  45.7 1.0 collective-permute-done.2.b1.i1_ref
  46.7 0.2 collective-permute-done.1.other_ref
  46.8 0.0 copy-done.9
  46.8 0.0 copy-start.4
  46.8 1.4 %copy-done.4 = bf16[256,3072]{1,0:T(8,128)(2,1)S(1)} copy-done((bf16[256,3072]{1,0:T(8,128)(2,1)S(1)}, bf16[256,3072]{1,0:T(8,128)(2,1)}, u32[]{:S(2)}) %copy-start.4) | copy-done | bytes 1572888
  48.2 3.5 %probs_sum.1 = f32[8,64,256]{2,1,0:T(8,128)S(1)} custom-call(s32[5]{0:T(128)S(1)} %stack.23.sc_ref, bf16[512,3072]{1,0:T(8,128)(2,1)S(1)} %copy-done.1, bf16[256,3072]{1,0:T(8,128)(2,1)S(1)} %copy-done.4, s32[1,256]{1,0:T(1,128)S(1)} %bitcast.14, s32[1,512]{1,0:T(1,128)S(1)} %bitcast.12, f32[8,640]{1,0:T(8,128)S(1)} %merge_parts.1.mine_ref.lse_ref, ...), custom_call_target="tpu_custom_call" | custom-call | tf_op jit(solution)/shard_map/probs_sum/pallas_call | solution.py:234
  51.7 0.0 copy-start.2
  51.8 0.0 copy-start.6
  51.8 0.0 copy-start.7
  51.8 14.6 %all_to_all.25.target_ref = f32[8,64,256]{2,1,0:T(8,128)S(1)} all-to-all(f32[8,64,256]{2,1,0:T(8,128)S(1)} %probs_sum.1), channel_id=1, replica_groups=mesh['z_lo'=2,'y'=4,'z_hi'=4,'x'=4,'core'=2] {'z_lo','y'}, dimensions={0} | all-to-all | bytes 1048576 | tf_op jit(solution)/shard_map/all_to_all | solution.py:434
  66.4 1.5 %prob_step.1 = (f32[8,2,64,128]{3,2,1,0:T(8,128)}, f32[2,16,128]{2,1,0:T(8,128)S(1)}, f32[2,16,128]{2,1,0:T(8,128)S(1)}, f32[2,16,128]{2,1,0:T(8,128)S(1)}, f32[2,16,128]{2,1,0:T(8,128)S(1)}) custom-call(s32[5]{0:T(128)S(1)} %stack.23.sc_ref, f32[8,64,256]{2,1,0:T(8,128)S(1)} %all_to_all.25.target_ref, f32[64,256]{1,0:T(8,128)S(1)} %get-tuple-element.26.logits_ref, ...), custom_call_target="tpu_custom_call" | custom-call | tf_op jit(solution)/shard_map/prob_step/pallas_call | solution.py:271
  68.0 5.2 %all-to-all-start.3 = ((f32[8,2,64,128]{3,2,1,0:T(8,128)}), f32[8,2,64,128]{3,2,1,0:T(8,128)S(1)}, u32[]{:S(2)}, u32[]{:S(2)}) async-start(f32[8,2,64,128]{3,2,1,0:T(8,128)} %get-tuple-element.31), calls=%async_computation.3 | async-start | bytes 1048576 | tf_op jit(solution)/shard_map/all_to_all | solution.py:437
  73.2 0.6 collective-permute-start.5
  73.7 2.0 %collective-permute-start.6 = (f32[2,16,128]{2,1,0:T(8,128)S(1)}, f32[2,16,128]{2,1,0:T(8,128)S(1)}, u32[]{:S(2)}, u32[]{:S(2)}) collective-permute-start(f32[2,16,128]{2,1,0:T(8,128)S(1)} %get-tuple-element.29), channel_id=1, source_target_pairs={{0,4},{2,6},{4,0},{6,2},{1,5},{3,7},{5,1},{7,3},{8,12},{10,14},{12... | collective-permute-start | bytes 49160 | tf_op jit(solution)/shard_map/ppermute | solution.py:33
  75.8 1.8 %collective-permute-start.7 = (f32[2,16,128]{2,1,0:T(8,128)S(1)}, f32[2,16,128]{2,1,0:T(8,128)S(1)}, u32[]{:S(2)}, u32[]{:S(2)}) collective-permute-start(f32[2,16,128]{2,1,0:T(8,128)S(1)} %get-tuple-element.30), channel_id=1, source_target_pairs={{0,6},{2,0},{4,2},{6,4},{1,7},{3,1},{5,3},{7,5},{8,14},{10,8},{12,... | collective-permute-start | bytes 49160 | tf_op jit(solution)/shard_map/ppermute | solution.py:33
  77.5 0.6 collective-permute-done.5.p1
  78.1 0.9 collective-permute-done.6.p2
  79.0 0.5 collective-permute-done.7.p3
  79.5 0.7 all-to-all-done.3.first.step_ref
  80.2 0.8 repeat_parts.1
  81.0 5.1 %all-to-all-start.4 = ((f32[8,4,2,16,128]{4,3,2,1,0:T(8,128)}), f32[8,4,2,16,128]{4,3,2,1,0:T(8,128)S(1)}, u32[]{:S(2)}, u32[]{:S(2)}) async-start(f32[8,4,2,16,128]{4,3,2,1,0:T(8,128)} %repeat_parts.1), calls=%async_computation.4 | async-start | bytes 1048576 | tf_op jit(solution)/shard_map/all_to_all | solution.py:439
  86.1 1.9 %key_part_grad.1 = f32[256,128]{1,0:T(8,128)S(1)} custom-call(f32[8,2,64,128]{3,2,1,0:T(8,128)S(1)} %all-to-all-done.3.first.step_ref, bf16[512,1024]{1,0:T(8,128)(2,1)S(1)} %copy-done.2, f32[256,128]{1,0:T(8,128)S(1)} %copy-done.6, f32[8,512]{1,0:T(8,128)S(1)} %bitcast.9), custom_call_target="tpu_custom_call" | custom-call | tf_op jit(solution)/shard_map/key_part_grad/pallas_call | solution.py:406
  87.9 1.6 %collective-permute-start.8 = (f32[256,128]{1,0:T(8,128)S(1)}, f32[256,128]{1,0:T(8,128)S(1)}, u32[]{:S(2)}, u32[]{:S(2)}) collective-permute-start(f32[256,128]{1,0:T(8,128)S(1)} %key_part_grad.1), channel_id=1, source_target_pairs={{0,128},{128,0},{1,129},{129,1},{2,130},{130,2},{3,131},{131,3},{4... | collective-permute-start | bytes 393224 | tf_op jit(solution)/shard_map/ppermute | solution.py:33
  89.5 5.8 %collective-permute-done.8 = f32[256,128]{1,0:T(8,128)S(1)} collective-permute-done((f32[256,128]{1,0:T(8,128)S(1)}, f32[256,128]{1,0:T(8,128)S(1)}, u32[]{:S(2)}, u32[]{:S(2)}) %collective-permute-start.8) | collective-permute-done | bytes 131104 | tf_op jit(solution)/shard_map/ppermute | solution.py:33
  95.3 0.0 all-to-all-done.4.step_ref
  95.3 2.8 %query_pieces.1 = (f32[64,1024]{1,0:T(8,128)S(1)}, f32[64,1024]{1,0:T(8,128)S(1)}) custom-call(s32[5]{0:T(128)S(1)} %stack.23.sc_ref, f32[8,4,2,16,128]{4,3,2,1,0:T(8,128)S(1)} %all-to-all-done.4.step_ref, bf16[512,1024]{1,0:T(8,128)(2,1)S(1)} %copy-done.2, f32[8,512]{1,0:T(8,128)S(1)} %bitcast.10, f32[256,128]{1,0:T(8,128)S(1)} %copy-done.6, ...), custom_call_target="tpu_custom_call" | custom-call | tf_op jit(solution)/shard_map/query_pieces/pallas_call | solution.py:350
  98.1 0.1 collective-permute-start.9
  98.2 0.6 collective-permute-start.15
  98.8 2.3 %collective-permute-start.14 = (f32[256,128]{1,0:T(8,128)S(1)}, f32[256,128]{1,0:T(8,128)S(1)}, u32[]{:S(2)}, u32[]{:S(2)}) collective-permute-start(f32[256,128]{1,0:T(8,128)S(1)} %add.33.first), channel_id=1, source_target_pairs={{0,64},{32,96},{64,0},{96,32},{1,65},{33,97},{65,1},{97,33},{2,66}... | collective-permute-start | bytes 393224 | tf_op jit(solution)/shard_map/ppermute | solution.py:33
  101.2 1.8 %collective-permute-start.13 = (f32[256,128]{1,0:T(8,128)S(1)}, f32[256,128]{1,0:T(8,128)S(1)}, u32[]{:S(2)}, u32[]{:S(2)}) collective-permute-start(f32[256,128]{1,0:T(8,128)S(1)} %add.33.first), channel_id=1, source_target_pairs={{0,32},{32,64},{64,96},{96,0},{1,33},{33,65},{65,97},{97,1},{2,34}... | collective-permute-start | bytes 393224 | tf_op jit(solution)/shard_map/ppermute | solution.py:33
  103.0 0.0 collective-permute-done.9.got_ref
  103.0 0.3 collective-permute-start.10
  103.3 2.9 %collective-permute-start.11 = (f32[16,1024]{1,0:T(8,128)S(1)}, f32[16,1024]{1,0:T(8,128)S(1)}, u32[]{:S(2)}, u32[]{:S(2)}) collective-permute-start(f32[16,1024]{1,0:T(8,128)S(1)} %get-tuple-element.36), channel_id=1, source_target_pairs={{0,16},{8,24},{16,0},{24,8},{1,17},{9,25},{17,1},{25,9},{2,18},{10... | collective-permute-start | bytes 196616 | tf_op jit(solution)/shard_map/ppermute | solution.py:33
  106.2 0.0 collective-permute-done.15
  106.2 3.6 %collective-permute-start.12 = (f32[16,1024]{1,0:T(8,128)S(1)}, f32[16,1024]{1,0:T(8,128)S(1)}, u32[]{:S(2)}, u32[]{:S(2)}) collective-permute-start(f32[16,1024]{1,0:T(8,128)S(1)} %get-tuple-element.37), channel_id=1, source_target_pairs={{0,24},{8,0},{16,8},{24,16},{1,25},{9,1},{17,9},{25,17},{2,26},{10... | collective-permute-start | bytes 196616 | tf_op jit(solution)/shard_map/ppermute | solution.py:33
  109.7 0.0 collective-permute-done.14
  109.7 0.0 collective-permute-done.13
  109.7 0.7 add_add_fusion
  110.4 0.0 collective-permute-done.10
  110.4 1.2 %collective-permute-done.11 = f32[16,1024]{1,0:T(8,128)S(1)} collective-permute-done((f32[16,1024]{1,0:T(8,128)S(1)}, f32[16,1024]{1,0:T(8,128)S(1)}, u32[]{:S(2)}, u32[]{:S(2)}) %collective-permute-start.11) | collective-permute-done | bytes 65568 | tf_op jit(solution)/shard_map/ppermute | solution.py:33
  111.6 3.3 %collective-permute-done.12 = f32[16,1024]{1,0:T(8,128)S(1)} collective-permute-done((f32[16,1024]{1,0:T(8,128)S(1)}, f32[16,1024]{1,0:T(8,128)S(1)}, u32[]{:S(2)}, u32[]{:S(2)}) %collective-permute-start.12) | collective-permute-done | bytes 65568 | tf_op jit(solution)/shard_map/ppermute | solution.py:33
  114.9 0.6 add_add_fusion.1
  (16 shorter events, 0.1 us)
Async XLA Ops:
  3.7 14.7 %all-to-all-start = ((f32[8,64,256]{2,1,0:T(8,128)}), f32[8,64,256]{2,1,0:T(8,128)}, u32[]{:S(2)}, u32[]{:S(2)}) async-start(f32[8,64,256]{2,1,0:T(8,128)} %get-tuple-element.21), calls=%async_computation | async-start | bytes 1048576 | tf_op jit(solution)/shard_map/all_to_all | solution.py:425
  10.0 1.9 %copy-start = (bf16[512,3072]{1,0:T(8,128)(2,1)S(1)}, bf16[512,3072]{1,0:T(8,128)(2,1)}, u32[]{:S(2)}) copy-start(bf16[512,3072]{1,0:T(8,128)(2,1)} %q_ref.3) | copy-start | bytes 9437188
  11.9 1.4 %copy-start.3 = (bf16[256,3072]{1,0:T(8,128)(2,1)S(1)}, bf16[256,3072]{1,0:T(8,128)(2,1)}, u32[]{:S(2)}) copy-start(bf16[256,3072]{1,0:T(8,128)(2,1)} %k_ref.3) | copy-start | bytes 4718596
  13.3 0.7 copy-start.8
  14.0 0.7 copy-start.10
  14.7 32.1 %copy-start.1 = (bf16[512,3072]{1,0:T(8,128)(2,1)S(1)}, bf16[512,3072]{1,0:T(8,128)(2,1)}, u32[]{:S(2)}) copy-start(bf16[512,3072]{1,0:T(8,128)(2,1)} %q_ref.3) | copy-start | bytes 9437188
  14.7 32.1 %copy-start.9 = (s32[512]{0:T(512)S(1)}, s32[512]{0:T(512)}, u32[]{:S(2)}) copy-start(s32[512]{0:T(512)} %param.12) | copy-start | bytes 6148
  14.7 32.1 %copy-start.11 = (s32[256]{0:T(256)S(1)}, s32[256]{0:T(256)}, u32[]{:S(2)}) copy-start(s32[256]{0:T(256)} %param.13) | copy-start | bytes 3076
  19.7 1.2 %collective-permute-start = (f32[8,640]{1,0:T(8,128)S(1)}, f32[8,640]{1,0:T(8,128)S(1)}, u32[]{:S(2)}, u32[]{:S(2)}) collective-permute-start(f32[8,640]{1,0:T(8,128)S(1)} %get-tuple-element.24), channel_id=1, source_target_pairs={{0,1},{1,0},{2,3},{3,2},{4,5},{5,4},{6,7},{7,6},{8,9},{9,8},{10,11... | collective-permute-start | bytes 61448 | tf_op jit(solution)/shard_map/ppermute | solution.py:33
  21.0 0.7 copy-start.5
  21.7 23.7 %all-to-all-start.1 = ((f32[16,8,640]{2,1,0:T(8,128)}), f32[16,8,640]{2,1,0:T(8,128)S(1)}, u32[]{:S(2)}, u32[]{:S(2)}) async-start(f32[16,8,640]{2,1,0:T(8,128)} %copy-done.5), calls=%async_computation.1 | async-start | bytes 655360 | tf_op jit(solution)/shard_map/all_to_all | solution.py:430
  31.9 13.8 %collective-permute-start.4 = (f32[256,128]{1,0:T(8,128)}, f32[256,128]{1,0:T(8,128)}, u32[]{:S(2)}, u32[]{:S(2)}) collective-permute-start(f32[256,128]{1,0:T(8,128)} %get-tuple-element.25.ik_ref.i0_ref), channel_id=1, source_target_pairs={{0,6},{2,0},{4,2},{6,4},{1,7},{3,1},{5,3},{7,5},{8,14},{10,8},{12,... | collective-permute-start | bytes 393224 | tf_op jit(solution)/shard_map/ppermute | solution.py:33
  35.0 10.6 %collective-permute-start.3 = (f32[256,128]{1,0:T(8,128)}, f32[256,128]{1,0:T(8,128)}, u32[]{:S(2)}, u32[]{:S(2)}) collective-permute-start(f32[256,128]{1,0:T(8,128)} %get-tuple-element.25.ik_ref.i0_ref), channel_id=1, source_target_pairs={{0,4},{2,6},{4,0},{6,2},{1,5},{3,7},{5,1},{7,3},{8,12},{10,14},{12... | collective-permute-start | bytes 393224 | tf_op jit(solution)/shard_map/ppermute | solution.py:33
  35.9 10.8 %collective-permute-start.2 = (f32[256,128]{1,0:T(8,128)}, f32[256,128]{1,0:T(8,128)}, u32[]{:S(2)}, u32[]{:S(2)}) collective-permute-start(f32[256,128]{1,0:T(8,128)} %get-tuple-element.25.ik_ref.i0_ref), channel_id=1, source_target_pairs={{0,2},{2,4},{4,6},{6,0},{1,3},{3,5},{5,7},{7,1},{8,10},{10,12},{12... | collective-permute-start | bytes 393224 | tf_op jit(solution)/shard_map/ppermute | solution.py:33
  45.5 1.3 %collective-permute-start.1 = (f32[8,640]{1,0:T(8,128)S(1)}, f32[8,640]{1,0:T(8,128)S(1)}, u32[]{:S(2)}, u32[]{:S(2)}) collective-permute-start(f32[8,640]{1,0:T(8,128)S(1)} %merge_parts.1.mine_ref.lse_ref), channel_id=1, source_target_pairs={{0,1},{1,0},{2,3},{3,2},{4,5},{5,4},{6,7},{7,6},{8,9},{9,8},{10,11... | collective-permute-start | bytes 61448 | tf_op jit(solution)/shard_map/ppermute | solution.py:33
  46.8 1.4 %copy-start.4 = (bf16[256,3072]{1,0:T(8,128)(2,1)S(1)}, bf16[256,3072]{1,0:T(8,128)(2,1)}, u32[]{:S(2)}) copy-start(bf16[256,3072]{1,0:T(8,128)(2,1)} %k_ref.3) | copy-start | bytes 4718596
  51.7 34.3 %copy-start.2 = (bf16[512,1024]{1,0:T(8,128)(2,1)S(1)}, bf16[512,1024]{1,0:T(8,128)(2,1)}, u32[]{:S(2)}) copy-start(bf16[512,1024]{1,0:T(8,128)(2,1)} %iq_ref.3) | copy-start | bytes 3145732
  51.8 34.3 %copy-start.6 = (f32[256,128]{1,0:T(8,128)S(1)}, f32[256,128]{1,0:T(8,128)}, u32[]{:S(2)}) copy-start(f32[256,128]{1,0:T(8,128)} %get-tuple-element.25.ik_ref.i0_ref) | copy-start | bytes 393220
  51.8 34.3 %copy-start.7 = (f32[512,8]{0,1:T(8,128)S(1)}, f32[512,8]{0,1:T(8,128)}, u32[]{:S(2)}) copy-start(f32[512,8]{0,1:T(8,128)} %param.11) | copy-start | bytes 49156
  68.0 12.2 %all-to-all-start.3 = ((f32[8,2,64,128]{3,2,1,0:T(8,128)}), f32[8,2,64,128]{3,2,1,0:T(8,128)S(1)}, u32[]{:S(2)}, u32[]{:S(2)}) async-start(f32[8,2,64,128]{3,2,1,0:T(8,128)} %get-tuple-element.31), calls=%async_computation.3 | async-start | bytes 1048576 | tf_op jit(solution)/shard_map/all_to_all | solution.py:437
  73.2 4.9 %collective-permute-start.5 = (f32[2,16,128]{2,1,0:T(8,128)S(1)}, f32[2,16,128]{2,1,0:T(8,128)S(1)}, u32[]{:S(2)}, u32[]{:S(2)}) collective-permute-start(f32[2,16,128]{2,1,0:T(8,128)S(1)} %get-tuple-element.28), channel_id=1, source_target_pairs={{0,2},{2,4},{4,6},{6,0},{1,3},{3,5},{5,7},{7,1},{8,10},{10,12},{12... | collective-permute-start | bytes 49160 | tf_op jit(solution)/shard_map/ppermute | solution.py:33
  73.7 5.2 %collective-permute-start.6 = (f32[2,16,128]{2,1,0:T(8,128)S(1)}, f32[2,16,128]{2,1,0:T(8,128)S(1)}, u32[]{:S(2)}, u32[]{:S(2)}) collective-permute-start(f32[2,16,128]{2,1,0:T(8,128)S(1)} %get-tuple-element.29), channel_id=1, source_target_pairs={{0,4},{2,6},{4,0},{6,2},{1,5},{3,7},{5,1},{7,3},{8,12},{10,14},{12... | collective-permute-start | bytes 49160 | tf_op jit(solution)/shard_map/ppermute | solution.py:33
  75.8 3.7 %collective-permute-start.7 = (f32[2,16,128]{2,1,0:T(8,128)S(1)}, f32[2,16,128]{2,1,0:T(8,128)S(1)}, u32[]{:S(2)}, u32[]{:S(2)}) collective-permute-start(f32[2,16,128]{2,1,0:T(8,128)S(1)} %get-tuple-element.30), channel_id=1, source_target_pairs={{0,6},{2,0},{4,2},{6,4},{1,7},{3,1},{5,3},{7,5},{8,14},{10,8},{12,... | collective-permute-start | bytes 49160 | tf_op jit(solution)/shard_map/ppermute | solution.py:33
  81.0 14.3 %all-to-all-start.4 = ((f32[8,4,2,16,128]{4,3,2,1,0:T(8,128)}), f32[8,4,2,16,128]{4,3,2,1,0:T(8,128)S(1)}, u32[]{:S(2)}, u32[]{:S(2)}) async-start(f32[8,4,2,16,128]{4,3,2,1,0:T(8,128)} %repeat_parts.1), calls=%async_computation.4 | async-start | bytes 1048576 | tf_op jit(solution)/shard_map/all_to_all | solution.py:439
  87.9 7.4 %collective-permute-start.8 = (f32[256,128]{1,0:T(8,128)S(1)}, f32[256,128]{1,0:T(8,128)S(1)}, u32[]{:S(2)}, u32[]{:S(2)}) collective-permute-start(f32[256,128]{1,0:T(8,128)S(1)} %key_part_grad.1), channel_id=1, source_target_pairs={{0,128},{128,0},{1,129},{129,1},{2,130},{130,2},{3,131},{131,3},{4... | collective-permute-start | bytes 393224 | tf_op jit(solution)/shard_map/ppermute | solution.py:33
  98.1 4.9 %collective-permute-start.9 = (f32[64,1024]{1,0:T(8,128)S(1)}, f32[64,1024]{1,0:T(8,128)S(1)}, u32[]{:S(2)}, u32[]{:S(2)}) collective-permute-start(f32[64,1024]{1,0:T(8,128)S(1)} %get-tuple-element.33), channel_id=1, source_target_pairs={{0,1},{1,0},{2,3},{3,2},{4,5},{5,4},{6,7},{7,6},{8,9},{9,8},{10,11... | collective-permute-start | bytes 786440 | tf_op jit(solution)/shard_map/ppermute | solution.py:33
  98.2 8.0 %collective-permute-start.15 = (f32[256,128]{1,0:T(8,128)S(1)}, f32[256,128]{1,0:T(8,128)S(1)}, u32[]{:S(2)}, u32[]{:S(2)}) collective-permute-start(f32[256,128]{1,0:T(8,128)S(1)} %add.33.first), channel_id=1, source_target_pairs={{0,96},{32,0},{64,32},{96,64},{1,97},{33,1},{65,33},{97,65},{2,98}... | collective-permute-start | bytes 393224 | tf_op jit(solution)/shard_map/ppermute | solution.py:33
  98.8 10.9 %collective-permute-start.14 = (f32[256,128]{1,0:T(8,128)S(1)}, f32[256,128]{1,0:T(8,128)S(1)}, u32[]{:S(2)}, u32[]{:S(2)}) collective-permute-start(f32[256,128]{1,0:T(8,128)S(1)} %add.33.first), channel_id=1, source_target_pairs={{0,64},{32,96},{64,0},{96,32},{1,65},{33,97},{65,1},{97,33},{2,66}... | collective-permute-start | bytes 393224 | tf_op jit(solution)/shard_map/ppermute | solution.py:33
  101.2 8.6 %collective-permute-start.13 = (f32[256,128]{1,0:T(8,128)S(1)}, f32[256,128]{1,0:T(8,128)S(1)}, u32[]{:S(2)}, u32[]{:S(2)}) collective-permute-start(f32[256,128]{1,0:T(8,128)S(1)} %add.33.first), channel_id=1, source_target_pairs={{0,32},{32,64},{64,96},{96,0},{1,33},{33,65},{65,97},{97,1},{2,34}... | collective-permute-start | bytes 393224 | tf_op jit(solution)/shard_map/ppermute | solution.py:33
  103.0 7.4 %collective-permute-start.10 = (f32[16,1024]{1,0:T(8,128)S(1)}, f32[16,1024]{1,0:T(8,128)S(1)}, u32[]{:S(2)}, u32[]{:S(2)}) collective-permute-start(f32[16,1024]{1,0:T(8,128)S(1)} %get-tuple-element.35), channel_id=1, source_target_pairs={{0,8},{8,16},{16,24},{24,0},{1,9},{9,17},{17,25},{25,1},{2,10},{10... | collective-permute-start | bytes 196616 | tf_op jit(solution)/shard_map/ppermute | solution.py:33
  103.3 8.3 %collective-permute-start.11 = (f32[16,1024]{1,0:T(8,128)S(1)}, f32[16,1024]{1,0:T(8,128)S(1)}, u32[]{:S(2)}, u32[]{:S(2)}) collective-permute-start(f32[16,1024]{1,0:T(8,128)S(1)} %get-tuple-element.36), channel_id=1, source_target_pairs={{0,16},{8,24},{16,0},{24,8},{1,17},{9,25},{17,1},{25,9},{2,18},{10... | collective-permute-start | bytes 196616 | tf_op jit(solution)/shard_map/ppermute | solution.py:33
  106.2 8.7 %collective-permute-start.12 = (f32[16,1024]{1,0:T(8,128)S(1)}, f32[16,1024]{1,0:T(8,128)S(1)}, u32[]{:S(2)}, u32[]{:S(2)}) collective-permute-start(f32[16,1024]{1,0:T(8,128)S(1)} %get-tuple-element.37), channel_id=1, source_target_pairs={{0,24},{8,0},{16,8},{24,16},{1,25},{9,1},{17,9},{25,17},{2,26},{10... | collective-permute-start | bytes 196616 | tf_op jit(solution)/shard_map/ppermute | solution.py:33

commit v5 on v4

--- a/solution.py
+++ b/solution.py
@@ -148,7 +148,7 @@
             jax.ShapeDtypeStruct((rows // n_head, keys), F32),
         ],
         scratch_shapes=[pltpu.VMEM((keys, rows), F32), pltpu.VMEM((rows, LANES), F32)],
-        compiler_params=PARAMS,
+        compiler_params=WIDE_PARAMS,
         name="scores_lse",
     )(sc, queries, attn_keys, off, qp)
 

time: 117 us -> 117 us (level)
  Pallas kernels: 18.7 us -> 21.3 us
  local copies, waits for them, and re-layouts: 6.89 us -> 4.32 us
    unnamed x24 -> x22, local copies, waits for them, and re-layouts: 6.81 us -> 3.75 us
    pallas_call x1, Pallas kernels: 3.71 us -> 6.37 us  [scores_lse(): pl.pallas_call(lse_kernel, in_specs=[SMEM_SPEC] + [VMEM_SPEC] * 4, out_sp...]
  transfers between devices with their start and end apart: 20 -> 20, of which waited for: 11 -> 12; matrix products, arithmetic and copies ran while one was open for 1% -> 1% of each run, Pallas kernels for 5% -> 7%
where the time goes in v5:
time: 117 us; the launch traced here: 116 us
  starting transfers between devices  49.5 us (42%)
  waiting for transfers between devices  24.9 us (21%)
  Pallas kernels  21.3 us (18%)
  blocking collectives  13.7 us (12%)
  local copies, waits for them, and re-layouts  4.32 us (4%)
  other arithmetic  1.35 us (1%)
    ppermute x16, starting transfers between devices, shift(): lax.ppermute(value, axis, [(i, (i + step) % size) for i in range(size)])  22.6 us
    ppermute x16, waiting for transfers between devices, shift(): lax.ppermute(value, axis, [(i, (i + step) % size) for i in range(size)])  14.5 us
    all_to_all x1, blocking collectives, shards(): target = lax.all_to_all(target, HEAD, 0, 0)  13.7 us
    all_to_all x1, starting transfers between devices, shards(): mine = merge_parts(lax.all_to_all(mine, CHIP, 0, 0))  10.1 us
    all_to_all x1, waiting for transfers between devices, shards(): mine = merge_parts(lax.all_to_all(mine, CHIP, 0, 0))  8.74 us
    pallas_call x1, Pallas kernels, scores_lse(): pl.pallas_call(lse_kernel, in_specs=[SMEM_SPEC] + [VMEM_SPEC] * 4, out_sp...  6.37 us
    all_to_all x1, starting transfers between devices, shards(): index = lax.all_to_all(index, HEAD, 0, 0)  6.29 us
    all_to_all x1, starting transfers between devices, shards(): lax.all_to_all(repeat_parts(pieces, step_key, n_head), HEAD, 0, 0)  5.23 us
  transfers between devices with their start and end apart: 20, of which 12 were waited for; matrix products, arithmetic and copies ran while one was open for 1% of the time, Pallas kernels for 7%

profile of v5, /device:TPU:8, one launch (start us, length us, event | category | flops | bytes accessed | tf_op | source)
XLA Modules:
  0.0 115.9 jit_solution(16573900433789921345)
XLA Ops:
  0.6 3.0 %front.1 = (f32[8,64,256]{2,1,0:T(8,128)}, f32[256,128]{1,0:T(8,128)}) custom-call(bf16[512,1024]{1,0:T(8,128)(2,1)} %iq_ref.3, bf16[256,128]{1,0:T(8,128)(2,1)} %ik_hbm.1, f32[8,512]{1,0:T(8,128)} %bitcast.8), custom_call_target="tpu_custom_call" | custom-call | tf_op jit(solution)/shard_map/front/pallas_call | solution.py:105
  3.7 6.3 %all-to-all-start = ((f32[8,64,256]{2,1,0:T(8,128)}), f32[8,64,256]{2,1,0:T(8,128)}, u32[]{:S(2)}, u32[]{:S(2)}) async-start(f32[8,64,256]{2,1,0:T(8,128)} %get-tuple-element.21), calls=%async_computation | async-start | bytes 1048576 | tf_op jit(solution)/shard_map/all_to_all | solution.py:425
  9.9 0.6 stack.23.sc_ref
  10.5 6.4 %scores_lse.1 = (f32[16,512]{1,0:T(8,128)}, f32[64,256]{1,0:T(8,128)}) custom-call(s32[5]{0:T(128)} %stack.23.sc_ref, bf16[512,3072]{1,0:T(8,128)(2,1)} %q_ref.3, bf16[256,3072]{1,0:T(8,128)(2,1)} %k_ref.3, s32[1,256]{1,0:T(1,128)} %bitcast.13, s32[1,512]{1,0:T(1,128)} %bitcast.11), custom_call_target="tpu_custom_call" | custom-call | tf_op jit(solution)/shard_map/scores_lse/pallas_call | solution.py:142
  16.9 1.2 %all-to-all-done.parts_ref = f32[8,64,256]{2,1,0:T(8,128)} async-done(((f32[8,64,256]{2,1,0:T(8,128)}), f32[8,64,256]{2,1,0:T(8,128)}, u32[]{:S(2)}, u32[]{:S(2)}) %all-to-all-start) | async-done | bytes 524320 | tf_op jit(solution)/shard_map/all_to_all | solution.py:425
  18.1 0.0 copy-done.8
  18.1 0.8 copy-done.6
  18.9 0.8 copy-done.7
  19.7 1.3 %join_lse.1 = (f32[8,640]{1,0:T(8,128)S(1)}, f32[8,640]{1,0:T(8,128)S(1)}, f32[64,256]{1,0:T(8,128)S(1)}) custom-call(s32[5]{0:T(128)S(1)} %copy-done.8, f32[16,512]{1,0:T(8,128)S(1)} %copy-done.7, f32[8,64,256]{2,1,0:T(8,128)} %all-to-all-done.parts_ref, f32[64,256]{1,0:T(8,128)S(1)} %copy-done.6), custom_call_target="tpu_custom_call" | custom-call | tf_op jit(solution)/shard_map/join_lse/pallas_call | solution.py:173
  21.0 0.0 collective-permute-start
  21.0 1.2 %collective-permute-done.got_ref = f32[8,640]{1,0:T(8,128)S(1)} collective-permute-done((f32[8,640]{1,0:T(8,128)S(1)}, f32[8,640]{1,0:T(8,128)S(1)}, u32[]{:S(2)}, u32[]{:S(2)}) %collective-permute-start) | collective-permute-done | bytes 20512 | tf_op jit(solution)/shard_map/ppermute | solution.py:33
  22.3 0.7 copy-done.3
  23.0 10.1 %all-to-all-start.1 = ((f32[16,8,640]{2,1,0:T(8,128)}), f32[16,8,640]{2,1,0:T(8,128)S(1)}, u32[]{:S(2)}, u32[]{:S(2)}) async-start(f32[16,8,640]{2,1,0:T(8,128)} %copy-done.3), calls=%async_computation.1 | async-start | bytes 655360 | tf_op jit(solution)/shard_map/all_to_all | solution.py:430
  33.1 3.1 %collective-permute-start.4 = (f32[256,128]{1,0:T(8,128)}, f32[256,128]{1,0:T(8,128)}, u32[]{:S(2)}, u32[]{:S(2)}) collective-permute-start(f32[256,128]{1,0:T(8,128)} %get-tuple-element.25.ik_ref.i0_ref), channel_id=1, source_target_pairs={{0,6},{2,0},{4,2},{6,4},{1,7},{3,1},{5,3},{7,5},{8,14},{10,8},{12,... | collective-permute-start | bytes 393224 | tf_op jit(solution)/shard_map/ppermute | solution.py:33
  36.3 0.9 collective-permute-start.3
  37.1 0.9 collective-permute-start.2
  38.0 8.7 %all-to-all-done.1.parts_ref = f32[16,8,640]{2,1,0:T(8,128)S(1)} async-done(((f32[16,8,640]{2,1,0:T(8,128)}), f32[16,8,640]{2,1,0:T(8,128)S(1)}, u32[]{:S(2)}, u32[]{:S(2)}) %all-to-all-start.1) | async-done | bytes 327712 | tf_op jit(solution)/shard_map/all_to_all | solution.py:430
  46.7 0.1 merge_parts.1.mine_ref.lse_ref
  46.8 0.1 collective-permute-start.1
  46.9 0.0 collective-permute-done.4.b3.i3_ref
  46.9 0.0 collective-permute-done.3.b2.i2_ref
  46.9 1.0 collective-permute-done.2.b1.i1_ref
  47.9 0.2 collective-permute-done.1.other_ref
  48.1 0.0 copy-done.9
  48.1 0.0 copy-start.2
  48.1 1.4 %copy-done.2 = bf16[256,3072]{1,0:T(8,128)(2,1)S(1)} copy-done((bf16[256,3072]{1,0:T(8,128)(2,1)S(1)}, bf16[256,3072]{1,0:T(8,128)(2,1)}, u32[]{:S(2)}) %copy-start.2) | copy-done | bytes 1572888
  49.5 3.5 %probs_sum.1 = f32[8,64,256]{2,1,0:T(8,128)S(1)} custom-call(s32[5]{0:T(128)S(1)} %copy-done.8, bf16[512,3072]{1,0:T(8,128)(2,1)S(1)} %copy-done, bf16[256,3072]{1,0:T(8,128)(2,1)S(1)} %copy-done.2, s32[1,256]{1,0:T(1,128)S(1)} %bitcast.14, s32[1,512]{1,0:T(1,128)S(1)} %bitcast.12, f32[8,640]{1,0:T(8,128)S(1)} %merge_parts.1.mine_ref.lse_ref, ...), custom_call_target="tpu_custom_call" | custom-call | tf_op jit(solution)/shard_map/probs_sum/pallas_call | solution.py:234
  53.0 0.0 copy-start.1
  53.0 0.0 copy-start.4
  53.0 0.0 copy-start.5
  53.0 13.7 %all_to_all.25.target_ref = f32[8,64,256]{2,1,0:T(8,128)S(1)} all-to-all(f32[8,64,256]{2,1,0:T(8,128)S(1)} %probs_sum.1), channel_id=1, replica_groups=mesh['z_lo'=2,'y'=4,'z_hi'=4,'x'=4,'core'=2] {'z_lo','y'}, dimensions={0} | all-to-all | bytes 1048576 | tf_op jit(solution)/shard_map/all_to_all | solution.py:434
  66.7 1.6 %prob_step.1 = (f32[8,2,64,128]{3,2,1,0:T(8,128)}, f32[2,16,128]{2,1,0:T(8,128)S(1)}, f32[2,16,128]{2,1,0:T(8,128)S(1)}, f32[2,16,128]{2,1,0:T(8,128)S(1)}, f32[2,16,128]{2,1,0:T(8,128)S(1)}) custom-call(s32[5]{0:T(128)S(1)} %copy-done.8, f32[8,64,256]{2,1,0:T(8,128)S(1)} %all_to_all.25.target_ref, f32[64,256]{1,0:T(8,128)S(1)} %get-tuple-element.26.logits_ref, ...), custom_call_target="tpu_custom_call" | custom-call | tf_op jit(solution)/shard_map/prob_step/pallas_call | solution.py:271
  68.3 5.2 %all-to-all-start.3 = ((f32[8,2,64,128]{3,2,1,0:T(8,128)}), f32[8,2,64,128]{3,2,1,0:T(8,128)S(1)}, u32[]{:S(2)}, u32[]{:S(2)}) async-start(f32[8,2,64,128]{3,2,1,0:T(8,128)} %get-tuple-element.31), calls=%async_computation.3 | async-start | bytes 1048576 | tf_op jit(solution)/shard_map/all_to_all | solution.py:437
  73.5 0.4 collective-permute-start.5
  73.9 2.4 %collective-permute-start.6 = (f32[2,16,128]{2,1,0:T(8,128)S(1)}, f32[2,16,128]{2,1,0:T(8,128)S(1)}, u32[]{:S(2)}, u32[]{:S(2)}) collective-permute-start(f32[2,16,128]{2,1,0:T(8,128)S(1)} %get-tuple-element.29), channel_id=1, source_target_pairs={{0,4},{2,6},{4,0},{6,2},{1,5},{3,7},{5,1},{7,3},{8,12},{10,14},{12... | collective-permute-start | bytes 49160 | tf_op jit(solution)/shard_map/ppermute | solution.py:33
  76.2 1.7 %collective-permute-start.7 = (f32[2,16,128]{2,1,0:T(8,128)S(1)}, f32[2,16,128]{2,1,0:T(8,128)S(1)}, u32[]{:S(2)}, u32[]{:S(2)}) collective-permute-start(f32[2,16,128]{2,1,0:T(8,128)S(1)} %get-tuple-element.30), channel_id=1, source_target_pairs={{0,6},{2,0},{4,2},{6,4},{1,7},{3,1},{5,3},{7,5},{8,14},{10,8},{12,... | collective-permute-start | bytes 49160 | tf_op jit(solution)/shard_map/ppermute | solution.py:33
  77.9 0.5 collective-permute-done.5.p1
  78.4 0.7 collective-permute-done.6.p2
  79.1 0.9 collective-permute-done.7.p3
  80.0 0.5 all-to-all-done.3.first.step_ref
  80.5 0.8 repeat_parts.1
  81.3 5.2 %all-to-all-start.4 = ((f32[8,4,2,16,128]{4,3,2,1,0:T(8,128)}), f32[8,4,2,16,128]{4,3,2,1,0:T(8,128)S(1)}, u32[]{:S(2)}, u32[]{:S(2)}) async-start(f32[8,4,2,16,128]{4,3,2,1,0:T(8,128)} %repeat_parts.1), calls=%async_computation.4 | async-start | bytes 1048576 | tf_op jit(solution)/shard_map/all_to_all | solution.py:439
  86.6 0.0 copy-done.5
  86.6 1.9 %key_part_grad.1 = f32[256,128]{1,0:T(8,128)S(1)} custom-call(f32[8,2,64,128]{3,2,1,0:T(8,128)S(1)} %all-to-all-done.3.first.step_ref, bf16[512,1024]{1,0:T(8,128)(2,1)S(1)} %copy-done.1, f32[256,128]{1,0:T(8,128)S(1)} %copy-done.4, f32[8,512]{1,0:T(8,128)S(1)} %bitcast.9), custom_call_target="tpu_custom_call" | custom-call | tf_op jit(solution)/shard_map/key_part_grad/pallas_call | solution.py:406
  88.4 1.6 %collective-permute-start.8 = (f32[256,128]{1,0:T(8,128)S(1)}, f32[256,128]{1,0:T(8,128)S(1)}, u32[]{:S(2)}, u32[]{:S(2)}) collective-permute-start(f32[256,128]{1,0:T(8,128)S(1)} %key_part_grad.1), channel_id=1, source_target_pairs={{0,128},{128,0},{1,129},{129,1},{2,130},{130,2},{3,131},{131,3},{4... | collective-permute-start | bytes 393224 | tf_op jit(solution)/shard_map/ppermute | solution.py:33
  90.0 5.6 %collective-permute-done.8 = f32[256,128]{1,0:T(8,128)S(1)} collective-permute-done((f32[256,128]{1,0:T(8,128)S(1)}, f32[256,128]{1,0:T(8,128)S(1)}, u32[]{:S(2)}, u32[]{:S(2)}) %collective-permute-start.8) | collective-permute-done | bytes 131104 | tf_op jit(solution)/shard_map/ppermute | solution.py:33
  95.7 0.0 all-to-all-done.4.step_ref
  95.7 2.8 %query_pieces.1 = (f32[64,1024]{1,0:T(8,128)S(1)}, f32[64,1024]{1,0:T(8,128)S(1)}) custom-call(s32[5]{0:T(128)S(1)} %copy-done.8, f32[8,4,2,16,128]{4,3,2,1,0:T(8,128)S(1)} %all-to-all-done.4.step_ref, bf16[512,1024]{1,0:T(8,128)(2,1)S(1)} %copy-done.1, f32[8,512]{1,0:T(8,128)S(1)} %bitcast.10, f32[256,128]{1,0:T(8,128)S(1)} %copy-done.4, ...), custom_call_target="tpu_custom_call" | custom-call | tf_op jit(solution)/shard_map/query_pieces/pallas_call | solution.py:350
  98.4 0.1 collective-permute-start.9
  98.5 0.6 collective-permute-start.15
  99.1 2.3 %collective-permute-start.14 = (f32[256,128]{1,0:T(8,128)S(1)}, f32[256,128]{1,0:T(8,128)S(1)}, u32[]{:S(2)}, u32[]{:S(2)}) collective-permute-start(f32[256,128]{1,0:T(8,128)S(1)} %add.33.first), channel_id=1, source_target_pairs={{0,64},{32,96},{64,0},{96,32},{1,65},{33,97},{65,1},{97,33},{2,66}... | collective-permute-start | bytes 393224 | tf_op jit(solution)/shard_map/ppermute | solution.py:33
  101.5 1.8 %collective-permute-start.13 = (f32[256,128]{1,0:T(8,128)S(1)}, f32[256,128]{1,0:T(8,128)S(1)}, u32[]{:S(2)}, u32[]{:S(2)}) collective-permute-start(f32[256,128]{1,0:T(8,128)S(1)} %add.33.first), channel_id=1, source_target_pairs={{0,32},{32,64},{64,96},{96,0},{1,33},{33,65},{65,97},{97,1},{2,34}... | collective-permute-start | bytes 393224 | tf_op jit(solution)/shard_map/ppermute | solution.py:33
  103.3 0.0 collective-permute-done.9.got_ref
  103.3 0.4 collective-permute-start.10
  103.7 2.9 %collective-permute-start.11 = (f32[16,1024]{1,0:T(8,128)S(1)}, f32[16,1024]{1,0:T(8,128)S(1)}, u32[]{:S(2)}, u32[]{:S(2)}) collective-permute-start(f32[16,1024]{1,0:T(8,128)S(1)} %get-tuple-element.36), channel_id=1, source_target_pairs={{0,16},{8,24},{16,0},{24,8},{1,17},{9,25},{17,1},{25,9},{2,18},{10... | collective-permute-start | bytes 196616 | tf_op jit(solution)/shard_map/ppermute | solution.py:33
  106.6 0.0 collective-permute-done.15
  106.6 3.5 %collective-permute-start.12 = (f32[16,1024]{1,0:T(8,128)S(1)}, f32[16,1024]{1,0:T(8,128)S(1)}, u32[]{:S(2)}, u32[]{:S(2)}) collective-permute-start(f32[16,1024]{1,0:T(8,128)S(1)} %get-tuple-element.37), channel_id=1, source_target_pairs={{0,24},{8,0},{16,8},{24,16},{1,25},{9,1},{17,9},{25,17},{2,26},{10... | collective-permute-start | bytes 196616 | tf_op jit(solution)/shard_map/ppermute | solution.py:33
  110.1 0.0 collective-permute-done.14
  110.1 0.0 collective-permute-done.13
  110.1 0.7 add_add_fusion
  110.8 0.0 collective-permute-done.10
  110.8 1.1 collective-permute-done.11
  111.9 3.3 %collective-permute-done.12 = f32[16,1024]{1,0:T(8,128)S(1)} collective-permute-done((f32[16,1024]{1,0:T(8,128)S(1)}, f32[16,1024]{1,0:T(8,128)S(1)}, u32[]{:S(2)}, u32[]{:S(2)}) %collective-permute-start.12) | collective-permute-done | bytes 65568 | tf_op jit(solution)/shard_map/ppermute | solution.py:33
  115.2 0.6 add_add_fusion.1
  (14 shorter events, 0.1 us)
Async XLA Ops:
  3.7 14.4 %all-to-all-start = ((f32[8,64,256]{2,1,0:T(8,128)}), f32[8,64,256]{2,1,0:T(8,128)}, u32[]{:S(2)}, u32[]{:S(2)}) async-start(f32[8,64,256]{2,1,0:T(8,128)} %get-tuple-element.21), calls=%async_computation | async-start | bytes 1048576 | tf_op jit(solution)/shard_map/all_to_all | solution.py:425
  10.5 7.6 %copy-start.8 = (s32[5]{0:T(128)S(1)}, s32[5]{0:T(128)}, u32[]{:S(2)}) copy-start(s32[5]{0:T(128)} %stack.23.sc_ref) | copy-start | bytes 64
  10.5 37.5 %copy-start = (bf16[512,3072]{1,0:T(8,128)(2,1)S(1)}, bf16[512,3072]{1,0:T(8,128)(2,1)}, u32[]{:S(2)}) copy-start(bf16[512,3072]{1,0:T(8,128)(2,1)} %q_ref.3) | copy-start | bytes 9437188
  10.5 37.5 %copy-start.9 = (s32[512]{0:T(512)S(1)}, s32[512]{0:T(512)}, u32[]{:S(2)}) copy-start(s32[512]{0:T(512)} %param.12) | copy-start | bytes 6148
  10.5 37.5 %copy-start.10 = (s32[256]{0:T(256)S(1)}, s32[256]{0:T(256)}, u32[]{:S(2)}) copy-start(s32[256]{0:T(256)} %param.13) | copy-start | bytes 3076
  18.1 0.8 copy-start.6
  18.9 0.8 copy-start.7
  21.0 1.2 %collective-permute-start = (f32[8,640]{1,0:T(8,128)S(1)}, f32[8,640]{1,0:T(8,128)S(1)}, u32[]{:S(2)}, u32[]{:S(2)}) collective-permute-start(f32[8,640]{1,0:T(8,128)S(1)} %get-tuple-element.24), channel_id=1, source_target_pairs={{0,1},{1,0},{2,3},{3,2},{4,5},{5,4},{6,7},{7,6},{8,9},{9,8},{10,11... | collective-permute-start | bytes 61448 | tf_op jit(solution)/shard_map/ppermute | solution.py:33
  22.2 0.7 copy-start.3
  23.0 23.7 %all-to-all-start.1 = ((f32[16,8,640]{2,1,0:T(8,128)}), f32[16,8,640]{2,1,0:T(8,128)S(1)}, u32[]{:S(2)}, u32[]{:S(2)}) async-start(f32[16,8,640]{2,1,0:T(8,128)} %copy-done.3), calls=%async_computation.1 | async-start | bytes 655360 | tf_op jit(solution)/shard_map/all_to_all | solution.py:430
  33.1 13.8 %collective-permute-start.4 = (f32[256,128]{1,0:T(8,128)}, f32[256,128]{1,0:T(8,128)}, u32[]{:S(2)}, u32[]{:S(2)}) collective-permute-start(f32[256,128]{1,0:T(8,128)} %get-tuple-element.25.ik_ref.i0_ref), channel_id=1, source_target_pairs={{0,6},{2,0},{4,2},{6,4},{1,7},{3,1},{5,3},{7,5},{8,14},{10,8},{12,... | collective-permute-start | bytes 393224 | tf_op jit(solution)/shard_map/ppermute | solution.py:33
  36.3 10.6 %collective-permute-start.3 = (f32[256,128]{1,0:T(8,128)}, f32[256,128]{1,0:T(8,128)}, u32[]{:S(2)}, u32[]{:S(2)}) collective-permute-start(f32[256,128]{1,0:T(8,128)} %get-tuple-element.25.ik_ref.i0_ref), channel_id=1, source_target_pairs={{0,4},{2,6},{4,0},{6,2},{1,5},{3,7},{5,1},{7,3},{8,12},{10,14},{12... | collective-permute-start | bytes 393224 | tf_op jit(solution)/shard_map/ppermute | solution.py:33
  37.1 10.8 %collective-permute-start.2 = (f32[256,128]{1,0:T(8,128)}, f32[256,128]{1,0:T(8,128)}, u32[]{:S(2)}, u32[]{:S(2)}) collective-permute-start(f32[256,128]{1,0:T(8,128)} %get-tuple-element.25.ik_ref.i0_ref), channel_id=1, source_target_pairs={{0,2},{2,4},{4,6},{6,0},{1,3},{3,5},{5,7},{7,1},{8,10},{10,12},{12... | collective-permute-start | bytes 393224 | tf_op jit(solution)/shard_map/ppermute | solution.py:33
  46.8 1.3 %collective-permute-start.1 = (f32[8,640]{1,0:T(8,128)S(1)}, f32[8,640]{1,0:T(8,128)S(1)}, u32[]{:S(2)}, u32[]{:S(2)}) collective-permute-start(f32[8,640]{1,0:T(8,128)S(1)} %merge_parts.1.mine_ref.lse_ref), channel_id=1, source_target_pairs={{0,1},{1,0},{2,3},{3,2},{4,5},{5,4},{6,7},{7,6},{8,9},{9,8},{10,11... | collective-permute-start | bytes 61448 | tf_op jit(solution)/shard_map/ppermute | solution.py:33
  48.1 1.4 %copy-start.2 = (bf16[256,3072]{1,0:T(8,128)(2,1)S(1)}, bf16[256,3072]{1,0:T(8,128)(2,1)}, u32[]{:S(2)}) copy-start(bf16[256,3072]{1,0:T(8,128)(2,1)} %k_ref.3) | copy-start | bytes 4718596
  53.0 33.6 %copy-start.1 = (bf16[512,1024]{1,0:T(8,128)(2,1)S(1)}, bf16[512,1024]{1,0:T(8,128)(2,1)}, u32[]{:S(2)}) copy-start(bf16[512,1024]{1,0:T(8,128)(2,1)} %iq_ref.3) | copy-start | bytes 3145732
  53.0 33.6 %copy-start.4 = (f32[256,128]{1,0:T(8,128)S(1)}, f32[256,128]{1,0:T(8,128)}, u32[]{:S(2)}) copy-start(f32[256,128]{1,0:T(8,128)} %get-tuple-element.25.ik_ref.i0_ref) | copy-start | bytes 393220
  53.0 33.6 %copy-start.5 = (f32[512,8]{0,1:T(8,128)S(1)}, f32[512,8]{0,1:T(8,128)}, u32[]{:S(2)}) copy-start(f32[512,8]{0,1:T(8,128)} %param.11) | copy-start | bytes 49156
  68.3 12.2 %all-to-all-start.3 = ((f32[8,2,64,128]{3,2,1,0:T(8,128)}), f32[8,2,64,128]{3,2,1,0:T(8,128)S(1)}, u32[]{:S(2)}, u32[]{:S(2)}) async-start(f32[8,2,64,128]{3,2,1,0:T(8,128)} %get-tuple-element.31), calls=%async_computation.3 | async-start | bytes 1048576 | tf_op jit(solution)/shard_map/all_to_all | solution.py:437
  73.5 4.9 %collective-permute-start.5 = (f32[2,16,128]{2,1,0:T(8,128)S(1)}, f32[2,16,128]{2,1,0:T(8,128)S(1)}, u32[]{:S(2)}, u32[]{:S(2)}) collective-permute-start(f32[2,16,128]{2,1,0:T(8,128)S(1)} %get-tuple-element.28), channel_id=1, source_target_pairs={{0,2},{2,4},{4,6},{6,0},{1,3},{3,5},{5,7},{7,1},{8,10},{10,12},{12... | collective-permute-start | bytes 49160 | tf_op jit(solution)/shard_map/ppermute | solution.py:33
  73.9 5.2 %collective-permute-start.6 = (f32[2,16,128]{2,1,0:T(8,128)S(1)}, f32[2,16,128]{2,1,0:T(8,128)S(1)}, u32[]{:S(2)}, u32[]{:S(2)}) collective-permute-start(f32[2,16,128]{2,1,0:T(8,128)S(1)} %get-tuple-element.29), channel_id=1, source_target_pairs={{0,4},{2,6},{4,0},{6,2},{1,5},{3,7},{5,1},{7,3},{8,12},{10,14},{12... | collective-permute-start | bytes 49160 | tf_op jit(solution)/shard_map/ppermute | solution.py:33
  76.2 3.7 %collective-permute-start.7 = (f32[2,16,128]{2,1,0:T(8,128)S(1)}, f32[2,16,128]{2,1,0:T(8,128)S(1)}, u32[]{:S(2)}, u32[]{:S(2)}) collective-permute-start(f32[2,16,128]{2,1,0:T(8,128)S(1)} %get-tuple-element.30), channel_id=1, source_target_pairs={{0,6},{2,0},{4,2},{6,4},{1,7},{3,1},{5,3},{7,5},{8,14},{10,8},{12,... | collective-permute-start | bytes 49160 | tf_op jit(solution)/shard_map/ppermute | solution.py:33
  81.3 14.3 %all-to-all-start.4 = ((f32[8,4,2,16,128]{4,3,2,1,0:T(8,128)}), f32[8,4,2,16,128]{4,3,2,1,0:T(8,128)S(1)}, u32[]{:S(2)}, u32[]{:S(2)}) async-start(f32[8,4,2,16,128]{4,3,2,1,0:T(8,128)} %repeat_parts.1), calls=%async_computation.4 | async-start | bytes 1048576 | tf_op jit(solution)/shard_map/all_to_all | solution.py:439
  88.4 7.2 %collective-permute-start.8 = (f32[256,128]{1,0:T(8,128)S(1)}, f32[256,128]{1,0:T(8,128)S(1)}, u32[]{:S(2)}, u32[]{:S(2)}) collective-permute-start(f32[256,128]{1,0:T(8,128)S(1)} %key_part_grad.1), channel_id=1, source_target_pairs={{0,128},{128,0},{1,129},{129,1},{2,130},{130,2},{3,131},{131,3},{4... | collective-permute-start | bytes 393224 | tf_op jit(solution)/shard_map/ppermute | solution.py:33
  98.4 4.9 %collective-permute-start.9 = (f32[64,1024]{1,0:T(8,128)S(1)}, f32[64,1024]{1,0:T(8,128)S(1)}, u32[]{:S(2)}, u32[]{:S(2)}) collective-permute-start(f32[64,1024]{1,0:T(8,128)S(1)} %get-tuple-element.33), channel_id=1, source_target_pairs={{0,1},{1,0},{2,3},{3,2},{4,5},{5,4},{6,7},{7,6},{8,9},{9,8},{10,11... | collective-permute-start | bytes 786440 | tf_op jit(solution)/shard_map/ppermute | solution.py:33
  98.5 8.1 %collective-permute-start.15 = (f32[256,128]{1,0:T(8,128)S(1)}, f32[256,128]{1,0:T(8,128)S(1)}, u32[]{:S(2)}, u32[]{:S(2)}) collective-permute-start(f32[256,128]{1,0:T(8,128)S(1)} %add.33.first), channel_id=1, source_target_pairs={{0,96},{32,0},{64,32},{96,64},{1,97},{33,1},{65,33},{97,65},{2,98}... | collective-permute-start | bytes 393224 | tf_op jit(solution)/shard_map/ppermute | solution.py:33
  99.1 11.0 %collective-permute-start.14 = (f32[256,128]{1,0:T(8,128)S(1)}, f32[256,128]{1,0:T(8,128)S(1)}, u32[]{:S(2)}, u32[]{:S(2)}) collective-permute-start(f32[256,128]{1,0:T(8,128)S(1)} %add.33.first), channel_id=1, source_target_pairs={{0,64},{32,96},{64,0},{96,32},{1,65},{33,97},{65,1},{97,33},{2,66}... | collective-permute-start | bytes 393224 | tf_op jit(solution)/shard_map/ppermute | solution.py:33
  101.5 8.6 %collective-permute-start.13 = (f32[256,128]{1,0:T(8,128)S(1)}, f32[256,128]{1,0:T(8,128)S(1)}, u32[]{:S(2)}, u32[]{:S(2)}) collective-permute-start(f32[256,128]{1,0:T(8,128)S(1)} %add.33.first), channel_id=1, source_target_pairs={{0,32},{32,64},{64,96},{96,0},{1,33},{33,65},{65,97},{97,1},{2,34}... | collective-permute-start | bytes 393224 | tf_op jit(solution)/shard_map/ppermute | solution.py:33
  103.3 7.5 %collective-permute-start.10 = (f32[16,1024]{1,0:T(8,128)S(1)}, f32[16,1024]{1,0:T(8,128)S(1)}, u32[]{:S(2)}, u32[]{:S(2)}) collective-permute-start(f32[16,1024]{1,0:T(8,128)S(1)} %get-tuple-element.35), channel_id=1, source_target_pairs={{0,8},{8,16},{16,24},{24,0},{1,9},{9,17},{17,25},{25,1},{2,10},{10... | collective-permute-start | bytes 196616 | tf_op jit(solution)/shard_map/ppermute | solution.py:33
  103.7 8.2 %collective-permute-start.11 = (f32[16,1024]{1,0:T(8,128)S(1)}, f32[16,1024]{1,0:T(8,128)S(1)}, u32[]{:S(2)}, u32[]{:S(2)}) collective-permute-start(f32[16,1024]{1,0:T(8,128)S(1)} %get-tuple-element.36), channel_id=1, source_target_pairs={{0,16},{8,24},{16,0},{24,8},{1,17},{9,25},{17,1},{25,9},{2,18},{10... | collective-permute-start | bytes 196616 | tf_op jit(solution)/shard_map/ppermute | solution.py:33
  106.6 8.6 %collective-permute-start.12 = (f32[16,1024]{1,0:T(8,128)S(1)}, f32[16,1024]{1,0:T(8,128)S(1)}, u32[]{:S(2)}, u32[]{:S(2)}) collective-permute-start(f32[16,1024]{1,0:T(8,128)S(1)} %get-tuple-element.37), channel_id=1, source_target_pairs={{0,24},{8,0},{16,8},{24,16},{1,25},{9,1},{17,9},{25,17},{2,26},{10... | collective-permute-start | bytes 196616 | tf_op jit(solution)/shard_map/ppermute | solution.py:33
